TPU v7x, 32 devices: a whole 2x2x4 slice. The times are simulated.
32 devices in a mesh: lat: 8 (over z, y), lon: 4 (over x, core).
Axes of the slice: x: 2, y: 2, z: 4, core: 2. Of those that a mesh axis runs over, the one named last changes fastest.
Arguments:
- tokens: bfloat16 [4, 192, 360, 256], P(None, 'lat', 'lon'), may hold values from -6 to 6
- cotangent: bfloat16 [4, 192, 360, 256], P(None, 'lat', 'lon'), may hold values from -6 to 6
- w_qkv: bfloat16 [256, 768], replicated, may hold values from -0.375 to 0.375
- q_bias: bfloat16 [256], replicated, may hold values from -4 to 4
- v_bias: bfloat16 [256], replicated, may hold values from -1.5 to 1.5
- w_proj: bfloat16 [256, 256], replicated, may hold values from -0.375 to 0.375
- b_proj: bfloat16 [256], replicated, may hold values from -1.5 to 1.5
- w_up: bfloat16 [256, 1024], replicated, may hold values from -0.375 to 0.375
- b_up: bfloat16 [1024], replicated, may hold values from -6 to 6
- w_down: bfloat16 [1024, 256], replicated, may hold values from -0.1875 to 0.1875
- b_down: bfloat16 [256], replicated, may hold values from -3 to 3
- w_mod: bfloat16 [256, 1024], replicated, may hold values from -0.375 to 0.375
- b_mod: bfloat16 [1024], replicated, may hold values from -4 to 4
- rel_table: bfloat16 [4, 3, 23, 11], replicated, may hold values from -6 to 6
- crop_rows: int32 [8], replicated, may hold values from 6 to 24, as said below
- lead_hours: int32 [1], replicated, may hold values from 1 to 240
Outputs:
- mixed: bfloat16 [4, 192, 360, 256], P(None, 'lat', 'lon')
- token_grad: bfloat16 [4, 192, 360, 256], P(None, 'lat', 'lon')
- grad_qkv: float32 [256, 768], replicated
- grad_q_bias: float32 [256], replicated
- grad_v_bias: float32 [256], replicated
- grad_proj: float32 [256, 256], replicated
- grad_proj_bias: float32 [256], replicated
- grad_up: float32 [256, 1024], replicated
- grad_up_bias: float32 [1024], replicated
- grad_down: float32 [1024, 256], replicated
- grad_down_bias: float32 [256], replicated
- grad_mod: float32 [256, 1024], replicated
- grad_mod_bias: float32 [1024], replicated
- grad_table: float32 [4, 3, 23, 11], replicated
Inputs may be any that keep to these rules, and one draw needn't show every extreme that they name: In each latitude band of 24 rows the crop holds the band's last crop_rows rows; some band is whole and some holds a quarter of 24 rows.
All inputs are finite; a program needn't handle non-finite values.
Results may differ from a plain program's by a relative error of at most 0.012.
Values may be sent and summed in bfloat16 or wider, within the bound.
A program may use at most 384 MiB of HBM per device.

v0:
```python
import math

import jax
import jax.numpy as jnp
from jax import lax
from jax.sharding import PartitionSpec as P

WZ = 2
WY = 12
WX = 6


NORM_EPSILON = 1e-05
MASKED_SCORE = -1000000000.0
PRECISE = lax.Precision.HIGHEST


def passed_along(block, axis, distance):
    devices = range(lax.axis_size(axis))
    route = [((i - distance) % len(devices), i) for i in devices]
    return lax.ppermute(block, axis, route)


def layer_norm(values):
    center = values - jnp.mean(values, axis=-1, keepdims=True)
    spread = jnp.mean(center * center, axis=-1, keepdims=True)
    return center * lax.rsqrt(spread + NORM_EPSILON)


def modulate(values, scale_vec, shift_vec):
    return layer_norm(values) * (1.0 + scale_vec) + shift_vec


def gelu_exact(values):
    return jax.nn.gelu(values, approximate=False)


def lead_context(lead_hours, feat_width):
    half_width = feat_width // 2
    fraction = jnp.arange(half_width, dtype=jnp.float32) / half_width
    angles = lead_hours.astype(jnp.float32)[0] * jnp.exp(-math.log(1000.0) * fraction)
    return jnp.concatenate([jnp.sin(angles), jnp.cos(angles)])


def one_hot_offsets(span_len):
    places = jnp.arange(span_len)
    offsets = places[:, None] - places[None, :] + span_len - 1
    return (offsets[:, :, None] == jnp.arange(2 * span_len - 1)[None, None, :]).astype(jnp.float32)


def relative_bias(table_bias):
    head_count = table_bias.shape[0]
    span_z = (table_bias.shape[1] + 1) // 2
    span_y = (table_bias.shape[2] + 1) // 2
    span_x = (table_bias.shape[3] + 1) // 2
    biases = jnp.einsum(
        "habc,ika,jlb,mnc->hijmkln",
        table_bias,
        one_hot_offsets(span_z),
        one_hot_offsets(span_y),
        one_hot_offsets(span_x),
        precision=PRECISE,
    )
    window = span_z * span_y * span_x
    return biases.reshape(head_count, window, window)


def to_windows(grid_field):
    level_count, row_count, col_count, feat_width = grid_field.shape
    rolled = jnp.roll(grid_field, -(WZ // 2), axis=0)
    pieces = rolled.reshape(
        level_count // WZ, WZ, row_count // WY, WY, col_count // WX, WX, feat_width
    )
    pieces = pieces.transpose(0, 2, 4, 1, 3, 5, 6)
    return pieces.reshape(
        level_count // WZ * (row_count // WY), col_count // WX * WZ * WY * WX, feat_width
    )


def from_windows(groups, level_count, row_count, col_count):
    feat_width = groups.shape[-1]
    pieces = groups.reshape(
        level_count // WZ, row_count // WY, col_count // WX, WZ, WY, WX, feat_width
    )
    grid_field = pieces.transpose(0, 3, 1, 4, 2, 5, 6).reshape(
        level_count, row_count, col_count, feat_width
    )
    return jnp.roll(grid_field, WZ // 2, axis=0)


def window_table(level_values, row_values, col_count):
    level_count = level_values.shape[0]
    row_count = row_values.shape[0]
    level_order = jnp.roll(jnp.arange(level_count, dtype=jnp.int32), -(WZ // 2)).reshape(
        level_count // WZ, WZ
    )
    level_pick = jnp.sum(
        jnp.where(
            level_order[:, :, None] == jnp.arange(level_count, dtype=jnp.int32)[None, None, :],
            level_values[None, None, :],
            0,
        ),
        axis=2,
    )
    row_pick = row_values.reshape(row_count // WY, WY)
    table = level_pick[:, None, None, :, None, None] + row_pick[None, :, None, None, :, None]
    table = jnp.broadcast_to(
        table, (level_count // WZ, row_count // WY, col_count // WX, WZ, WY, WX)
    )
    return table.reshape(level_count // WZ * (row_count // WY), col_count // WX, WZ * WY * WX)


def extend(tile_field, move_cols, move_rows):
    row_count = tile_field.shape[1]
    col_count = tile_field.shape[2]
    arriving = move_cols(tile_field[:, :, col_count - WX // 2 :])
    widened = jnp.concatenate([arriving, tile_field[:, :, : col_count - WX // 2]], axis=2)
    above_rows = move_rows(widened[:, row_count - WY // 2 :])
    return jnp.concatenate([above_rows, widened[:, : row_count - WY // 2]], axis=1)


def fold(region, move_rows, move_cols):
    returned = move_rows(region[:, : WY // 2])
    taller = jnp.concatenate([region[:, WY // 2 :], returned], axis=1)
    leftover = move_cols(taller[:, :, : WX // 2])
    return jnp.concatenate([taller[:, :, WX // 2 :], leftover], axis=2)


def window_scores(group_qkv, group_seg, group_valid, biases):
    count_win, window = group_seg.shape
    head_count = biases.shape[0]
    split_heads = group_qkv.reshape(count_win, window, 3, head_count, -1)
    queries = split_heads[:, :, 0]
    keys_win = split_heads[:, :, 1]
    values_win = split_heads[:, :, 2]
    score_scale = queries.shape[-1] ** (-0.5)
    raw_scores = (
        jnp.einsum("wqhd,wkhd->whqk", queries, keys_win, preferred_element_type=jnp.float32)
        * score_scale
        + biases[None]
    )
    same_part = group_seg[:, :, None] == group_seg[:, None, :]
    usable = (group_valid[:, None, :] > 0) | jnp.eye(window, dtype=jnp.bool_)[None]
    scores = jnp.where((same_part & usable)[:, None], raw_scores, MASKED_SCORE)
    return (scores, queries, keys_win, values_win, score_scale)


def on_device(
    tokens,
    cotangent,
    w_qkv,
    q_bias,
    v_bias,
    w_proj,
    b_proj,
    w_up,
    b_up,
    w_down,
    b_down,
    w_mod,
    b_mod,
    rel_table,
    crop_rows,
    lead_hours,
):
    level_count, row_count, col_count, feat_width = tokens.shape
    token_count = level_count * row_count * col_count
    band_count = lax.axis_size("lat")
    context = jax.nn.silu(lead_context(lead_hours, feat_width))
    modulation = jnp.dot(
        context[None, :],
        w_mod.astype(jnp.float32),
        precision=PRECISE,
        preferred_element_type=jnp.float32,
    )[0] + b_mod.astype(jnp.float32)
    shift_one, scale_one, shift_two, scale_two = jnp.split(modulation, 4)
    biases, bias_pull = jax.vjp(relative_bias, rel_table.astype(jnp.float32))
    first_row = lax.axis_index("lat") * row_count - WY // 2
    global_rows = jnp.mod(
        first_row + jnp.arange(row_count, dtype=jnp.int32), band_count * row_count
    )
    band_ids = global_rows // row_count
    crop_here = jnp.sum(
        jnp.where(
            band_ids[:, None] == jnp.arange(band_count, dtype=jnp.int32)[None, :],
            crop_rows[None, :],
            0,
        ),
        axis=1,
    )
    valid_rows = (global_rows % row_count >= row_count - crop_here).astype(jnp.int32)
    level_part = 2 * (jnp.arange(level_count, dtype=jnp.int32) == 0).astype(jnp.int32)
    row_part = (global_rows < WY // 2).astype(jnp.int32)
    seg_groups = window_table(level_part, row_part, col_count)
    valid_groups = window_table(jnp.zeros((level_count,), jnp.int32), valid_rows, col_count)
    region_tokens = extend(
        tokens,
        lambda border: passed_along(border, "lon", 1),
        lambda border: passed_along(border, "lat", 1),
    )
    token_windows = to_windows(region_tokens)
    group_count, group_len = (token_windows.shape[0], token_windows.shape[1])
    region_flat = token_windows.reshape(token_count, feat_width)
    qkv_shift = jnp.concatenate([q_bias, jnp.zeros_like(q_bias), v_bias]).astype(jnp.float32)
    projected = (
        jnp.dot(region_flat, w_qkv, preferred_element_type=jnp.float32) + qkv_shift
    ).astype(jnp.bfloat16)
    qkv_groups = projected.reshape(group_count, group_len, 3 * feat_width)

    def attend(pieces):
        group_qkv, group_seg, group_valid = pieces
        scores, queries, keys_win, values_win, score_scale = window_scores(
            group_qkv, group_seg, group_valid, biases
        )
        top_score = jnp.max(scores, axis=-1, keepdims=True)
        exp_scores = jnp.exp(scores - top_score)
        exp_total = jnp.sum(exp_scores, axis=-1, keepdims=True)
        weights = (exp_scores / exp_total).astype(jnp.bfloat16)
        attended = jnp.einsum(
            "whqk,wkhd->wqhd", weights, values_win, preferred_element_type=jnp.float32
        )
        return (
            attended.reshape(group_qkv.shape[0], feat_width).astype(jnp.bfloat16),
            (top_score + jnp.log(exp_total))[..., 0],
        )

    att_groups, lse_groups = lax.map(attend, (qkv_groups, seg_groups, valid_groups))
    att_region = from_windows(att_groups, level_count, row_count, col_count)
    attended = fold(
        att_region,
        lambda border: passed_along(border, "lat", -1),
        lambda border: passed_along(border, "lon", -1),
    )
    att_flat = attended.reshape(token_count, feat_width)
    token_flat = tokens.reshape(token_count, feat_width).astype(jnp.float32)
    out_grad_flat = cotangent.reshape(token_count, feat_width).astype(jnp.float32)
    branch = jnp.dot(att_flat, w_proj, preferred_element_type=jnp.float32) + b_proj.astype(
        jnp.float32
    )
    mod_one, post_one = jax.vjp(modulate, branch, scale_one, shift_one)
    middle = token_flat + mod_one
    middle_low = middle.astype(jnp.bfloat16)
    hidden_pre = jnp.dot(middle_low, w_up, preferred_element_type=jnp.float32) + b_up.astype(
        jnp.float32
    )
    hidden_act, gelu_pull = jax.vjp(gelu_exact, hidden_pre)
    hidden = hidden_act.astype(jnp.bfloat16)
    second = jnp.dot(hidden, w_down, preferred_element_type=jnp.float32) + b_down.astype(
        jnp.float32
    )
    mod_two, post_two = jax.vjp(modulate, second, scale_two, shift_two)
    mixed_flat = (middle + mod_two).astype(jnp.bfloat16)
    second_grad, scale_two_grad, shift_two_grad = post_two(out_grad_flat)
    second_low = second_grad.astype(jnp.bfloat16)
    grad_down = jnp.einsum("nf,nd->fd", hidden, second_low, preferred_element_type=jnp.float32)
    grad_down_bias = jnp.sum(second_low, axis=0, dtype=jnp.float32)
    hidden_grad = jnp.einsum("nd,fd->nf", second_low, w_down, preferred_element_type=jnp.float32)
    pre_low = gelu_pull(hidden_grad)[0].astype(jnp.bfloat16)
    grad_up = jnp.einsum("nd,nf->df", middle_low, pre_low, preferred_element_type=jnp.float32)
    grad_up_bias = jnp.sum(pre_low, axis=0, dtype=jnp.float32)
    middle_grad = out_grad_flat + jnp.einsum(
        "nf,df->nd", pre_low, w_up, preferred_element_type=jnp.float32
    )
    branch_grad, scale_one_grad, shift_one_grad = post_one(middle_grad)
    branch_low = branch_grad.astype(jnp.bfloat16)
    grad_proj = jnp.einsum("ne,nd->ed", att_flat, branch_low, preferred_element_type=jnp.float32)
    grad_proj_bias = jnp.sum(branch_low, axis=0, dtype=jnp.float32)
    att_grad = jnp.einsum(
        "nd,ed->ne", branch_low, w_proj, preferred_element_type=jnp.float32
    ).astype(jnp.bfloat16)
    att_grad_region = extend(
        att_grad.reshape(level_count, row_count, col_count, feat_width),
        lambda border: passed_along(border, "lon", 1),
        lambda border: passed_along(border, "lat", 1),
    )
    att_grad_groups = to_windows(att_grad_region)

    def attend_back(bias_grad, pieces):
        group_qkv, group_seg, group_valid, group_lse, group_out_grad = pieces
        scores, queries, keys_win, values_win, score_scale = window_scores(
            group_qkv, group_seg, group_valid, biases
        )
        prob_full = jnp.exp(scores - group_lse[..., None])
        weights = prob_full.astype(jnp.bfloat16)
        out_grad = group_out_grad.reshape(queries.shape)
        prob_grad = jnp.einsum(
            "wqhd,wkhd->whqk", out_grad, values_win, preferred_element_type=jnp.float32
        )
        score_grad = (
            prob_full * (prob_grad - jnp.sum(prob_grad * prob_full, axis=-1, keepdims=True))
        ).astype(jnp.bfloat16)
        query_grad = (
            jnp.einsum("whqk,wkhd->wqhd", score_grad, keys_win, preferred_element_type=jnp.float32)
            * score_scale
        )
        key_grad = (
            jnp.einsum("whqk,wqhd->wkhd", score_grad, queries, preferred_element_type=jnp.float32)
            * score_scale
        )
        value_grad = jnp.einsum(
            "whqk,wqhd->wkhd", weights, out_grad, preferred_element_type=jnp.float32
        )
        qkv_grad = (
            jnp.stack([query_grad, key_grad, value_grad], axis=2)
            .astype(jnp.bfloat16)
            .reshape(group_qkv.shape)
        )
        return (bias_grad + jnp.sum(score_grad, axis=0, dtype=jnp.float32), qkv_grad)

    table_sum, qkv_grad_groups = lax.scan(
        attend_back,
        jnp.zeros(biases.shape, jnp.float32),
        (qkv_groups, seg_groups, valid_groups, lse_groups, att_grad_groups),
    )
    grad_table = bias_pull(table_sum)[0]
    qkv_grad = qkv_grad_groups.reshape(token_count, 3 * feat_width)
    grad_qkv = jnp.einsum("nd,ne->de", region_flat, qkv_grad, preferred_element_type=jnp.float32)
    qkv_sums = jnp.sum(qkv_grad, axis=0, dtype=jnp.float32)
    grad_q_bias = qkv_sums[:feat_width]
    grad_v_bias = qkv_sums[2 * feat_width :]
    input_part = jnp.einsum("ne,de->nd", qkv_grad, w_qkv, preferred_element_type=jnp.float32)
    mixed = mixed_flat.reshape(tokens.shape)
    input_grid = from_windows(
        input_part.reshape(group_count, group_len, feat_width), level_count, row_count, col_count
    )
    input_back = fold(
        input_grid,
        lambda border: passed_along(border.astype(jnp.bfloat16), "lat", -1).astype(border.dtype),
        lambda border: passed_along(border.astype(jnp.bfloat16), "lon", -1).astype(border.dtype),
    )
    token_grad = (
        (middle_grad + input_back.reshape(token_count, feat_width))
        .astype(jnp.bfloat16)
        .reshape(tokens.shape)
    )
    (
        grad_qkv,
        grad_q_bias,
        grad_v_bias,
        grad_proj,
        grad_proj_bias,
        scale_one_grad,
        shift_one_grad,
        grad_table,
        grad_up,
        grad_up_bias,
        grad_down,
        grad_down_bias,
        scale_two_grad,
        shift_two_grad,
    ) = lax.psum(
        (
            grad_qkv,
            grad_q_bias,
            grad_v_bias,
            grad_proj,
            grad_proj_bias,
            scale_one_grad,
            shift_one_grad,
            grad_table,
            grad_up,
            grad_up_bias,
            grad_down,
            grad_down_bias,
            scale_two_grad,
            shift_two_grad,
        ),
        ("lat", "lon"),
    )
    grad_mod_bias = jnp.concatenate(
        [shift_one_grad, scale_one_grad, shift_two_grad, scale_two_grad]
    )
    grad_mod = context[:, None] * grad_mod_bias[None, :]
    return (
        mixed,
        token_grad,
        grad_qkv,
        grad_q_bias,
        grad_v_bias,
        grad_proj,
        grad_proj_bias,
        grad_up,
        grad_up_bias,
        grad_down,
        grad_down_bias,
        grad_mod,
        grad_mod_bias,
        grad_table,
    )


def solution(mesh):
    return jax.shard_map(
        on_device,
        mesh=mesh,
        in_specs=(
            P(None, "lat", "lon", None),
            P(None, "lat", "lon", None),
            P(),
            P(),
            P(),
            P(),
            P(),
            P(),
            P(),
            P(),
            P(),
            P(),
            P(),
            P(),
            P(),
            P(),
        ),
        out_specs=(
            P(None, "lat", "lon", None),
            P(None, "lat", "lon", None),
            P(),
            P(),
            P(),
            P(),
            P(),
            P(),
            P(),
            P(),
            P(),
            P(),
            P(),
            P(),
        ),
        check_vma=False,
    )
```

profile of v0, /device:TPU:0, one launch (start us, length us, event | category | flops | bytes accessed | tf_op | source)
XLA Modules:
  0.0 1476.7 jit_solution(6004732408501761716)
XLA Ops:
  39.6 11.3 copy.195
  84.4 9.6 reshape.443
  108.6 10.3 reshape.429
  133.5 10.6 add_convert_fusion.1
  144.2 17.1 %copy.194 = bf16[4,2160,768]{1,2,0:T(8,128)(2,1)} copy(bf16[4,2160,768]{2,1,0:T(8,128)(2,1)} %bitcast.264) | data formatting | bytes 26542080 | tf_op jit(solution)/shard_map/while | solution.py:227
  161.2 158.9 %while.27 = (s32[]{:T(128)}, bf16[4,2160,256]{1,2,0:T(8,128)(2,1)}, f32[4,15,4,144]{3,2,1,0:T(4,128)}, bf16[4,2160,768]{1,2,0:T(8,128)(2,1)}, s32[4,15,144]{2,1,...) while((s32[]{:T(128)}, bf16[4,2160,256]{1,2,0:T(8,128)(2,1)}, ...), condition=%wide.wide.region_5.6_spmd, body=%wide.wide.region_2.5_spmd.sunk | while | flops 338667712 | bytes 49198936 | solution.py:227
  166.4 12.2 reshape.465
  206.1 12.2 reshape.465
  245.8 12.2 reshape.465
  285.5 12.2 reshape.465
  328.5 9.9 reshape.431
  347.3 10.8 reshape.432
  373.8 19.0 %collective-permute-done.2 = bf16[4,6,90,256]{3,0,2,1:T(4,128)(2,1)S(1)} collective-permute-done((bf16[4,6,90,256]{3,0,2,1:T(4,128)(2,1)S(1)}, bf16[4,6,90,256]{3,0,2,1:T(4,128)(2,1)S(1)}, u32[]{:S(2)}, u32[]{:S(2)}) %collective-permute-start.2) | collective-permute-done | bytes 1105952 | tf_op jit(solution)/shard_map/ppermute | solution.py:21
  426.7 86.1 %multiply_convert_fusion.3 = (bf16[8640,1024]{1,0:T(8,128)(2,1)}, f32[8640,1024]{1,0:T(8,128)}, f32[8640,1024]{1,0:T(8,128)}) fusion(f32[1024]{0:T(1024)S(1)} %copy-done.44, bf16[256,1024]{1,0:T(8,128)(2,1)S(1)} %copy-done, f32[8640,256]{1,0:T(8,128)S(1)} %add_add_fusion.2), kind=kOutput, calls=%fused_computation.53 | convolution fusion | flops 5115985920 | bytes 97849344 | tf_op jit(solution)/shard_map/dot_general | solution.py:243
  551.5 33.3 %convert_reduce_fusion.1 = (f32[1024]{0:T(1024)}, bf16[8640,1024]{1,0:T(8,128)(2,1)}) fusion(f32[8640,1024]{1,0:T(8,128)} %get-tuple-element.346, bf16[8640,256]{1,0:T(8,128)(2,1)} %get-tuple-element.338, bf16[1024,256]{1,0:T(8,128)(2,1)S(1)} %copy-done.53, f32[8640,1024]{1,0:T(8,128)} %get-tuple-element.366, f32[1024]{0:T(1024)S(1)} %copy-done.44), kind=kOutput, calls=%fused_computation.51 | convolution fusion | flops 4680252416 | bytes 93429760 | tf_op jit(solution)/shard_map/nd,fd->nf/dot_general | solution.py:257
  584.8 21.0 %multiply_reduce_fusion.2 = (f32[256]{0:T(256)}, f32[8640]{0:T(1024)S(1)}, f32[256]{0:T(256)}, f32[8640,256]{1,0:T(8,128)}) fusion(f32[8640,256]{1,0:T(8,128)} %copy-done.6, f32[8640]{0:T(1024)S(1)} %copy-done.24, f32[8640]{0:T(1024)S(1)} %copy-done.17, f32[256]{0:T(256)S(1)} %copy-done.32, f32[8640,256]{1,0:T(8,128)} %reshape.444, ...), kind=kOutput, calls=%fused_computation.83 | convolution fusion | flops 4549745664 | bytes 44867840 | tf_op jit(solution)/shard_map/nf,df->nd/dot_general | solution.py:261
  634.0 13.2 fusion.88
  652.8 10.0 fusion.45
  692.2 9.9 reshape.436
  710.9 10.8 reshape.437
  730.0 368.6 %while.28 = (s32[]{:T(128)}, f32[4,144,144]{1,2,0:T(8,128)}, bf16[4,2160,768]{1,2,0:T(8,128)(2,1)}, s32[4,15,144]{2,1,0:T(8,128)}, s32[4,15,144]{2,1,0:T(8,128)}...) while((s32[]{:T(128)}, f32[4,144,144]{1,2,0:T(8,128)}, ...), condition=%wide.wide.region_17.18_spmd.clone, body=%wide.wide.region_14.17_spmd.clone.sunk | while | flops 818305216 | bytes 134796368 | solution.py:310
  737.8 12.2 reshape.466
  767.7 11.3 multiply_reduce_fusion.9
  779.0 10.4 convert_reduce_fusion.8
  806.9 10.7 convert_element_type.235
  828.9 12.2 reshape.466
  858.8 11.3 multiply_reduce_fusion.9
  870.1 10.4 convert_reduce_fusion.8
  899.2 10.7 convert_element_type.235
  921.3 12.2 reshape.466
  951.1 11.3 multiply_reduce_fusion.9
  962.4 10.4 convert_reduce_fusion.8
  991.6 10.7 convert_element_type.235
  1013.6 12.2 reshape.466
  1043.4 11.3 multiply_reduce_fusion.9
  1054.8 10.4 convert_reduce_fusion.8
  1083.9 10.7 convert_element_type.235
  1098.6 22.2 %copy.207 = bf16[4,2160,768]{2,0,1:T(4,128)(2,1)} copy(bf16[4,2160,768]{1,2,0:T(8,128)(2,1)} %get-tuple-element.675) | data formatting | bytes 26542080 | tf_op jit(solution)/shard_map/while | solution.py:310
  1120.8 18.3 %copy.211 = bf16[4,2160,768]{2,1,0:T(8,128)(2,1)} copy(bf16[4,2160,768]{1,2,0:T(8,128)(2,1)} %get-tuple-element.675) | data formatting | bytes 26542080 | tf_op jit(solution)/shard_map/while | solution.py:310
  1145.8 26.8 %dot_general.91 = bf16[2,2,15,2,12,6,768]{6,1,0,5,4,3,2:T(2,128)(2,1)} reshape(bf16[4,2160,768]{2,0,1:T(4,128)(2,1)} %copy.207) | data formatting | bytes 26542080 | tf_op jit(solution)/shard_map/ne,de->nd/dot_general | solution.py:321
  1172.6 21.9 %fusion.40 = f32[2,2,2,12,15,6,256]{6,4,5,3,1,2,0:T(8,128)S(1)} fusion(bf16[2,2,15,2,12,6,768]{6,1,0,5,4,3,2:T(2,128)(2,1)} %dot_general.91, bf16[256,768]{1,0:T(8,128)(2,1)S(1)} %copy-done.55), kind=kOutput, calls=%fused_computation.120 | convolution fusion | flops 3397386240 | bytes 22511616 | tf_op jit(solution)/shard_map/ne,de->nd/dot_general | solution.py:321
  1202.5 12.9 reshape.438
  1238.5 9.6 reshape.442
  1248.1 20.8 %fusion.31 = f32[12,12,4,3,6,6]{5,3,4,2,1,0:T(4,128)S(1)} fusion(f32[12,12,4,6,6,2,2]{4,1,6,3,0,5,2:T(8,128)} %bitcast.265, s32[2,2]{1,0:T(2,128)S(1)} %copy-done.48), kind=kOutput, calls=%fused_computation.101 | convolution fusion | flops 2985996 | bytes 580624 | tf_op jit(solution)/shard_map/transpose(jvp(habc,ika,jlb,mnc->hijmkln))/dot_general | solution.py:56
  1268.9 12.7 fusion.49
  1282.4 38.3 %all-reduce = (f32[256]{0:T(256)}, f32[256]{0:T(256)}, f32[256]{0:T(256)}, f32[1024]{0:T(1024)}, f32[256]{0:T(256)}, /*index=5*/f32[256]{0:T(256)S(1)}, f32[256]...) all-reduce(f32[256]{0:T(256)S(1)} %get-tuple-element.359, ...), channel_id=1, replica_groups=mesh['lat'=8,'lon'=4] {'lat','lon'}, use_global_device_ids=true, to_apply=%region_20.21 | all-reduce | flops 6108 | bytes 48864 | tf_op jit(solution)/shard_map/psum | solution.py:351
  1341.8 9.6 reshape.439
  1374.5 86.9 %all-reduce.4.cloned.1.call-done = (f32[256,768]{1,0:T(8,128)}, f32[256,256]{1,0:T(8,128)}, f32[256,1024]{1,0:T(8,128)}, f32[1024,256]{1,0:T(8,128)}) async-done(((f32[256,768]{1,0:T(8,128)}, f32[256,256]{1,0:T(8,128)}, f32[256,1024]{1,0:T(8,128)}, f32[1024,256]{1,0:T(8,128)}), (f32[256,768]{1,0:T(8,128)}, f32[256,256]{1,0:T(8,128)}, f32[256,1024]{1,0:T(8,128)}, ...) | async-done | bytes 3145744 | tf_op jit(solution)/shard_map/psum | solution.py:351
  (492 shorter events, 668.7 us)
Async XLA Ops:
  7.2 419.4 %copy-start = (bf16[256,1024]{1,0:T(8,128)(2,1)S(1)}, bf16[256,1024]{1,0:T(8,128)(2,1)}, u32[]{:S(2)}) copy-start(bf16[256,1024]{1,0:T(8,128)(2,1)} %param.27) | copy-start | bytes 1572868
  7.2 1454.2 %all-reduce.4.cloned.1.call-start = ((), (), s32[]{:S(2)}) async-start(), calls=%async_computation | async-start | bytes 6291456 | tf_op jit(solution)/shard_map/psum | solution.py:351
  8.3 18.6 %collective-permute-start = (bf16[4,24,3,256]{3,2,1,0:T(4,128)(2,1)S(1)}, bf16[4,24,3,256]{3,2,1,0:T(4,128)(2,1)S(1)}, u32[]{:S(2)}, u32[]{:S(2)}) collective-permute-start(bf16[4,24,3,256]{3,2,1,0:T(4,128)(2,1)S(1)} %copy.244), channel_id=1, source_target_pairs={{3,0},{0,1},{1,2},{2,3},{7,4},{4,5},{5,6},{6,7},{11,8},{8,9},{9,10... | collective-permute-start | bytes 442376 | tf_op jit(solution)/shard_map/ppermute | solution.py:21
  8.8 14.9 %copy-start.25 = (s32[12,12]{1,0:T(8,128)}, s32[12,12]{1,0:T(8,128)S(1)}, u32[]{:S(2)}) copy-start(s32[12,12]{1,0:T(8,128)S(1)} %subtract_add_fusion) | copy-start | bytes 1732
  8.8 14.9 %copy-start.27 = (s32[6,6]{1,0:T(8,128)}, s32[6,6]{1,0:T(8,128)S(1)}, u32[]{:S(2)}) copy-start(s32[6,6]{1,0:T(8,128)S(1)} %subtract_add_fusion.1) | copy-start | bytes 436
  8.9 14.8 %copy-start.47 = (s32[2,2]{1,0:T(2,128)}, s32[2,2]{1,0:T(2,128)S(1)}, u32[]{:S(2)}) copy-start(s32[2,2]{1,0:T(2,128)S(1)} %subtract_add_fusion.2) | copy-start | bytes 52
  29.7 67.2 %collective-permute-start.1 = (bf16[4,6,90,256]{3,2,1,0:T(8,128)(2,1)}, bf16[4,6,90,256]{3,2,1,0:T(8,128)(2,1)S(1)}, u32[]{:S(2)}, u32[]{:S(2)}) collective-permute-start(bf16[4,6,90,256]{3,2,1,0:T(8,128)(2,1)} %pad_maximum_fusion.11), channel_id=1, source_target_pairs={{28,0},{0,4},{4,8},{8,12},{12,16},{16,20},{20,24},{24,28},{29,1},{... | collective-permute-start | bytes 3317768 | tf_op jit(solution)/shard_map/ppermute | solution.py:21
  84.4 11.9 copy-start.46
  118.9 14.6 copy-start.54
  320.2 18.2 %copy-start.14 = (s32[4,15,144]{2,1,0:T(8,128)}, s32[4,15,144]{2,1,0:T(8,128)S(1)}, u32[]{:S(2)}) copy-start(s32[4,15,144]{2,1,0:T(8,128)S(1)} %get-tuple-element.701) | copy-start | bytes 103684
  320.2 18.2 %copy-start.15 = (s32[4,15,144]{2,1,0:T(8,128)}, s32[4,15,144]{2,1,0:T(8,128)S(1)}, u32[]{:S(2)}) copy-start(s32[4,15,144]{2,1,0:T(8,128)S(1)} %get-tuple-element.702) | copy-start | bytes 103684
  347.3 21.3 %slice-start.20 = ((s8[4423680]{0:T(1024)(128)(4,1)}), s8[229376]{0:T(1024)(128)(4,1)S(1)}, s32[]{:S(2)}) async-start(s8[4423680]{0:T(1024)(128)(4,1)} %bitcast.260), calls=%async_computation.21 | async-start | bytes 458752
  358.0 12.2 slice-start.11
  365.5 27.3 %collective-permute-start.2 = (bf16[4,6,90,256]{3,0,2,1:T(4,128)(2,1)S(1)}, bf16[4,6,90,256]{3,0,2,1:T(4,128)(2,1)S(1)}, u32[]{:S(2)}, u32[]{:S(2)}) collective-permute-start(bf16[4,6,90,256]{3,0,2,1:T(4,128)(2,1)S(1)} %pad_maximum_fusion.12), channel_id=1, source_target_pairs={{4,0},{8,4},{12,8},{16,12},{20,16},{24,20},{28,24},{0,28},{5,1},{9... | collective-permute-start | bytes 3317768 | tf_op jit(solution)/shard_map/ppermute | solution.py:21
  392.9 6.5 collective-permute-start.3
  426.6 107.6 %copy-start.7 = (f32[8640,256]{1,0:T(8,128)}, f32[8640,256]{1,0:T(8,128)S(1)}, u32[]{:S(2)}) copy-start(f32[8640,256]{1,0:T(8,128)S(1)} %add_add_fusion.2) | copy-start | bytes 26542084
  426.6 86.2 %copy-start.53 = (bf16[1024,256]{1,0:T(8,128)(2,1)S(1)}, bf16[1024,256]{1,0:T(8,128)(2,1)}, u32[]{:S(2)}) copy-start(bf16[1024,256]{1,0:T(8,128)(2,1)} %param.29) | copy-start | bytes 1572868
  426.7 86.2 %copy-start.58 = (f32[256]{0:T(256)S(1)}, f32[256]{0:T(256)}, u32[]{:S(2)}) copy-start(f32[256]{0:T(256)} %convert_element_type.156) | copy-start | bytes 3076
  551.5 33.3 %copy-start.17 = (f32[8640]{0:T(1024)S(1)}, f32[8640]{0:T(1024)}, u32[]{:S(2)}) copy-start(f32[8640]{0:T(1024)} %copy-done.16) | copy-start | bytes 103684
  551.5 33.3 %copy-start.24 = (f32[8640]{0:T(1024)S(1)}, f32[8640]{0:T(1024)}, u32[]{:S(2)}) copy-start(f32[8640]{0:T(1024)} %copy-done.23) | copy-start | bytes 103684
  551.5 33.3 %copy-start.32 = (f32[256]{0:T(256)S(1)}, f32[256]{0:T(256)}, u32[]{:S(2)}) copy-start(f32[256]{0:T(256)} %get-tuple-element.363) | copy-start | bytes 3076
  584.8 21.0 %copy-start.22 = (f32[8640]{0:T(1024)S(1)}, f32[8640]{0:T(1024)}, u32[]{:S(2)}) copy-start(f32[8640]{0:T(1024)} %copy-done.21) | copy-start | bytes 103684
  632.5 14.7 slice-start.18
  633.9 13.2 slice-start.19
  633.9 13.6 collective-permute-start.4
  651.1 30.4 %collective-permute-start.5 = (bf16[4,6,90,256]{3,0,2,1:T(4,128)(2,1)S(1)}, bf16[4,6,90,256]{3,0,2,1:T(4,128)(2,1)S(1)}, u32[]{:S(2)}, u32[]{:S(2)}) collective-permute-start(bf16[4,6,90,256]{3,0,2,1:T(4,128)(2,1)S(1)} %copy.200), channel_id=1, source_target_pairs={{28,0},{0,4},{4,8},{8,12},{12,16},{16,20},{20,24},{24,28},{29,1},{... | collective-permute-start | bytes 3317768 | tf_op jit(solution)/shard_map/ppermute | solution.py:21
  662.8 14.3 slice-start.5
  710.9 19.1 %copy-start.11 = (f32[4,144,144]{2,1,0:T(8,128)S(1)}, f32[4,144,144]{2,1,0:T(8,128)}, u32[]{:S(2)}) copy-start(f32[4,144,144]{2,1,0:T(8,128)} %add.431) | copy-start | bytes 995332
  806.9 14.6 copy-start.12
  899.2 14.7 copy-start.12
  991.6 14.6 copy-start.12
  1083.9 14.6 copy-start.12
  1145.8 26.8 %copy-start.55 = (bf16[256,768]{1,0:T(8,128)(2,1)S(1)}, bf16[256,768]{1,0:T(8,128)(2,1)}, u32[]{:S(2)}) copy-start(bf16[256,768]{1,0:T(8,128)(2,1)} %param.22) | copy-start | bytes 1179652
  1215.4 14.2 slice-start.16
  1225.0 102.9 %collective-permute-start.6 = (bf16[4,6,90,256]{3,0,2,1:T(4,128)(2,1)}, bf16[4,6,90,256]{3,0,2,1:T(4,128)(2,1)}, u32[]{:S(2)}, u32[]{:S(2)}) collective-permute-start(bf16[4,6,90,256]{3,0,2,1:T(4,128)(2,1)} %fusion.44), channel_id=1, source_target_pairs={{4,0},{8,4},{12,8},{16,12},{20,16},{24,20},{28,24},{0,28},{5,1},{9... | collective-permute-start | bytes 3317768 | tf_op jit(solution)/shard_map/ppermute | solution.py:21
  1248.0 20.8 %copy-start.28 = (s32[6,6]{1,0:T(8,128)S(1)}, s32[6,6]{1,0:T(8,128)}, u32[]{:S(2)}) copy-start(s32[6,6]{1,0:T(8,128)} %copy-done.27) | copy-start | bytes 436
  1248.0 33.6 %copy-start.26 = (s32[12,12]{1,0:T(8,128)S(1)}, s32[12,12]{1,0:T(8,128)}, u32[]{:S(2)}) copy-start(s32[12,12]{1,0:T(8,128)} %copy-done.25) | copy-start | bytes 1732
  1268.8 13.5 copy-start.36
  1268.8 13.5 copy-start.37
  1268.8 13.5 copy-start.38
  1268.9 13.5 copy-start.39
  1268.9 13.5 copy-start.41
  1268.9 13.5 copy-start.49
  1268.9 13.5 copy-start.50
  1268.9 52.5 %copy-start.34 = (f32[1024]{0:T(1024)S(1)}, f32[1024]{0:T(1024)}, u32[]{:S(2)}) copy-start(f32[1024]{0:T(1024)} %custom-call.1) | copy-start | bytes 12292
  1268.9 52.5 %copy-start.30 = (f32[256]{0:T(256)S(1)}, f32[256]{0:T(256)}, u32[]{:S(2)}) copy-start(f32[256]{0:T(256)} %copy-done.29) | copy-start | bytes 3076
  1329.6 4.8 collective-permute-start.7
  1360.2 109.4 %copy-start.1 = (bf16[256,1024]{1,0:T(8,128)(2,1)S(1)}, bf16[256,1024]{1,0:T(8,128)(2,1)}, u32[]{:S(2)}) copy-start(bf16[256,1024]{1,0:T(8,128)(2,1)} %param.27) | copy-start | bytes 1572868
  (64 other events, 450.7 us)
Sparse Core Ops, SparseCore 0:
  1321.6 139.7 all-reduce.3
where the time goes:
time: 1490 us; the launch traced here: 1480 us
  local copies, waits for them, and re-layouts  694 us (47%)
  matrix products  408 us (27%)
  other arithmetic  198 us (13%)
  waiting for transfers between devices  107 us (7%)
  blocking collectives  38.3 us (3%)
  between operations  16.1 us (1%)
    reshape x8, local copies, waits for them, and re-layouts, window_scores(): split_heads = group_qkv.reshape(count_win, window, 3, head_count, -1)  97.8 us
    psum x1, waiting for transfers between devices, on_device(): lax.psum((grad_qkv, grad_q_bias, grad_v_bias, grad_proj, grad_proj_bias,...  86.9 us
    dot_general x1, matrix products, on_device(): jnp.dot(middle_low, w_up, preferred_element_type=jnp.float32)  86.1 us
    dot_general x6, matrix products, relative_bias(): jnp.einsum('habc,ika,jlb,mnc->hijmkln', table_bias, one_hot_offsets(span_...  47.9 us
    dot_general x4, matrix products, attend_back(): jnp.einsum('wqhd,wkhd->whqk', out_grad, values_win, preferred_element_typ...  45.2 us
    dot_general x8, matrix products, window_scores(): jnp.einsum('wqhd,wkhd->whqk', queries, keys_win, preferred_element_type=j...  43.3 us
    convert_element_type x4, local copies, waits for them, and re-layouts, attend_back(): qkv_grad = jnp.stack([query_grad, key_grad, value_grad], axis=2).astype(j...  42.9 us
    reduce_sum x4, other arithmetic, attend_back(): jnp.sum(score_grad, axis=0, dtype=jnp.float32)  41.7 us
  transfers between devices with their start and end apart: 9, of which 3 were waited for; matrix products, arithmetic and copies ran while one was open for 16% of the time, Pallas kernels for 0%

commit v1 on v0

v1 whole, which is shorter than its diff:
```python
import functools
import math

import jax
import jax.numpy as jnp
from jax import lax
from jax.experimental import pallas as pl
from jax.experimental.pallas import tpu as pltpu
from jax.sharding import PartitionSpec as P

WZ = 2
WY = 12
WX = 6
WINDOW = WZ * WY * WX
HEADS = 4
BLOCK_WINDOWS = 3

NORM_EPSILON = 1e-05
MASKED_SCORE = -1000000000.0
PRECISE = lax.Precision.HIGHEST
F32 = jnp.float32
BF16 = jnp.bfloat16


def passed_along(block, axis, distance):
    devices = range(lax.axis_size(axis))
    route = [((i - distance) % len(devices), i) for i in devices]
    return lax.ppermute(block, axis, route)


def lead_context(lead_hours, feat_width):
    half_width = feat_width // 2
    fraction = jnp.arange(half_width, dtype=jnp.float32) / half_width
    angles = lead_hours.astype(jnp.float32)[0] * jnp.exp(-math.log(1000.0) * fraction)
    return jnp.concatenate([jnp.sin(angles), jnp.cos(angles)])


def one_hot_offsets(span_len):
    places = jnp.arange(span_len)
    offsets = places[:, None] - places[None, :] + span_len - 1
    return (offsets[:, :, None] == jnp.arange(2 * span_len - 1)[None, None, :]).astype(jnp.float32)


def relative_bias(table_bias):
    biases = jnp.einsum(
        "habc,ika,jlb,mnc->nklhmij",
        table_bias,
        one_hot_offsets(WZ),
        one_hot_offsets(WY),
        one_hot_offsets(WX),
        precision=PRECISE,
    )
    return biases.reshape(WINDOW, HEADS * WINDOW)


def to_windows(region):
    level_count, row_count, col_count, feat_width = region.shape
    rolled = jnp.roll(region, -(WZ // 2), axis=0)
    pieces = rolled.reshape(level_count // WZ, WZ, row_count // WY, WY, col_count, feat_width)
    return pieces.transpose(0, 2, 4, 1, 3, 5).reshape(-1, feat_width)


def from_windows(flat, level_count, row_count, col_count):
    feat_width = flat.shape[-1]
    pieces = flat.reshape(level_count // WZ, row_count // WY, col_count, WZ, WY, feat_width)
    region = pieces.transpose(0, 3, 1, 4, 2, 5).reshape(
        level_count, row_count, col_count, feat_width
    )
    return jnp.roll(region, WZ // 2, axis=0)


def extend(tile_field):
    row_count = tile_field.shape[1]
    col_count = tile_field.shape[2]
    arriving = passed_along(tile_field[:, :, col_count - WX // 2 :], "lon", 1)
    widened = jnp.concatenate([arriving, tile_field[:, :, : col_count - WX // 2]], axis=2)
    above_rows = passed_along(widened[:, row_count - WY // 2 :], "lat", 1)
    return jnp.concatenate([above_rows, widened[:, : row_count - WY // 2]], axis=1)


def fold(region):
    returned = passed_along(region[:, : WY // 2], "lat", -1)
    taller = jnp.concatenate([region[:, WY // 2 :], returned], axis=1)
    leftover = passed_along(taller[:, :, : WX // 2], "lon", -1)
    return jnp.concatenate([taller[:, :, WX // 2 :], leftover], axis=2)


def dot_nn(left, right):
    return lax.dot_general(left, right, (((1,), (0,)), ((), ())), preferred_element_type=F32)


def dot_nt(left, right):
    return lax.dot_general(left, right, (((1,), (1,)), ((), ())), preferred_element_type=F32)


def dot_tn(left, right):
    return lax.dot_general(left, right, (((0,), (0,)), ((), ())), preferred_element_type=F32)


def row_mean(values):
    return jnp.mean(values, axis=-1, keepdims=True)


def norm(values):
    center = values - row_mean(values)
    inverse = lax.rsqrt(row_mean(center * center) + NORM_EPSILON)
    return center * inverse, inverse


def norm_back(grad, normed, inverse):
    return inverse * (grad - row_mean(grad) - normed * row_mean(grad * normed))


def gelu_both(values):
    gauss_cdf = 0.5 * (1.0 + lax.erf(values * math.sqrt(0.5)))
    density = jnp.exp(values * values * -0.5) * (1.0 / math.sqrt(2.0 * math.pi))
    return values * gauss_cdf, gauss_cdf + values * density


def by_head(values):
    width = values.shape[-1] // HEADS
    lane_head = lax.broadcasted_iota(jnp.int32, values.shape, 1) // width
    zero = jnp.zeros_like(values)
    return jnp.concatenate([jnp.where(lane_head == h, values, zero) for h in range(HEADS)], axis=0)


def own_head(stacked):
    cells = stacked.shape[0] // HEADS
    width = stacked.shape[-1] // HEADS
    lane_head = lax.broadcasted_iota(jnp.int32, (cells, stacked.shape[-1]), 1) // width
    picked = stacked[:cells]
    for h in range(1, HEADS):
        picked = jnp.where(lane_head == h, stacked[h * cells : (h + 1) * cells], picked)
    return picked


def block_kernel(
    x_ref, g_ref, score_bias_ref, w_qkv_ref, qkv_shift_ref, w_proj_ref, w_up_ref, b_up_ref,
    w_down_ref, vec_ref,
    mixed_ref, token_grad_ref, grad_qkv_ref, grad_qkv_bias_ref, grad_proj_ref, grad_up_ref,
    grad_up_bias_ref, grad_down_ref, vec_grad_ref, score_sum_ref,
    qkv_ref, prob_ref, att_ref, dqkv_ref,
):
    @pl.when(pl.program_id(0) == 0)
    def _():
        for ref in (grad_qkv_ref, grad_qkv_bias_ref, grad_proj_ref, grad_up_ref,
                    grad_up_bias_ref, grad_down_ref, vec_grad_ref, score_sum_ref):
            ref[...] = jnp.zeros_like(ref)

    windows = x_ref.shape[0] // WINDOW
    width = x_ref.shape[1]
    score_scale = (width // HEADS) ** -0.5
    shift_one, scale_one, shift_two, scale_two, b_proj, b_down = [
        vec_ref[i : i + 1, :] for i in range(6)
    ]
    x = x_ref[...]
    qkv_ref[...] = (dot_nn(x, w_qkv_ref[...]) + qkv_shift_ref[...]).astype(BF16)
    for w in range(windows):
        cells = pl.ds(w * WINDOW, WINDOW)
        queries = by_head(qkv_ref[cells, :width] * BF16(score_scale))
        scores = dot_nt(qkv_ref[cells, width : 2 * width], queries) + score_bias_ref[0]
        top = jnp.max(scores, axis=0, keepdims=True)
        exps = jnp.exp(scores - top)
        prob = exps * (1.0 / jnp.sum(exps, axis=0, keepdims=True))
        prob_ref[w] = prob
        att_ref[cells, :] = own_head(
            dot_tn(prob.astype(BF16), qkv_ref[cells, 2 * width :])
        ).astype(BF16)

    att = att_ref[...]
    branch = dot_nn(att, w_proj_ref[...]) + b_proj
    norm_one, inverse_one = norm(branch)
    middle = x.astype(F32) + norm_one * (1.0 + scale_one) + shift_one
    middle_low = middle.astype(BF16)
    pre = dot_nn(middle_low, w_up_ref[...]) + b_up_ref[...]
    hidden, slope = gelu_both(pre)
    hidden = hidden.astype(BF16)
    second = dot_nn(hidden, w_down_ref[...]) + b_down
    norm_two, inverse_two = norm(second)
    mixed_ref[...] = (middle + norm_two * (1.0 + scale_two) + shift_two).astype(BF16)

    g = g_ref[...].astype(F32)
    second_low = norm_back(g * (1.0 + scale_two), norm_two, inverse_two).astype(BF16)
    grad_down_ref[...] += dot_tn(second_low, hidden)
    pre_grad = dot_nt(second_low, w_down_ref[...]) * slope
    pre_low = pre_grad.astype(BF16)
    grad_up_ref[...] += dot_tn(middle_low, pre_low)
    grad_up_bias_ref[...] += jnp.sum(pre_grad, axis=0, keepdims=True)
    middle_grad = g + dot_nt(pre_low, w_up_ref[...])
    branch_low = norm_back(middle_grad * (1.0 + scale_one), norm_one, inverse_one).astype(BF16)
    grad_proj_ref[...] += dot_tn(att, branch_low)
    att_ref[...] = dot_nt(branch_low, w_proj_ref[...]).astype(BF16)
    sums = [
        jnp.sum(v, axis=0, keepdims=True)
        for v in (
            middle_grad, middle_grad * norm_one, g, g * norm_two,
            branch_low.astype(F32), second_low.astype(F32),
        )
    ]
    vec_grad_ref[0:6, :] += jnp.concatenate(sums, axis=0)

    for w in range(windows):
        cells = pl.ds(w * WINDOW, WINDOW)
        queries = by_head(qkv_ref[cells, :width] * BF16(score_scale))
        out_grad = by_head(att_ref[cells, :])
        prob = prob_ref[w]
        prob_grad = dot_nt(qkv_ref[cells, 2 * width :], out_grad)
        score_grad = prob * (prob_grad - jnp.sum(prob_grad * prob, axis=0, keepdims=True))
        score_sum_ref[...] += score_grad
        score_grad = score_grad.astype(BF16)
        dqkv_ref[cells, :width] = (
            own_head(dot_tn(score_grad, qkv_ref[cells, width : 2 * width])) * score_scale
        ).astype(BF16)
        dqkv_ref[cells, width : 2 * width] = dot_nn(score_grad, queries).astype(BF16)
        dqkv_ref[cells, 2 * width :] = dot_nn(prob.astype(BF16), out_grad).astype(BF16)

    dqkv = dqkv_ref[...]
    grad_qkv_ref[...] += dot_tn(x, dqkv)
    grad_qkv_bias_ref[...] += jnp.sum(dqkv.astype(F32), axis=0, keepdims=True)
    token_grad_ref[...] = (middle_grad + dot_nt(dqkv, w_qkv_ref[...])).astype(BF16)


def block_call(x, g, score_bias, w_qkv, qkv_shift, w_proj, w_up, b_up, w_down, vecs):
    cell_count, width = x.shape
    hidden_width = w_up.shape[1]
    rows = BLOCK_WINDOWS * WINDOW
    steps = cell_count // rows
    per_group = steps // score_bias.shape[0]

    def whole(shape):
        return pl.BlockSpec(shape, lambda i: (0,) * len(shape))

    tile = pl.BlockSpec((rows, width), lambda i: (i, 0))
    outs = [
        (grad_shape, whole(grad_shape))
        for grad_shape in (
            (width, 3 * width), (1, 3 * width), (width, width), (width, hidden_width),
            (1, hidden_width), (width, hidden_width), (8, width), (WINDOW, HEADS * WINDOW),
        )
    ]
    return pl.pallas_call(
        block_kernel,
        grid=(steps,),
        in_specs=[
            tile, tile,
            pl.BlockSpec((1, WINDOW, HEADS * WINDOW), lambda i: (i // per_group, 0, 0)),
        ] + [whole(w.shape) for w in (w_qkv, qkv_shift, w_proj, w_up, b_up, w_down, vecs)],
        out_specs=[tile, tile] + [spec for _, spec in outs],
        out_shape=[jax.ShapeDtypeStruct(x.shape, BF16)] * 2
        + [jax.ShapeDtypeStruct(s, F32) for s, _ in outs],
        scratch_shapes=[
            pltpu.VMEM((rows, 3 * width), BF16),
            pltpu.VMEM((BLOCK_WINDOWS, WINDOW, HEADS * WINDOW), F32),
            pltpu.VMEM((rows, width), BF16),
            pltpu.VMEM((rows, 3 * width), BF16),
        ],
        compiler_params=pltpu.CompilerParams(vmem_limit_bytes=60 * 2**20),
    )(x, g, score_bias, w_qkv, qkv_shift, w_proj, w_up, b_up, w_down, vecs)


def on_device(
    tokens, cotangent, w_qkv, q_bias, v_bias, w_proj, b_proj, w_up, b_up, w_down, b_down,
    w_mod, b_mod, rel_table, crop_rows, lead_hours,
):
    level_count, row_count, col_count, feat_width = tokens.shape
    band_count = lax.axis_size("lat")
    context = jax.nn.silu(lead_context(lead_hours, feat_width))
    modulation = jnp.dot(
        context[None, :], w_mod.astype(F32), precision=PRECISE, preferred_element_type=F32
    )[0] + b_mod.astype(F32)
    vecs = jnp.concatenate(
        [
            modulation.reshape(4, feat_width),
            b_proj.astype(F32)[None],
            b_down.astype(F32)[None],
            jnp.zeros((2, feat_width), F32),
        ]
    )
    biases, bias_pull = jax.vjp(relative_bias, rel_table.astype(F32))

    first_row = lax.axis_index("lat") * row_count - WY // 2
    global_rows = jnp.mod(
        first_row + jnp.arange(row_count, dtype=jnp.int32), band_count * row_count
    )
    band_ids = global_rows // row_count
    crop_here = jnp.sum(
        jnp.where(
            band_ids[:, None] == jnp.arange(band_count, dtype=jnp.int32)[None, :],
            crop_rows[None, :],
            0,
        ),
        axis=1,
    )
    valid_rows = (global_rows % row_count >= row_count - crop_here).reshape(-1, WY)
    row_part = (global_rows < WY // 2).reshape(-1, WY)
    level_part = jnp.roll(jnp.arange(level_count) == 0, -(WZ // 2)).reshape(-1, WZ)
    group_shape = (level_part.shape[0], row_part.shape[0], WX, WZ, WY)
    part = 2 * level_part[:, None, None, :, None] + row_part[None, :, None, None, :]
    part = jnp.broadcast_to(part, group_shape).reshape(-1, WINDOW)
    valid = jnp.broadcast_to(valid_rows[None, :, None, None, :], group_shape).reshape(-1, WINDOW)
    allowed = (part[:, :, None] == part[:, None, :]) & (
        valid[:, :, None] | jnp.eye(WINDOW, dtype=jnp.bool_)[None]
    )
    masks = jnp.where(allowed, 0.0, MASKED_SCORE).astype(F32)
    score_bias = biases[None] + jnp.tile(masks, (1, 1, HEADS))

    qkv_shift = jnp.concatenate([q_bias, jnp.zeros_like(q_bias), v_bias]).astype(F32)[None]
    (
        mixed, token_grad, grad_qkv, grad_qkv_bias, grad_proj, grad_up, grad_up_bias, grad_down,
        vec_grad, score_sum,
    ) = block_call(
        to_windows(extend(tokens)), to_windows(extend(cotangent)), score_bias, w_qkv, qkv_shift,
        w_proj, w_up, b_up.astype(F32)[None], w_down, vecs,
    )
    mixed = fold(from_windows(mixed, level_count, row_count, col_count))
    token_grad = fold(from_windows(token_grad, level_count, row_count, col_count))
    grad_table = bias_pull(score_sum)[0]
    grad_qkv, grad_qkv_bias, grad_proj, grad_up, grad_up_bias, grad_down, vec_grad, grad_table = (
        lax.psum(
            (grad_qkv, grad_qkv_bias, grad_proj, grad_up, grad_up_bias, grad_down, vec_grad,
             grad_table),
            ("lat", "lon"),
        )
    )
    grad_mod_bias = vec_grad[:4].reshape(-1)
    grad_mod = context[:, None] * grad_mod_bias[None, :]
    return (
        mixed,
        token_grad,
        grad_qkv,
        grad_qkv_bias[0, :feat_width],
        grad_qkv_bias[0, 2 * feat_width :],
        grad_proj,
        vec_grad[4],
        grad_up,
        grad_up_bias[0],
        grad_down.T,
        vec_grad[5],
        grad_mod,
        grad_mod_bias,
        grad_table,
    )


def solution(mesh):
    split = P(None, "lat", "lon", None)
    return jax.shard_map(
        on_device,
        mesh=mesh,
        in_specs=(split, split) + (P(),) * 14,
        out_specs=(split, split) + (P(),) * 12,
        check_vma=False,
    )
```

time: 1490 us -> 550 us (0.37)
  local copies, waits for them, and re-layouts: 694 us -> 146 us
  matrix products: 408 us -> 40 us
  other arithmetic: 198 us -> 23.6 us
  Pallas kernels: 0 us -> 135 us
  waiting for transfers between devices: 107 us -> 130 us
    dot_general x47 -> x7, matrix products: 408 us -> 40 us  [the longest x6 39.7 us: relative_bias(): jnp.einsum('habc,ika,jlb,mnc->nklhmij', table_bias, one_hot_offsets(WZ),...]
    reshape x24 -> x7, local copies, waits for them, and re-layouts: 228 us -> 54.7 us  [the longest x2 22.1 us: relative_bias(): return biases.reshape(WINDOW, HEADS * WINDOW)]
    pallas_call x0 -> x1, Pallas kernels: none -> 135 us  [block_call(): pl.pallas_call(block_kernel, grid=(steps,), in_specs=[tile, tile, pl.Bloc...]
    reduce_sum x18 -> x0, other arithmetic: 110 us -> none  [the longest x4 41.7 us: attend_back(): jnp.sum(score_grad, axis=0, dtype=jnp.float32)]
    convert_element_type x16 -> x0, local copies, waits for them, and re-layouts: 95.1 us -> none  [the longest x4 42.9 us: attend_back(): qkv_grad = jnp.stack([query_grad, key_grad, value_grad], axis=2).astype(j...]
    while x62 -> x0, local copies, waits for them, and re-layouts: 78.3 us -> none  [the longest x3 41.6 us: on_device(): lax.scan(attend_back, jnp.zeros(biases.shape, jnp.float32), (qkv_groups,...]
    dynamic_slice x12 -> x0, local copies, waits for them, and re-layouts: 41.1 us -> none  [the longest x8 31.5 us: on_device(): lax.map(attend, (qkv_groups, seg_groups, valid_groups))]
    slice x17 -> x15, local copies, waits for them, and re-layouts: 47.5 us -> 14.2 us  [the longest x4 4.22 us: from_windows(): return jnp.roll(region, WZ // 2, axis=0)]
  transfers between devices with their start and end apart: 9 -> 9, of which waited for: 3 -> 3; matrix products, arithmetic and copies ran while one was open for 16% -> 27% of each run, Pallas kernels for 0% -> 0%
where the time goes in v1:
time: 550 us; the launch traced here: 541 us
  local copies, waits for them, and re-layouts  146 us (27%)
  Pallas kernels  135 us (25%)
  waiting for transfers between devices  130 us (24%)
  matrix products  40 us (7%)
  blocking collectives  39.6 us (7%)
  other arithmetic  23.6 us (4%)
  between operations  15.9 us (3%)
  starting transfers between devices  11.3 us (2%)
    pallas_call x1, Pallas kernels, block_call(): pl.pallas_call(block_kernel, grid=(steps,), in_specs=[tile, tile, pl.Bloc...  135 us
    psum x1, waiting for transfers between devices, on_device(): lax.psum((grad_qkv, grad_qkv_bias, grad_proj, grad_up, grad_up_bias, grad...  91.4 us
    dot_general x6, matrix products, relative_bias(): jnp.einsum('habc,ika,jlb,mnc->nklhmij', table_bias, one_hot_offsets(WZ),...  39.7 us
    psum x1, blocking collectives, on_device(): lax.psum((grad_qkv, grad_qkv_bias, grad_proj, grad_up, grad_up_bias, grad...  39.6 us
    ppermute x8, waiting for transfers between devices, passed_along(): return lax.ppermute(block, axis, route)  38.2 us
    unnamed x67, local copies, waits for them, and re-layouts  26.3 us
    reshape x2, local copies, waits for them, and re-layouts, relative_bias(): return biases.reshape(WINDOW, HEADS * WINDOW)  22.1 us
    reshape x2, local copies, waits for them, and re-layouts, from_windows(): flat.reshape(level_count // WZ, row_count // WY, col_count, WZ, WY, feat_...  16.3 us
  transfers between devices with their start and end apart: 9, of which 3 were waited for; matrix products, arithmetic and copies ran while one was open for 27% of the time, Pallas kernels for 0%

profile of v1, /device:TPU:0, one launch (start us, length us, event | category | flops | bytes accessed | tf_op | source)
XLA Modules:
  0.0 541.2 jit_solution(2434612782123824033)
XLA Ops:
  10.4 2.7 collective-permute-start
  13.2 4.6 slice.100
  17.8 2.3 slice.106
  23.4 2.9 tile.10
  26.2 3.1 copy.118
  29.7 5.2 convolution_bitcast_fusion.1
  36.4 1.7 collective-permute-start.3
  38.2 7.3 %convolution_bitcast_fusion = f32[6,2,12,4,6,2,12]{2,1,5,0,4,3,6:T(2,128)} fusion(f32[12,12,4,3,6,6,1]{1,5,4,3,2,0,6:T(8,128)S(1)} %convolution_bitcast_fusion.1, s32[2,2]{1,0:T(2,128)S(1)} %subtract_add_fusion.2), kind=kOutput, calls=%fused_computation.27 | convolution fusion | flops 2985996 | bytes 580624 | tf_op jit(solution)/shard_map/jvp(habc,ika,jlb,mnc->nklhmij)/dot_general | solution.py:45
  45.5 9.1 %copy.87 = f32[6,2,12,4,6,2,12]{6,5,4,3,2,1,0:T(2,128)} copy(f32[6,2,12,4,6,2,12]{2,1,5,0,4,3,6:T(2,128)} %convolution_bitcast_fusion) | data formatting | bytes 663552 | tf_op jit(solution)/shard_map/jvp(habc,ika,jlb,mnc->nklhmij)/transpose | solution.py:45
  54.6 5.4 %add.153 = f32[144,576]{1,0:T(8,128)S(1)} reshape(f32[6,2,12,4,6,2,12]{6,5,4,3,2,1,0:T(2,128)} %copy.87) | data formatting | bytes 663552 | tf_op jit(solution)/shard_map/add | solution.py:305
  60.0 3.1 copy.116
  64.5 1.9 copy.77
  66.4 1.7 collective-permute-start.1
  70.2 2.3 fusion.8
  72.7 1.6 fusion.7
  74.3 5.4 %copy.84 = bf16[2,2,90,2,12,256]{5,4,3,2,1,0:T(8,128)(2,1)} copy(bf16[2,2,90,2,12,256]{5,2,4,1,3,0:T(8,128)(2,1)S(1)} %bitcast.89) | data formatting | bytes 8847360 | tf_op jit(solution)/shard_map/transpose | solution.py:60
  79.7 8.1 %reshape.262.g_ref = bf16[8640,256]{1,0:T(8,128)(2,1)} reshape(bf16[2,2,90,2,12,256]{5,4,3,2,1,0:T(8,128)(2,1)} %copy.84) | data formatting | bytes 8847360 | tf_op jit(solution)/shard_map/reshape | solution.py:60
  87.9 7.8 %collective-permute-done.1 = bf16[4,6,90,256]{3,0,2,1:T(4,128)(2,1)} collective-permute-done((bf16[4,6,90,256]{3,0,2,1:T(4,128)(2,1)}, bf16[4,6,90,256]{3,0,2,1:T(4,128)(2,1)}, u32[]{:S(2)}, u32[]{:S(2)}) %collective-permute-start.1) | collective-permute-done | bytes 1105952 | tf_op jit(solution)/shard_map/ppermute | solution.py:28
  95.7 1.6 copy.78
  97.3 3.7 fusion.10
  101.3 1.6 fusion.9
  102.9 5.4 %copy.79 = bf16[2,2,90,2,12,256]{5,4,3,2,1,0:T(8,128)(2,1)} copy(bf16[2,2,90,2,12,256]{5,2,4,1,3,0:T(8,128)(2,1)S(1)} %bitcast.90) | data formatting | bytes 8847360 | tf_op jit(solution)/shard_map/transpose | solution.py:60
  108.3 8.1 %reshape.260.x_ref = bf16[8640,256]{1,0:T(8,128)(2,1)} reshape(bf16[2,2,90,2,12,256]{5,4,3,2,1,0:T(8,128)(2,1)} %copy.79) | data formatting | bytes 8847360 | tf_op jit(solution)/shard_map/reshape | solution.py:60
  116.5 135.0 %shard_map.263 = (bf16[8640,256]{1,0:T(8,128)(2,1)}, bf16[8640,256]{1,0:T(8,128)(2,1)}, f32[256,768]{1,0:T(8,128)}, f32[1,768]{1,0:T(1,128)}, f32[256,256]{1,0:T...) custom-call(bf16[8640,256]{1,0:T(8,128)(2,1)} %reshape.260.x_ref, ...), custom_call_target="tpu_custom_call" | custom-call | tf_op jit(solution)/shard_map/pallas_call | solution.py:241
  251.5 8.1 %reshape.264 = bf16[2,2,90,2,12,256]{5,4,3,2,1,0:T(8,128)(2,1)} reshape(bf16[8640,256]{1,0:T(8,128)(2,1)} %get-tuple-element.24) | data formatting | bytes 8847360 | tf_op jit(solution)/shard_map/reshape | solution.py:65
  259.6 5.2 copy.88
  264.9 2.0 slice.133
  266.9 8.2 %reshape.266 = bf16[2,2,90,2,12,256]{5,4,3,2,1,0:T(8,128)(2,1)} reshape(bf16[8640,256]{1,0:T(8,128)(2,1)} %get-tuple-element.25) | data formatting | bytes 8847360 | tf_op jit(solution)/shard_map/reshape | solution.py:65
  275.1 5.2 copy.91
  280.4 2.0 slice.139
  283.8 1.8 copy.89
  286.3 7.4 %reshape.268 = f32[6,2,12,4,6,2,12]{6,5,4,3,2,1,0:T(2,128)} reshape(f32[144,576]{1,0:T(8,128)S(1)} %copy-done.8) | data formatting | bytes 663552 | tf_op jit(solution)/shard_map/transpose(jvp())/reshape | solution.py:53
  293.6 14.7 %copy.94 = f32[6,2,12,4,6,2,12]{0,1,5,4,3,2,6:T(2,128)} copy(f32[6,2,12,4,6,2,12]{6,5,4,3,2,1,0:T(2,128)} %reshape.268) | data formatting | bytes 663552 | tf_op jit(solution)/shard_map/transpose(jvp())/reshape | solution.py:53
  308.4 13.4 %fusion.4 = f32[12,12,4,3,6,6]{5,3,4,2,1,0:T(4,128)S(1)} fusion(f32[6,2,12,4,6,2,12]{0,1,5,4,3,2,6:T(2,128)} %copy.94, s32[2,2]{1,0:T(2,128)S(1)} %subtract_add_fusion.2), kind=kOutput, calls=%fused_computation.4 | convolution fusion | flops 2985996 | bytes 580624 | tf_op jit(solution)/shard_map/transpose(jvp(habc,ika,jlb,mnc->nklhmij))/dot_general | solution.py:45
  321.8 12.7 %fusion.16 = f32[12,12,4,3,11]{1,4,0,3,2:T(8,128)S(1)} fusion(f32[12,12,4,3,6,6]{5,3,4,2,1,0:T(4,128)S(1)} %fusion.4, s32[6,6]{1,0:T(8,128)S(1)} %subtract_add_fusion.1), kind=kOutput, calls=%fused_computation.32 | convolution fusion | flops 8211852 | bytes 325008 | tf_op jit(solution)/shard_map/transpose(jvp(habc,ika,jlb,mnc->nklhmij))/dot_general | solution.py:45
  335.2 39.6 %all-reduce = (f32[1,768]{1,0:T(1,128)S(1)}, f32[8,256]{1,0:T(8,128)S(1)}, f32[1024]{0:T(1024)}, f32[4,3,23,11]{2,3,1,0:T(8,128)S(1)}) all-reduce(f32[1,768]{1,0:T(1,128)S(1)} %copy-done.13, f32[8,256]{1,0:T(8,128)S(1)} %copy-done.11, f32[1024]{0:T(1024)S(1)} %bitcast.103, ...), channel_id=1, replica_groups=mesh['lat'=8,'lon'=4] {'lat','lon'}, use_global_device_ids=true, to_apply=%region_2.3 | all-reduce | flops 6876 | bytes 55008 | tf_op jit(solution)/shard_map/psum | solution.py:319
  376.1 1.9 copy.92
  377.9 3.9 collective-permute-start.6
  382.4 2.1 fusion.14
  387.9 1.4 copy.90
  389.5 30.3 %collective-permute-done.6 = bf16[4,6,90,256]{3,0,2,1:T(4,128)(2,1)} collective-permute-done((bf16[4,6,90,256]{3,0,2,1:T(4,128)(2,1)}, bf16[4,6,90,256]{3,0,2,1:T(4,128)(2,1)}, u32[]{:S(2)}, u32[]{:S(2)}) %collective-permute-start.6) | collective-permute-done | bytes 1105952 | tf_op jit(solution)/shard_map/ppermute | solution.py:28
  421.5 1.5 fusion.12
  425.0 4.7 copy.97
  430.5 4.7 copy.98
  435.2 91.4 %all-reduce.4.cloned.1.call-done = (f32[256,768]{1,0:T(8,128)}, f32[256,256]{1,0:T(8,128)}, f32[256,1024]{1,0:T(8,128)}, f32[1024,256]{0,1:T(8,128)}) async-done(((f32[256,768]{1,0:T(8,128)}, f32[256,256]{1,0:T(8,128)}, f32[256,1024]{1,0:T(8,128)}, f32[1024,256]{0,1:T(8,128)}), (f32[256,768]{1,0:T(8,128)}, f32[256,256]{1,0:T(8,128)}, f32[256,1024]{1,0:T(8,128)}, ...) | async-done | bytes 3145744 | tf_op jit(solution)/shard_map/psum | solution.py:319
  526.6 2.6 copy.99
  529.2 2.1 copy.135
  531.3 1.7 copy.136
  (136 shorter events, 25.1 us)
Async XLA Ops:
  7.2 14.3 %copy-start = (bf16[256,1024]{1,0:T(8,128)(2,1)S(1)}, bf16[256,1024]{1,0:T(8,128)(2,1)}, u32[]{:S(2)}) copy-start(bf16[256,1024]{1,0:T(8,128)(2,1)} %param.27) | copy-start | bytes 1572868
  7.2 519.4 %all-reduce.4.cloned.1.call-start = ((), (), s32[]{:S(2)}) async-start(), calls=%async_computation | async-start | bytes 6291456 | tf_op jit(solution)/shard_map/psum | solution.py:319
  9.0 25.9 %collective-permute-start.2 = (bf16[4,24,3,256]{3,2,1,0:T(4,128)(2,1)}, bf16[4,24,3,256]{3,2,1,0:T(4,128)(2,1)S(1)}, u32[]{:S(2)}, u32[]{:S(2)}) collective-permute-start(bf16[4,24,3,256]{3,2,1,0:T(4,128)(2,1)} %copy.117), channel_id=1, source_target_pairs={{3,0},{0,1},{1,2},{2,3},{7,4},{4,5},{5,6},{6,7},{11,8},{8,9},{9,10... | collective-permute-start | bytes 442376 | tf_op jit(solution)/shard_map/ppermute | solution.py:28
  10.4 7.3 %slice-start.4 = ((s8[4423680]{0:T(1024)(128)(4,1)}), s8[4194304]{0:T(1024)(128)(4,1)S(1)}, s32[]{:S(2)}) async-start(s8[4423680]{0:T(1024)(128)(4,1)} %bitcast.95), calls=%async_computation.5 | async-start | bytes 8388608
  10.4 53.4 %collective-permute-start = (bf16[4,24,3,256]{3,2,1,0:T(4,128)(2,1)S(1)}, bf16[4,24,3,256]{3,2,1,0:T(4,128)(2,1)S(1)}, u32[]{:S(2)}, u32[]{:S(2)}) collective-permute-start(bf16[4,24,3,256]{3,2,1,0:T(4,128)(2,1)S(1)} %copy.115), channel_id=1, source_target_pairs={{3,0},{0,1},{1,2},{2,3},{7,4},{4,5},{5,6},{6,7},{11,8},{8,9},{9,10... | collective-permute-start | bytes 442376 | tf_op jit(solution)/shard_map/ppermute | solution.py:28
  13.2 4.6 slice-start.5
  17.7 3.3 copy-start.16
  17.8 3.6 copy-start.17
  17.8 3.6 copy-start.18
  17.8 3.6 copy-start.19
  17.8 3.6 copy-start.20
  17.8 4.0 copy-start.14
  17.8 4.0 copy-start.15
  26.2 3.1 copy-start.9
  29.3 6.2 %copy-start.2 = (bf16[4,24,87,256]{3,2,1,0:T(8,128)(2,1)}, bf16[4,24,87,256]{3,2,1,0:T(8,128)(2,1)S(1)}, u32[]{:S(2)}) copy-start(bf16[4,24,87,256]{3,2,1,0:T(8,128)(2,1)S(1)} %copy.118) | copy-start | bytes 12828676
  36.4 33.5 %collective-permute-start.3 = (bf16[4,6,90,256]{3,0,2,1:T(4,128)(2,1)S(1)}, bf16[4,6,90,256]{3,0,2,1:T(4,128)(2,1)S(1)}, u32[]{:S(2)}, u32[]{:S(2)}) collective-permute-start(bf16[4,6,90,256]{3,0,2,1:T(4,128)(2,1)S(1)} %copy.82), channel_id=1, source_target_pairs={{28,0},{0,4},{4,8},{8,12},{12,16},{16,20},{20,24},{24,28},{29,1},{... | collective-permute-start | bytes 3317768 | tf_op jit(solution)/shard_map/ppermute | solution.py:28
  63.1 6.8 %copy-start.3 = (bf16[4,24,87,256]{3,2,1,0:T(8,128)(2,1)}, bf16[4,24,87,256]{3,2,1,0:T(8,128)(2,1)S(1)}, u32[]{:S(2)}) copy-start(bf16[4,24,87,256]{3,2,1,0:T(8,128)(2,1)S(1)} %copy.116) | copy-start | bytes 12828676
  63.1 5.6 %copy-start.6 = (f32[4,144,576]{2,1,0:T(8,128)S(1)}, f32[4,144,576]{2,1,0:T(8,128)}, u32[]{:S(2)}) copy-start(f32[4,144,576]{2,1,0:T(8,128)} %tile.10) | copy-start | bytes 3981316
  63.9 6.2 %slice-start = ((s8[4325376]{0:T(1024)(128)(4,1)}), s8[4194304]{0:T(1024)(128)(4,1)S(1)}, s32[]{:S(2)}) async-start(s8[4325376]{0:T(1024)(128)(4,1)} %bitcast.83), calls=%async_computation.1 | async-start | bytes 8388608
  64.5 5.6 %slice-start.1 = ((s8[4325376]{0:T(1024)(128)(4,1)}), s8[131072]{0:T(1024)(128)(4,1)S(1)}, s32[]{:S(2)}) async-start(s8[4325376]{0:T(1024)(128)(4,1)} %bitcast.83), calls=%async_computation.2 | async-start | bytes 262144
  66.4 29.4 %collective-permute-start.1 = (bf16[4,6,90,256]{3,0,2,1:T(4,128)(2,1)}, bf16[4,6,90,256]{3,0,2,1:T(4,128)(2,1)}, u32[]{:S(2)}, u32[]{:S(2)}) collective-permute-start(bf16[4,6,90,256]{3,0,2,1:T(4,128)(2,1)} %copy.77), channel_id=1, source_target_pairs={{28,0},{0,4},{4,8},{8,12},{12,16},{16,20},{20,24},{24,28},{29,1},{... | collective-permute-start | bytes 3317768 | tf_op jit(solution)/shard_map/ppermute | solution.py:28
  95.7 5.6 %slice-start.2 = ((s8[4325376]{0:T(1024)(128)(4,1)}), s8[4194304]{0:T(1024)(128)(4,1)S(1)}, s32[]{:S(2)}) async-start(s8[4325376]{0:T(1024)(128)(4,1)} %bitcast.85), calls=%async_computation.3 | async-start | bytes 8388608
  97.3 4.0 slice-start.3
  280.4 3.3 copy-start.4
  283.6 2.6 copy-start.8
  285.6 102.4 %collective-permute-start.4 = (bf16[4,6,90,256]{3,0,2,1:T(4,128)(2,1)}, bf16[4,6,90,256]{3,0,2,1:T(4,128)(2,1)}, u32[]{:S(2)}, u32[]{:S(2)}) collective-permute-start(bf16[4,6,90,256]{3,0,2,1:T(4,128)(2,1)} %copy.89), channel_id=1, source_target_pairs={{4,0},{8,4},{12,8},{16,12},{20,16},{24,20},{28,24},{0,28},{5,1},{9... | collective-permute-start | bytes 3317768 | tf_op jit(solution)/shard_map/ppermute | solution.py:28
  321.8 13.4 %copy-start.11 = (f32[8,256]{1,0:T(8,128)S(1)}, f32[8,256]{1,0:T(8,128)}, u32[]{:S(2)}) copy-start(f32[8,256]{1,0:T(8,128)} %get-tuple-element.29) | copy-start | bytes 24580
  321.8 13.4 %copy-start.12 = (f32[1,1024]{1,0:T(1,128)S(1)}, f32[1,1024]{1,0:T(1,128)}, u32[]{:S(2)}) copy-start(f32[1,1024]{1,0:T(1,128)} %get-tuple-element.31) | copy-start | bytes 12292
  321.8 13.4 %copy-start.13 = (f32[1,768]{1,0:T(1,128)S(1)}, f32[1,768]{1,0:T(1,128)}, u32[]{:S(2)}) copy-start(f32[1,768]{1,0:T(1,128)} %get-tuple-element.27) | copy-start | bytes 9220
  377.9 41.9 %collective-permute-start.6 = (bf16[4,6,90,256]{3,0,2,1:T(4,128)(2,1)}, bf16[4,6,90,256]{3,0,2,1:T(4,128)(2,1)}, u32[]{:S(2)}, u32[]{:S(2)}) collective-permute-start(bf16[4,6,90,256]{3,0,2,1:T(4,128)(2,1)} %copy.92), channel_id=1, source_target_pairs={{4,0},{8,4},{12,8},{16,12},{20,16},{24,20},{28,24},{0,28},{5,1},{9... | collective-permute-start | bytes 3317768 | tf_op jit(solution)/shard_map/ppermute | solution.py:28
  382.4 2.8 copy-start.5
  386.2 35.1 %copy-start.10 = (f32[1,2,4,128]{3,1,2,0:T(2,128)}, f32[1,2,4,128]{3,1,2,0:T(2,128)S(1)}, u32[]{:S(2)}) copy-start(f32[1,2,4,128]{3,1,2,0:T(2,128)S(1)} %copy.119) | copy-start | bytes 12292
  389.5 34.7 %collective-permute-start.5 = (bf16[4,24,3,256]{3,2,1,0:T(4,128)(2,1)S(1)}, bf16[4,24,3,256]{3,2,1,0:T(4,128)(2,1)S(1)}, u32[]{:S(2)}, u32[]{:S(2)}) collective-permute-start(bf16[4,24,3,256]{3,2,1,0:T(4,128)(2,1)S(1)} %pad_maximum_fusion.13), channel_id=1, source_target_pairs={{1,0},{2,1},{3,2},{0,3},{5,4},{6,5},{7,6},{4,7},{9,8},{10,9},{11,1... | collective-permute-start | bytes 442376 | tf_op jit(solution)/shard_map/ppermute | solution.py:28
  421.4 8.3 %collective-permute-start.7 = (bf16[4,24,3,256]{3,2,1,0:T(4,128)(2,1)S(1)}, bf16[4,24,3,256]{3,2,1,0:T(4,128)(2,1)S(1)}, u32[]{:S(2)}, u32[]{:S(2)}) collective-permute-start(bf16[4,24,3,256]{3,2,1,0:T(4,128)(2,1)S(1)} %pad_maximum_fusion.12), channel_id=1, source_target_pairs={{1,0},{2,1},{3,2},{0,3},{5,4},{6,5},{7,6},{4,7},{9,8},{10,9},{11,1... | collective-permute-start | bytes 442376 | tf_op jit(solution)/shard_map/ppermute | solution.py:28
  430.5 103.4 %copy-start.1 = (bf16[256,1024]{1,0:T(8,128)(2,1)S(1)}, bf16[256,1024]{1,0:T(8,128)(2,1)}, u32[]{:S(2)}) copy-start(bf16[256,1024]{1,0:T(8,128)(2,1)} %param.27) | copy-start | bytes 1572868
  526.6 6.4 %copy-start.7 = (f32[256,1024]{1,0:T(8,128)S(1)}, f32[256,1024]{1,0:T(8,128)}, u32[]{:S(2)}) copy-start(f32[256,1024]{1,0:T(8,128)} %get-tuple-element.113) | copy-start | bytes 3145732
Sparse Core Ops, SparseCore 0:
  382.6 144.0 all-reduce.3

commit v2 on v1

v2 whole, which is shorter than its diff:
```python
import functools
import math

import jax
import jax.numpy as jnp
from jax import lax
from jax.experimental import pallas as pl
from jax.experimental.pallas import tpu as pltpu
from jax.sharding import PartitionSpec as P

WZ = 2
WY = 12
WX = 6
CELLS = WZ * WY
WINDOW = CELLS * WX
HEADS = 4
SCORES = HEADS * WINDOW
HALF_Y = WY // 2
HALF_X = WX // 2
BLOCK_WINDOWS = 5
OFFSETS = (2 * WZ - 1) * (2 * WX - 1)
VECTORS = 16
TABLE_ROWS = 2 * WY
EDGE = HALF_X * CELLS
PACKED_COLS = 8

NORM_EPSILON = 1e-05
MASKED_SCORE = -1000000000.0
F32 = jnp.float32
BF16 = jnp.bfloat16
MESH = pl.DeviceIdType.MESH
ANY = pl.BlockSpec(memory_space=pl.ANY)
VMEM_LIMIT = 60 * 2**20


def dot_nn(left, right):
    return lax.dot_general(left, right, (((1,), (0,)), ((), ())), preferred_element_type=F32)


def dot_nt(left, right):
    return lax.dot_general(left, right, (((1,), (1,)), ((), ())), preferred_element_type=F32)


def dot_tn(left, right):
    return lax.dot_general(left, right, (((0,), (0,)), ((), ())), preferred_element_type=F32)


def iota(shape, axis):
    return lax.broadcasted_iota(jnp.int32, shape, axis)


def whole(shape, buffers=1):
    return pl.BlockSpec(
        shape, lambda *_: (0,) * len(shape), pipeline_mode=pl.Buffered(buffers)
    )


def shape_of(shape, dtype):
    return jax.ShapeDtypeStruct(shape, dtype)


def strips_kernel(tokens_ref, cotangent_ref, rows_ref, cols_ref):
    _, col_count, row_count, width = tokens_ref.shape
    for a, ref in enumerate((tokens_ref, cotangent_ref)):
        cols_ref[a, 0] = ref[0, col_count - HALF_X :].reshape(HALF_X * row_count, width)
        for start in range(0, col_count, PACKED_COLS):
            count = min(PACKED_COLS, col_count - start)
            block = ref[0, start : start + count].astype(F32)
            packed = jnp.concatenate(
                [block[c, row_count - HALF_Y :] for c in range(count)], axis=0
            )
            rows_ref[a, 0, start * HALF_Y : (start + count) * HALF_Y, :] = packed.astype(BF16)


def packed_rows(col_count):
    return -(-col_count * HALF_Y // 16) * 16


def cut_strips(tokens, cotangent):
    level_count, col_count, row_count, width = tokens.shape
    field = pl.BlockSpec((1, col_count, row_count, width), lambda i: (i, 0, 0, 0))

    def strip(count):
        return pl.BlockSpec((2, 1, count, width), lambda i: (0, i, 0, 0))

    counts = (packed_rows(col_count), HALF_X * row_count)
    return pl.pallas_call(
        strips_kernel,
        grid=(level_count,),
        in_specs=[field, field],
        out_specs=[strip(count) for count in counts],
        out_shape=[shape_of((2, level_count, count, width), BF16) for count in counts],
        compiler_params=pltpu.CompilerParams(vmem_limit_bytes=VMEM_LIMIT),
    )(tokens, cotangent)


def offset_pick(key_x, key_z):
    lane = iota((HEADS * OFFSETS, SCORES), 1)
    head, rest = lane // WINDOW, lane % WINDOW
    query_x, query_z = rest // CELLS, (rest % CELLS) // WY
    offset_z, offset_x = query_z - key_z + WZ - 1, query_x - key_x + WX - 1
    place = (offset_z * (2 * WX - 1) + offset_x) * HEADS + head
    return iota((HEADS * OFFSETS, SCORES), 0) == place


def setup_kernel(
    lead_ref, w_mod_ref, b_mod_ref, b_proj_ref, b_down_ref, q_bias_ref, v_bias_ref, b_up_ref,
    table_ref, bias_ref, vec_ref, context_ref,
):
    width = w_mod_ref.shape[0]
    half = width // 2
    lanes = context_ref.shape[1]
    fraction = iota((half, lanes), 0).astype(F32) / half
    angles = lead_ref[0].astype(F32) * jnp.exp(-math.log(1000.0) * fraction)
    waves = jnp.concatenate([jnp.sin(angles), jnp.cos(angles)], axis=0)
    context = waves * (1.0 / (1.0 + jnp.exp(-waves)))
    context_ref[...] = context
    for part in range(4):
        pieces = []
        for j in range(width // lanes):
            start = part * width + j * lanes
            pieces.append(
                jnp.sum(context * w_mod_ref[:, start : start + lanes].astype(F32), axis=0, keepdims=True)
            )
        vec_ref[part : part + 1, :] = jnp.concatenate(pieces, axis=1) + b_mod_ref[
            :, part * width : (part + 1) * width
        ].astype(F32)
    rows = [b_proj_ref[...], b_down_ref[...], q_bias_ref[...], jnp.zeros((1, width), BF16), v_bias_ref[...]]
    rows += [b_up_ref[:, j * width : (j + 1) * width] for j in range(4)]
    rows += [jnp.zeros((1, width), BF16)] * (VECTORS - 4 - len(rows))
    for i, row in enumerate(rows):
        vec_ref[4 + i : 5 + i, :] = row.astype(F32)

    offsets_y = 2 * WY - 1
    backwards = iota((TABLE_ROWS, offsets_y), 0) + iota((TABLE_ROWS, offsets_y), 1) == offsets_y - 1
    table = dot_nt(backwards.astype(BF16), table_ref[...]).astype(BF16)
    query_y = iota((WY, SCORES), 1) % WY
    for key_x in range(WX):
        for key_z in range(WZ):
            spread = dot_nn(table, offset_pick(key_x, key_z).astype(BF16))
            rows = spread[WY - 1 : 2 * WY - 1]
            for y in range(1, WY):
                rows = jnp.where(query_y == y, spread[WY - 1 - y : 2 * WY - 1 - y], rows)
            start = key_x * CELLS + key_z * WY
            bias_ref[start : start + WY, :] = rows


def set_up(lead_hours, w_mod, b_mod, b_proj, b_down, q_bias, v_bias, b_up, table):
    width = w_mod.shape[0]
    vmem = pl.BlockSpec(memory_space=pltpu.VMEM)
    vectors = [v[None] for v in (b_mod, b_proj, b_down, q_bias, v_bias, b_up)]
    return pl.pallas_call(
        setup_kernel,
        in_specs=[pl.BlockSpec(memory_space=pltpu.SMEM)] + [vmem] * 8,
        out_specs=[vmem] * 3,
        out_shape=[
            shape_of((WINDOW, SCORES), F32),
            shape_of((VECTORS, width), F32),
            shape_of((width, 128), F32),
        ],
        compiler_params=pltpu.CompilerParams(vmem_limit_bytes=VMEM_LIMIT),
    )(lead_hours, w_mod, *vectors, table)


def table_grad(score_sum_ref):
    query_y = iota((WY, SCORES), 1) % WY
    total = jnp.zeros((TABLE_ROWS, HEADS * OFFSETS), F32)
    for key_x in range(WX):
        for key_z in range(WZ):
            start = key_x * CELLS + key_z * WY
            rows = score_sum_ref[start : start + WY, :]
            spread = jnp.zeros((TABLE_ROWS, SCORES), F32)
            for y in range(WY):
                own = jnp.where(query_y == y, rows, 0.0)
                pads = (WY - 1 - y, TABLE_ROWS - (2 * WY - 1 - y))
                parts = [jnp.zeros((p, SCORES), F32) for p in pads]
                spread = spread + jnp.concatenate(
                    ([parts[0]] if pads[0] else []) + [own, parts[1]], axis=0
                )
            pick = offset_pick(key_x, key_z).astype(BF16)
            high = spread.astype(BF16)
            low = (spread - high.astype(F32)).astype(BF16)
            total = total + dot_nt(high, pick) + dot_nt(low, pick)
    return total


def row_mean(values):
    return jnp.mean(values, axis=-1, keepdims=True)


def norm(values):
    center = values - row_mean(values)
    inverse = lax.rsqrt(row_mean(center * center) + NORM_EPSILON)
    return center * inverse, inverse


def norm_back(grad, normed, inverse):
    return inverse * (grad - row_mean(grad) - normed * row_mean(grad * normed))


def gelu_both(values):
    gauss_cdf = 0.5 * (1.0 + lax.erf(values * math.sqrt(0.5)))
    density = jnp.exp(values * values * -0.5) * (1.0 / math.sqrt(2.0 * math.pi))
    return values * gauss_cdf, gauss_cdf + values * density


def by_head(values):
    width = values.shape[-1] // HEADS
    lane_head = iota(values.shape, 1) // width
    zero = jnp.zeros_like(values)
    return jnp.concatenate([jnp.where(lane_head == h, values, zero) for h in range(HEADS)], axis=0)


def own_head(stacked):
    cells = stacked.shape[0] // HEADS
    width = stacked.shape[-1] // HEADS
    lane_head = iota((cells, stacked.shape[-1]), 1) // width
    picked = stacked[:cells]
    for h in range(1, HEADS):
        picked = jnp.where(lane_head == h, stacked[h * cells : (h + 1) * cells], picked)
    return picked


def store_windows(field, z_pieces, out_ref):
    width = out_ref.shape[1]
    for c in range(HALF_X):
        out_ref[c * CELLS : (c + 1) * CELLS, :] = jnp.concatenate(
            [z_pieces(c, z) for z in range(WZ)], axis=0
        )
    own_cols = out_ref.shape[0] // CELLS - HALF_X
    for start in range(0, own_cols, PACKED_COLS):
        count = min(PACKED_COLS, own_cols - start)
        both = jnp.concatenate([field(start, count, z) for z in range(WZ)], axis=1)
        first = (start + HALF_X) * CELLS
        out_ref[first : first + count * CELLS, :] = both.reshape(count * CELLS, width)


def unpack_strip(rows, count):
    return jnp.stack([rows[c * HALF_Y : (c + 1) * HALF_Y] for c in range(count)], axis=0)


def mask_scores(bias, level_wraps, straddles, first_band, crop_own, crop_before, row_count):
    def parts(cell):
        z, y = (cell % CELLS) // WY, cell % WY
        part = 2 * jnp.where(z == WZ - 1, level_wraps, 0)
        if straddles:
            part = part + jnp.where(y >= HALF_Y, first_band, 0)
            own = y - HALF_Y >= row_count - crop_own
            before = row_count - HALF_Y + y >= row_count - crop_before
            valid = jnp.where(y >= HALF_Y, own.astype(jnp.int32), before.astype(jnp.int32))
        else:
            valid = (HALF_Y + y >= row_count - crop_own).astype(jnp.int32)
        return part, valid

    key = iota(bias.shape, 0)
    query = iota(bias.shape, 1) % WINDOW
    key_part, key_valid = parts(key)
    query_part, _ = parts(query)
    allowed = (key_part == query_part) & ((key_valid > 0) | (key == query))
    return jnp.where(allowed, bias, bias + MASKED_SCORE)


def block_kernel(straddles, first_pair, last, *refs):
    refs = list(refs)

    def take(count):
        taken, refs[:count] = refs[:count], []
        return taken

    (crop_ref,) = take(1)
    field_refs = [take(WZ), take(WZ)]
    col_refs = [take(WZ), take(WZ)]
    row_refs, corner_refs = ([take(WZ), take(WZ)], [take(WZ), take(WZ)]) if straddles else (None, None)
    bias_ref, vec_ref, w_qkv_ref, w_proj_ref, w_up_ref, w_down_ref = take(6)
    grad_in_ref, small_in_ref, scores_in_ref = take(3)
    out_ref, edge_ref, grad_ref, small_ref = take(4)
    (score_sum_ref,) = take(0 if last else 1) or (None,)
    (back_ref,) = take(1 if straddles else 0) or (None,)
    score_bias_ref, xw_ref, gw_ref, qkv_ref, prob_ref, att_ref, dqkv_ref = take(7)
    if last:
        (score_sum_ref,) = take(1)

    step = pl.program_id(0)
    width = vec_ref.shape[1]
    hidden_width = w_up_ref.shape[1]
    _, col_count, row_count, _ = field_refs[0][0].shape
    band_count = crop_ref.shape[0]
    score_scale = (width // HEADS) ** -0.5

    @pl.when(step == 0)
    def _():
        grad_ref[...] = grad_in_ref[...]
        small_ref[...] = small_in_ref[...]
        score_sum_ref[...] = scores_in_ref[...]

    band = lax.axis_index("lat")
    score_bias_ref[...] = mask_scores(
        bias_ref[...], (step + first_pair == 1).astype(jnp.int32), straddles,
        (band == 0).astype(jnp.int32), crop_ref[band],
        crop_ref[lax.rem(band + band_count - 1, band_count)], row_count,
    )

    for a, target in enumerate((xw_ref, gw_ref)):
        def field(start, count, z, a=a):
            rows = field_refs[a][z][0, start : start + count].astype(F32)
            if not straddles:
                return rows[:, HALF_Y : HALF_Y + WY]
            strip = row_refs[a][z][0, 0, start * HALF_Y : (start + count) * HALF_Y, :].astype(F32)
            return jnp.concatenate([unpack_strip(strip, count), rows[:, :HALF_Y]], axis=1)

        def western(c, z, a=a):
            own = slice(c * row_count, (c + 1) * row_count)
            rows = col_refs[a][z][0, 0, own, :].astype(F32)
            if not straddles:
                return rows[HALF_Y : HALF_Y + WY]
            before = corner_refs[a][z][0, 0, own, :].astype(F32)
            return jnp.concatenate([before[row_count - HALF_Y :], rows[:HALF_Y]], axis=0)

        store_windows(field, western, target)

    rows = BLOCK_WINDOWS * WINDOW
    shift_one, scale_one, shift_two, scale_two, b_proj, b_down = [
        vec_ref[i : i + 1, :] for i in range(6)
    ]
    qkv_shift = jnp.concatenate([vec_ref[i : i + 1, :] for i in range(6, 9)], axis=1)
    b_up = jnp.concatenate([vec_ref[i : i + 1, :] for i in range(9, 13)], axis=1)

    def add_grad(first, value):
        for j in range(value.shape[1] // width):
            grad_ref[(first + j) * width : (first + j + 1) * width, :] += value[
                :, j * width : (j + 1) * width
            ]

    def block(index, carry):
        here = pl.ds(pl.multiple_of(index * rows, 16), rows)
        x32 = xw_ref[here, :]
        x = x32.astype(BF16)
        qkv_ref[...] = (dot_nn(x, w_qkv_ref[...]) + qkv_shift).astype(BF16)
        for w in range(BLOCK_WINDOWS):
            cells = pl.ds(w * WINDOW, WINDOW)
            queries = by_head(qkv_ref[cells, :width] * BF16(score_scale))
            scores = dot_nt(qkv_ref[cells, width : 2 * width], queries) + score_bias_ref[...]
            top = jnp.max(scores, axis=0, keepdims=True)
            exps = jnp.exp(scores - top)
            prob = exps * (1.0 / jnp.sum(exps, axis=0, keepdims=True))
            prob_ref[w] = prob
            att_ref[cells, :] = own_head(
                dot_tn(prob.astype(BF16), qkv_ref[cells, 2 * width :])
            ).astype(BF16)

        att = att_ref[...]
        branch = dot_nn(att, w_proj_ref[...]) + b_proj
        norm_one, inverse_one = norm(branch)
        middle = x32 + norm_one * (1.0 + scale_one) + shift_one
        middle_low = middle.astype(BF16)
        pre = dot_nn(middle_low, w_up_ref[...]) + b_up
        hidden, slope = gelu_both(pre)
        hidden = hidden.astype(BF16)
        second = dot_nn(hidden, w_down_ref[...]) + b_down
        norm_two, inverse_two = norm(second)
        out_ref[0, 0, here, :] = (middle + norm_two * (1.0 + scale_two) + shift_two).astype(BF16)

        g = gw_ref[here, :]
        second_low = norm_back(g * (1.0 + scale_two), norm_two, inverse_two).astype(BF16)
        add_grad(8, dot_tn(second_low, hidden))
        pre_grad = dot_nt(second_low, w_down_ref[...]) * slope
        pre_low = pre_grad.astype(BF16)
        add_grad(4, dot_tn(middle_low, pre_low))
        middle_grad = g + dot_nt(pre_low, w_up_ref[...])
        branch_low = norm_back(middle_grad * (1.0 + scale_one), norm_one, inverse_one).astype(BF16)
        add_grad(3, dot_tn(att, branch_low))
        att_ref[...] = dot_nt(branch_low, w_proj_ref[...]).astype(BF16)

        for w in range(BLOCK_WINDOWS):
            cells = pl.ds(w * WINDOW, WINDOW)
            queries = by_head(qkv_ref[cells, :width] * BF16(score_scale))
            out_grad = by_head(att_ref[cells, :])
            prob = prob_ref[w]
            prob_grad = dot_nt(qkv_ref[cells, 2 * width :], out_grad)
            score_grad = prob * (prob_grad - jnp.sum(prob_grad * prob, axis=0, keepdims=True))
            score_sum_ref[...] += score_grad
            score_grad = score_grad.astype(BF16)
            dqkv_ref[cells, :width] = (
                own_head(dot_tn(score_grad, qkv_ref[cells, width : 2 * width])) * score_scale
            ).astype(BF16)
            dqkv_ref[cells, width : 2 * width] = dot_nn(score_grad, queries).astype(BF16)
            dqkv_ref[cells, 2 * width :] = dot_nn(prob.astype(BF16), out_grad).astype(BF16)

        dqkv = dqkv_ref[...]
        add_grad(0, dot_tn(x, dqkv))
        out_ref[1, 0, here, :] = (middle_grad + dot_nt(dqkv, w_qkv_ref[...])).astype(BF16)

        def column_sums(values):
            return jnp.sum(values, axis=0, keepdims=True)

        qkv_sums = column_sums(dqkv.astype(F32))
        up_sums = column_sums(pre_grad)
        sums = [
            column_sums(middle_grad), column_sums(middle_grad * norm_one), column_sums(g),
            column_sums(g * norm_two), column_sums(branch_low.astype(F32)),
            column_sums(second_low.astype(F32)),
        ]
        sums += [qkv_sums[:, j * width : (j + 1) * width] for j in range(3)]
        sums += [up_sums[:, j * width : (j + 1) * width] for j in range(hidden_width // width)]
        sums += [jnp.zeros((VECTORS - len(sums), width), F32)]
        small_ref[:VECTORS, :] += jnp.concatenate(sums, axis=0)
        return carry

    lax.fori_loop(0, col_count // WX // BLOCK_WINDOWS, block, 0)
    for a in range(2):
        edge_ref[a, 0] = out_ref[a, 0, :EDGE, :]
        if straddles:
            for start in range(0, col_count - HALF_X, PACKED_COLS):
                count = min(PACKED_COLS, col_count - HALF_X - start)
                first = (start + HALF_X) * CELLS
                cells = out_ref[a, 0, first : first + count * CELLS, :].astype(F32)
                for z in range(WZ):
                    pieces = [
                        cells[c * CELLS + z * WY : c * CELLS + z * WY + HALF_Y] for c in range(count)
                    ]
                    back_ref[a, z, start * HALF_Y : (start + count) * HALF_Y, :] = jnp.concatenate(
                        pieces, axis=0
                    ).astype(BF16)
    if last:
        @pl.when(step == pl.num_programs(0) - 1)
        def _():
            small_ref[VECTORS:, : HEADS * OFFSETS] = table_grad(score_sum_ref)


def block_call(straddles, first_pair, pair_count, last, crop_rows, fields, halos, constants, sums):
    level_count, col_count, row_count, width = fields[0].shape

    def level_of(i, z):
        return (WZ * (i + first_pair) + z + WZ // 2) % level_count

    specs, values = [pl.BlockSpec(memory_space=pltpu.SMEM)], [crop_rows]
    for field in fields:
        for z in range(WZ):
            specs.append(pl.BlockSpec(
                (1, col_count, row_count, width), lambda i, z=z: (level_of(i, z), 0, 0, 0)
            ))
            values.append(field)
    for halo in halos:
        for a in range(2):
            for z in range(WZ):
                specs.append(pl.BlockSpec(
                    (1, 1) + halo.shape[2:], lambda i, a=a, z=z: (a, level_of(i, z), 0, 0)
                ))
                values.append(halo)
    specs += [whole(v.shape) for v in constants + sums]
    values += constants + sums

    cells = col_count * CELLS
    kept = sums[:2] if last else sums
    out_specs = [
        pl.BlockSpec((2, 1, count, width), lambda i: (0, i, 0, 0)) for count in (cells, EDGE)
    ] + [whole(v.shape) for v in kept]
    out_shape = [shape_of((2, pair_count, count, width), BF16) for count in (cells, EDGE)]
    out_shape += [shape_of(v.shape, F32) for v in kept]
    if straddles:
        packed = packed_rows(col_count)
        out_specs.append(pl.BlockSpec((2, WZ, packed, width), lambda i: (0, i, 0, 0)))
        out_shape.append(shape_of((2, pair_count * WZ, packed, width), BF16))
    rows = BLOCK_WINDOWS * WINDOW
    scratch = [
        pltpu.VMEM((WINDOW, SCORES), F32),
        pltpu.VMEM((cells, width), F32),
        pltpu.VMEM((cells, width), F32),
        pltpu.VMEM((rows, 3 * width), BF16),
        pltpu.VMEM((BLOCK_WINDOWS, WINDOW, SCORES), F32),
        pltpu.VMEM((rows, width), BF16),
        pltpu.VMEM((rows, 3 * width), BF16),
    ]
    if last:
        scratch.append(pltpu.VMEM((WINDOW, SCORES), F32))
    return pl.pallas_call(
        functools.partial(block_kernel, straddles, first_pair, last),
        grid=(pair_count,),
        in_specs=specs,
        out_specs=out_specs,
        out_shape=out_shape,
        scratch_shapes=scratch,
        cost_estimate=pl.CostEstimate(
            flops=pair_count * cells * 5_200_000, bytes_accessed=16 * 2**20, transcendentals=0
        ),
        compiler_params=pltpu.CompilerParams(vmem_limit_bytes=VMEM_LIMIT),
    )(*values)


def halved(rows, count):
    sizes = [rows >> (i + 1) for i in range(count)]
    return sizes, [sum(sizes[:i]) for i in range(count + 1)]


def sum_kernel(
    bits, halvings, parts, grad_ref, small_ref, out_ref, small_out_ref,
    acc_ref, send_ref, recv_ref, more_ref, small_recv_ref, sems, small_sems,
):
    axes = ("lat", "lon")
    places = {axis: lax.axis_index(axis) for axis in axes}
    own_bit, partner = {}, {}
    for axis, bit in bits:
        value = (places[axis] // 2**bit) % 2
        own_bit[axis, bit] = value
        moved = dict(places)
        moved[axis] = places[axis] + 2**bit * (1 - 2 * value)
        partner[axis, bit] = tuple(moved[name] for name in axes)

    barrier = pltpu.get_barrier_semaphore()
    for bit in bits:
        pl.semaphore_signal(barrier, inc=1, device_id=partner[bit], device_id_type=MESH)
    pl.semaphore_wait(barrier, len(bits))

    def send(source, target, pair, bit):
        copy = pltpu.make_async_remote_copy(
            src_ref=source, dst_ref=target, send_sem=pair.at[0], recv_sem=pair.at[1],
            device_id=partner[bit], device_id_type=MESH,
        )
        copy.start()
        return copy

    part_rows = grad_ref.shape[0] // parts
    sizes, starts = halved(part_rows, halvings)
    shard = sizes[-1]
    orders = []
    for p in range(parts):
        order = list(bits[:halvings])
        if p == 1 and halvings > 2:
            order[1], order[2] = order[2], order[1]
        orders.append(order)
    low = [p * part_rows for p in range(parts)]
    small_out_ref[...] = small_ref[...]
    acc_ref[...] = grad_ref[...]

    def halve(p, s):
        bit, size = orders[p][s], sizes[s]
        place = pl.ds(p * starts[-1] + starts[s], size)
        away = pl.multiple_of(low[p] + (1 - own_bit[bit]) * size, 16)
        send_ref[place, :] = acc_ref[pl.ds(away, size), :].astype(BF16)
        low[p] = low[p] + own_bit[bit] * size
        return send(send_ref.at[place], recv_ref.at[place], sems.at[p, s], bit)

    def add_half(p, s, copy):
        size = sizes[s]
        copy.wait()
        place = pl.ds(p * starts[-1] + starts[s], size)
        here = pl.ds(pl.multiple_of(low[p], 16), size)
        acc_ref[here, :] += recv_ref[place, :].astype(F32)

    copies = [halve(p, 0) for p in range(parts)]
    for s, bit in enumerate(bits):
        small_copy = send(small_out_ref, small_recv_ref.at[s], small_sems.at[s], bit)
        if s < halvings:
            for p in range(parts):
                add_half(p, s, copies[p])
                if s + 1 < halvings:
                    copies[p] = halve(p, s + 1)
        small_copy.wait()
        small_out_ref[...] += small_recv_ref[s]

    for p in range(parts):
        here = pl.ds(pl.multiple_of(low[p], 16), shard)
        out_ref[here, :] = acc_ref[here, :].astype(BF16)
        for s in range(halvings, len(bits)):
            mine = more_ref.at[0, p, s - halvings]
            theirs = more_ref.at[1, p, s - halvings]
            mine[...] = out_ref[here, :]
            send(mine, theirs, sems.at[p, s], bits[s]).wait()
            out_ref[here, :] = (mine[...].astype(F32) + theirs[...].astype(F32)).astype(BF16)

    def give(p, s):
        here = out_ref.at[pl.ds(pl.multiple_of(low[p], 16), sizes[s]), :]
        low[p] = low[p] - own_bit[orders[p][s]] * sizes[s]
        return send(here, here, sems.at[p, len(bits) + s], orders[p][s])

    copies = [give(p, halvings - 1) for p in range(parts)]
    for s in reversed(range(halvings)):
        for p in range(parts):
            copies[p].wait()
            if s:
                copies[p] = give(p, s - 1)


def sum_over_devices(grad, small):
    bits = [("lon", 0), ("lon", 1), ("lat", 0), ("lat", 1), ("lat", 2)]
    bits = [b for b in bits if 2 ** b[1] < lax.axis_size(b[0])]
    bits += [("lat", b) for b in range(3, lax.axis_size("lat").bit_length() - 1)]
    bits += [("lon", b) for b in range(2, lax.axis_size("lon").bit_length() - 1)]
    if not bits:
        return grad.astype(BF16), small
    halvings, parts = min(5, len(bits)), 2
    rows, width = grad.shape
    sizes, starts = halved(rows // parts, halvings)
    more = max(1, len(bits) - halvings)
    vmem = pl.BlockSpec(memory_space=pltpu.VMEM)
    return pl.pallas_call(
        functools.partial(sum_kernel, tuple(bits), halvings, parts),
        in_specs=[vmem, vmem],
        out_specs=[vmem, vmem],
        out_shape=[shape_of(grad.shape, BF16), shape_of(small.shape, F32)],
        scratch_shapes=[
            pltpu.VMEM(grad.shape, F32),
            pltpu.VMEM((parts * starts[-1], width), BF16),
            pltpu.VMEM((parts * starts[-1], width), BF16),
            pltpu.VMEM((2, parts, more, sizes[-1], width), BF16),
            pltpu.VMEM((len(bits),) + small.shape, F32),
            pltpu.SemaphoreType.DMA((parts, len(bits) + halvings, 2)),
            pltpu.SemaphoreType.DMA((len(bits), 2)),
        ],
        compiler_params=pltpu.CompilerParams(
            collective_id=0, has_side_effects=True, vmem_limit_bytes=VMEM_LIMIT
        ),
    )(grad, small)


def merge_kernel(
    first_ref, second_ref, straddle_ref, rows_ref, first_edge_ref, second_edge_ref,
    straddle_edge_ref, corner_ref, grad_ref, small_ref, context_ref, *out_refs,
):
    fields, grads = out_refs[:2], out_refs[2:]
    _, col_count, row_count, width = fields[0].shape
    step = pl.program_id(0)

    def piece(ref, a, first_col, count, first, size):
        block = ref[a, 0, first_col * CELLS : (first_col + count) * CELLS, :].astype(F32)
        return block.reshape(count, CELLS, width)[:, first : first + size]

    for pair, z in ((0, 0), (0, 1), (1, 0), (1, 1)):
        inner_ref = (first_ref, second_ref)[pair]
        inner_edge_ref = (first_edge_ref, second_edge_ref)[pair]

        @pl.when(step == pair * WZ + z)
        def _():
            first = z * WY
            for a, field in enumerate(fields):
                for start in range(0, col_count - HALF_X, PACKED_COLS):
                    count = min(PACKED_COLS, col_count - HALF_X - start)
                    strip = rows_ref[a, 0, start * HALF_Y : (start + count) * HALF_Y, :]
                    block = jnp.concatenate([
                        piece(straddle_ref, a, start + HALF_X, count, first + HALF_Y, HALF_Y),
                        piece(inner_ref, a, start + HALF_X, count, first, WY),
                        unpack_strip(strip.astype(F32), count),
                    ], axis=1)
                    field[0, start : start + count] = block.astype(BF16)
                block = jnp.concatenate([
                    piece(straddle_edge_ref, a, 0, HALF_X, first + HALF_Y, HALF_Y),
                    piece(inner_edge_ref, a, 0, HALF_X, first, WY),
                    piece(corner_ref, a, 0, HALF_X, first, HALF_Y),
                ], axis=1)
                field[0, col_count - HALF_X :] = block.astype(BF16)

    grad_qkv, grad_proj, grad_up, grad_down, grad_mod, *vectors = grads

    def slab(index):
        return grad_ref[index * width : (index + 1) * width, :].astype(F32)

    @pl.when(step == 0)
    def _():
        for j in range(3):
            grad_qkv[:, j * width : (j + 1) * width] = slab(j)
        grad_proj[...] = slab(3)

    @pl.when(step == 1)
    def _():
        for j in range(grad_up.shape[1] // width):
            grad_up[:, j * width : (j + 1) * width] = slab(4 + j)

    @pl.when(step == 2)
    def _():
        for j in range(grad_down.shape[0] // width):
            grad_down[j * width : (j + 1) * width, :] = slab(8 + j).T

    @pl.when(step == 3)
    def _():
        lanes = context_ref.shape[1]
        for part in range(4):
            row = small_ref[part : part + 1, :]
            for j in range(0, width, lanes):
                grad_mod[:, part * width + j : part * width + j + lanes] = (
                    context_ref[...] * row[:, j : j + lanes]
                )
        mod_bias, proj_bias, down_bias, q_bias, v_bias, up_bias = vectors
        mod_bias[...] = jnp.concatenate([small_ref[i : i + 1, :] for i in range(4)], axis=1)
        up_bias[...] = jnp.concatenate([small_ref[i : i + 1, :] for i in range(9, 13)], axis=1)
        for ref, i in ((proj_bias, 4), (down_bias, 5), (q_bias, 6), (v_bias, 8)):
            ref[...] = small_ref[i : i + 1, :]


def merge(
    field_shape, hidden_width, first, second, straddle, rows, first_edge, second_edge,
    straddle_edge, corner, grad, small, context,
):
    level_count, col_count, row_count, width = field_shape

    def level_of(i):
        return (i + WZ // 2) % level_count

    def by_pair(value):
        return pl.BlockSpec((2, 1) + value.shape[2:], lambda i: (0, i // WZ, 0, 0))

    shapes = [
        (width, 3 * width), (width, width), (width, hidden_width), (hidden_width, width),
        (width, 4 * width), (1, 4 * width), (1, width), (1, width), (1, width), (1, width),
        (1, hidden_width),
    ]
    field = pl.BlockSpec((1,) + field_shape[1:], lambda i: (level_of(i), 0, 0, 0))
    return pl.pallas_call(
        merge_kernel,
        grid=(level_count,),
        in_specs=[
            whole(first.shape), whole(second.shape), by_pair(straddle),
            pl.BlockSpec((2, 1) + rows.shape[2:], lambda i: (0, i, 0, 0)),
            whole(first_edge.shape), whole(second_edge.shape), by_pair(straddle_edge),
            by_pair(corner),
        ] + [whole(v.shape) for v in (grad, small, context)],
        out_specs=[field, field] + [whole(s) for s in shapes],
        out_shape=[shape_of(field_shape, BF16)] * 2 + [shape_of(s, F32) for s in shapes],
        compiler_params=pltpu.CompilerParams(vmem_limit_bytes=VMEM_LIMIT),
    )(
        first, second, straddle, rows, first_edge, second_edge, straddle_edge, corner, grad, small,
        context,
    )


def pass_along(block, lat_step, lon_step):
    lat, lon = lax.axis_size("lat"), lax.axis_size("lon")
    route = []
    for i in range(lat):
        for j in range(lon):
            target = ((i + lat_step) % lat) * lon + (j + lon_step) % lon
            route.append((i * lon + j, target))
    return lax.ppermute(block, ("lat", "lon"), route)


def on_device(
    tokens, cotangent, w_qkv, q_bias, v_bias, w_proj, b_proj, w_up, b_up, w_down, b_down,
    w_mod, b_mod, rel_table, crop_rows, lead_hours,
):
    width = tokens.shape[-1]
    fields = [field.transpose(0, 2, 1, 3) for field in (tokens, cotangent)]
    rows, own_cols = cut_strips(*fields)
    cols = pass_along(own_cols, 0, 1)
    rows = pass_along(rows, 1, 0)
    corner = pass_along(own_cols, 1, 1)

    table = rel_table.transpose(1, 3, 0, 2).reshape(HEADS * OFFSETS, 2 * WY - 1)
    bias, vecs, context = set_up(
        lead_hours, w_mod, b_mod, b_proj, b_down, q_bias, v_bias, b_up, table
    )
    constants = [bias, vecs, w_qkv, w_proj, w_up, w_down]
    sums = [
        jnp.zeros((4 * width + 2 * w_up.shape[1], width), F32),
        jnp.zeros((VECTORS + TABLE_ROWS, width), F32),
        jnp.zeros((WINDOW, SCORES), F32),
    ]
    first, first_edge, *sums = block_call(
        False, 0, 1, False, crop_rows, fields, [cols], constants, sums
    )
    straddle, straddle_edge, *sums, rows_back = block_call(
        True, 0, 2, False, crop_rows, fields, [cols, rows, corner], constants, sums
    )
    rows_back = pass_along(rows_back, -1, 0)
    corner_back = pass_along(straddle_edge, -1, -1)
    straddle_edge = pass_along(straddle_edge, 0, -1)
    first_edge = pass_along(first_edge, 0, -1)
    second, second_edge, grad, small = block_call(
        False, 1, 1, True, crop_rows, fields, [cols], constants, sums
    )
    second_edge = pass_along(second_edge, 0, -1)
    grad, small = sum_over_devices(grad, small)
    (
        mixed, token_grad, grad_qkv, grad_proj, grad_up, grad_down, grad_mod, grad_mod_bias,
        grad_proj_bias, grad_down_bias, grad_q_bias, grad_v_bias, grad_up_bias,
    ) = merge(
        fields[0].shape, w_up.shape[1], first, second, straddle, rows_back, first_edge, second_edge,
        straddle_edge, corner_back, grad, small, context,
    )
    table_sum = small[VECTORS : VECTORS + 2 * WY - 1, : HEADS * OFFSETS][::-1]
    grad_table = table_sum.reshape(2 * WY - 1, 2 * WZ - 1, 2 * WX - 1, HEADS).transpose(3, 1, 0, 2)
    return (
        mixed.transpose(0, 2, 1, 3),
        token_grad.transpose(0, 2, 1, 3),
        grad_qkv,
        grad_q_bias[0],
        grad_v_bias[0],
        grad_proj,
        grad_proj_bias[0],
        grad_up,
        grad_up_bias[0],
        grad_down,
        grad_down_bias[0],
        grad_mod,
        grad_mod_bias[0],
        grad_table,
    )


def solution(mesh):
    split = P(None, "lat", "lon", None)
    return jax.shard_map(
        on_device,
        mesh=mesh,
        in_specs=(split, split) + (P(),) * 14,
        out_specs=(split, split) + (P(),) * 12,
        check_vma=False,
    )
```

time: 550 us -> 245 us (0.45)
  local copies, waits for them, and re-layouts: 146 us -> 11.1 us
  waiting for transfers between devices: 130 us -> 6.77 us
  Pallas kernels: 135 us -> 211 us
  matrix products: 40 us -> 0 us
  blocking collectives: 39.6 us -> 0 us
  other arithmetic: 23.6 us -> 0 us
  between operations: 15.9 us -> 1.69 us
    psum x1 -> x0, waiting for transfers between devices: 91.4 us -> none  [on_device(): lax.psum((grad_qkv, grad_qkv_bias, grad_proj, grad_up, grad_up_bias, grad...]
    pallas_call x1 -> x7, Pallas kernels: 135 us -> 211 us  [the longest x3 145 us: block_call(): pl.pallas_call(functools.partial(block_kernel, straddles, first_pair, las...]
    reshape x7 -> x2, local copies, waits for them, and re-layouts: 54.7 us -> 1.29 us  [the longest x1 0.65 us: on_device(): table_sum.reshape(2 * WY - 1, 2 * WZ - 1, 2 * WX - 1, HEADS)]
    dot_general x7 -> x0, matrix products: 40 us -> none  [the longest x6 39.7 us: relative_bias(): jnp.einsum('habc,ika,jlb,mnc->nklhmij', table_bias, one_hot_offsets(WZ),...]
    psum x1 -> x0, blocking collectives: 39.6 us -> none  [on_device(): lax.psum((grad_qkv, grad_qkv_bias, grad_proj, grad_up, grad_up_bias, grad...]
    ppermute x8, waiting for transfers between devices: 38.2 us -> 6.77 us  [pass_along(): return lax.ppermute(block, ('lat', 'lon'), route)]
    transpose x5 -> x0, local copies, waits for them, and re-layouts: 30.4 us -> none  [the longest x2 10.9 us: to_windows(): return pieces.transpose(0, 2, 4, 1, 3, 5).reshape(-1, feat_width)]
    unnamed x67 -> x30, local copies, waits for them, and re-layouts: 26.3 us -> 2.21 us
  transfers between devices with their start and end apart: 9 -> 8, of which waited for: 3 -> 1; matrix products, arithmetic and copies ran while one was open for 27% -> 4% of each run, Pallas kernels for 0% -> 51%
where the time goes in v2:
time: 245 us; the launch traced here: 241 us
  Pallas kernels  211 us (86%)
  local copies, waits for them, and re-layouts  11.1 us (5%)
  starting transfers between devices  10.8 us (4%)
  waiting for transfers between devices  6.77 us (3%)
    pallas_call x3, Pallas kernels, block_call(): pl.pallas_call(functools.partial(block_kernel, straddles, first_pair, las...  145 us
    pallas_call x1, Pallas kernels, sum_over_devices(): pl.pallas_call(functools.partial(sum_kernel, tuple(bits), halvings, parts...  44 us
    pallas_call x1, Pallas kernels, merge(): pl.pallas_call(merge_kernel, grid=(level_count,), in_specs=[whole(first.s...  12.5 us
    ppermute x8, starting transfers between devices, pass_along(): return lax.ppermute(block, ('lat', 'lon'), route)  10.8 us
    ppermute x8, waiting for transfers between devices, pass_along(): return lax.ppermute(block, ('lat', 'lon'), route)  6.77 us
    pallas_call x1, Pallas kernels, cut_strips(): pl.pallas_call(strips_kernel, grid=(level_count,), in_specs=[field, field...  5.52 us
  transfers between devices with their start and end apart: 8, of which 1 were waited for; matrix products, arithmetic and copies ran while one was open for 4% of the time, Pallas kernels for 51%

profile of v2, /device:TPU:0, one launch (start us, length us, event | category | flops | bytes accessed | tf_op | source)
XLA Modules:
  0.0 241.3 jit_solution(4593100056514895314)
XLA Ops:
  0.7 5.5 %shard_map.263 = (bf16[2,4,544,256]{3,2,1,0:T(8,128)(2,1)}, bf16[2,4,72,256]{3,2,1,0:T(8,128)(2,1)}) custom-call(bf16[4,90,24,256]{3,2,1,0:T(8,128)(2,1)} %bitcast.14, bf16[4,90,24,256]{3,2,1,0:T(8,128)(2,1)} %bitcast.21), custom_call_target="tpu_custom_call" | custom-call | tf_op jit(solution)/shard_map/pallas_call | solution.py:87
  6.2 3.0 %collective-permute-start.1 = (bf16[2,4,544,256]{3,2,1,0:T(8,128)(2,1)}, bf16[2,4,544,256]{3,2,1,0:T(8,128)(2,1)}, u32[]{:S(2)}, u32[]{:S(2)}) collective-permute-start(bf16[2,4,544,256]{3,2,1,0:T(8,128)(2,1)} %get-tuple-element.53), channel_id=1, source_target_pairs={{0,4},{1,5},{2,6},{3,7},{4,8},{5,9},{6,10},{7,11},{8,12},{9,13},{1... | collective-permute-start | bytes 6684680 | tf_op jit(solution)/shard_map/ppermute | solution.py:732
  9.2 0.0 collective-permute-start
  9.2 2.7 %collective-permute-start.2 = (bf16[2,4,72,256]{3,2,1,0:T(8,128)(2,1)}, bf16[2,4,72,256]{3,2,1,0:T(8,128)(2,1)S(1)}, u32[]{:S(2)}, u32[]{:S(2)}) collective-permute-start(bf16[2,4,72,256]{3,2,1,0:T(8,128)(2,1)} %get-tuple-element.49), channel_id=1, source_target_pairs={{0,5},{1,6},{2,7},{3,4},{4,9},{5,10},{6,11},{7,8},{8,13},{9,14},{1... | collective-permute-start | bytes 884744 | tf_op jit(solution)/shard_map/ppermute | solution.py:732
  11.9 0.6 reshape.34.table_ref
  12.6 0.6 broadcast_in_dim.27.b_mod_ref
  13.2 0.0 copy-done.7
  13.2 0.6 broadcast_in_dim.32.b_up_ref
  13.8 0.6 broadcast_in_dim.28.b_proj_ref
  14.4 0.6 broadcast_in_dim.29.b_down_ref
  14.9 0.6 broadcast_in_dim.30.q_bias_ref
  15.5 0.6 broadcast_in_dim.31.v_bias_ref
  16.7 3.7 %shard_map.264 = (f32[144,576]{1,0:T(8,128)}, f32[16,256]{1,0:T(8,128)}, f32[256,128]{1,0:T(8,128)}) custom-call(s32[1]{0:T(128)S(6)} %copy.32.lead_ref, bf16[256,1024]{1,0:T(8,128)(2,1)} %w_mod_ref.1, bf16[1,1024]{1,0:T(2,128)(2,1)} %broadcast_in_dim.27.b_mod_ref, bf16[1,256]{1,0:T(2,128)(2,1)} %broadcast_in_dim.28.b_proj_ref, ...), custom_call_target="tpu_custom_call" | custom-call | tf_op jit(solution)/shard_map/pallas_call | solution.py:152
  20.4 0.0 collective-permute-done.refs_5_.refs_6_.refs_7_.refs_8_
  20.4 1.9 broadcast_in_dim.33.refs_15_
  22.3 0.8 broadcast_in_dim.35.refs_17_
  23.0 0.6 broadcast_in_dim.34.refs_16_
  23.7 0.0 copy-done.8
  23.7 37.1 %shard_map.265 = (bf16[2,1,2160,256]{3,2,1,0:T(8,128)(2,1)}, bf16[2,1,72,256]{3,2,1,0:T(8,128)(2,1)}, f32[3072,256]{1,0:T(8,128)}, f32[40,256]{1,0:T(8,128)}, f32[144,576]{1,0:T(8,128)}) custom-call(s32[8]{0:T(128)} %refs_0_.5, bf16[4,90,24,256]{3,2,1,0:T(8,128)(2,1)} %bitcast.15, bf16[4,90,24,256]{3,2,1,0:T(8,128)(2,1)} %bitcast.16, ...), custom_call_target="tpu_custom_call" | custom-call | flops 11232000000 | bytes 16777216 | tf_op jit(solution)/shard_map/pallas_call | solution.py:476
  60.7 6.8 %collective-permute-done.2.refs_13_.refs_14_.refs_15_.refs_16_ = bf16[2,4,72,256]{3,2,1,0:T(8,128)(2,1)S(1)} collective-permute-done((bf16[2,4,72,256]{3,2,1,0:T(8,128)(2,1)}, bf16[2,4,72,256]{3,2,1,0:T(8,128)(2,1)S(1)}, u32[]{:S(2)}, u32[]{:S(2)}) %collective-permute-start.2) | collective-permute-done | bytes 294944 | tf_op jit(solution)/shard_map/ppermute | solution.py:732
  67.5 0.0 collective-permute-done.1.refs_9_.refs_10_.refs_11_.refs_12_
  67.5 0.7 copy-done.9
  68.2 69.3 %shard_map.266 = (bf16[2,2,2160,256]{3,2,1,0:T(8,128)(2,1)}, bf16[2,2,72,256]{3,2,1,0:T(8,128)(2,1)}, f32[3072,256]{1,0:T(8,128)}, f32[40,256]{1,0:T(8,128)}, f3...) custom-call(s32[8]{0:T(128)} %refs_0_.5, bf16[4,90,24,256]{3,2,1,0:T(8,128)(2,1)} %bitcast.17, ...), custom_call_target="tpu_custom_call" | custom-call | flops 22464000000 | bytes 16777216 | tf_op jit(solution)/shard_map/pallas_call | solution.py:476
  137.5 0.1 collective-permute-start.3
  137.5 0.0 copy-done.10
  137.6 2.1 collective-permute-start.4
  139.6 0.0 collective-permute-start.6
  139.7 1.9 collective-permute-start.7
  141.6 38.9 %shard_map.267 = (bf16[2,1,2160,256]{3,2,1,0:T(8,128)(2,1)}, bf16[2,1,72,256]{3,2,1,0:T(8,128)(2,1)}, f32[3072,256]{1,0:T(8,128)}, f32[40,256]{1,0:T(8,128)}) custom-call(s32[8]{0:T(128)} %refs_0_.5, bf16[4,90,24,256]{3,2,1,0:T(8,128)(2,1)} %bitcast.19, bf16[4,90,24,256]{3,2,1,0:T(8,128)(2,1)} %bitcast.20, bf16[4,90,24,256]{3,2,1,0:T(8,128)(2,1)} %bitcast.26, ...), custom_call_target="tpu_custom_call" | custom-call | flops 11232000000 | bytes 16777216 | tf_op jit(solution)/shard_map/pallas_call | solution.py:476
  180.5 1.0 collective-permute-start.5
  181.5 44.0 %shard_map.268 = (bf16[3072,256]{1,0:T(8,128)(2,1)}, f32[40,256]{1,0:T(8,128)}) custom-call(f32[3072,256]{1,0:T(8,128)} %get-tuple-element.66.grad_ref, f32[40,256]{1,0:T(8,128)} %get-tuple-element.67.small_ref), custom_call_target="tpu_custom_call" | custom-call | tf_op jit(solution)/shard_map/pallas_call | solution.py:596
  225.5 0.7 slice.3
  226.3 0.1 rev.3
  226.3 0.1 copy.31
  226.4 0.7 reshape.35
  227.1 0.0 collective-permute-done.4.first_edge_ref
  227.1 0.0 collective-permute-done.5.second_edge_ref
  227.1 0.0 copy-start.4
  227.1 0.0 collective-permute-done.6.straddle_edge_ref
  227.1 0.0 collective-permute-done.7.corner_ref
  227.1 0.0 collective-permute-done.3.rows_ref
  227.1 0.0 copy-start
  227.2 0.6 copy-done.3
  227.7 0.0 copy-done.4
  227.7 0.1 copy-done.1
  227.8 0.1 copy-done.2
  227.9 0.8 copy-done
  228.6 12.5 %shard_map.269 = (bf16[4,90,24,256]{3,2,1,0:T(8,128)(2,1)}, bf16[4,90,24,256]{3,2,1,0:T(8,128)(2,1)}, f32[256,768]{1,0:T(8,128)}, f32[256,256]{1,0:T(8,128)}, f3...) custom-call(bf16[2,1,2160,256]{3,2,1,0:T(8,128)(2,1)} %get-tuple-ele, ...), custom_call_target="tpu_custom_call" | custom-call | tf_op jit(solution)/shard_map/pallas_call | solution.py:707
  (19 shorter events, 0.0 us)
Async XLA Ops:
  0.6 11.3 %copy-start.5 = (bf16[4,3,23,11]{2,0,3,1:T(4,128)(2,1)S(1)}, bf16[4,3,23,11]{2,0,3,1:T(4,128)(2,1)}, u32[]{:S(2)}) copy-start(bf16[4,3,23,11]{2,0,3,1:T(4,128)(2,1)} %param.29) | copy-start | bytes 18220
  0.7 11.9 %copy-start.6 = (bf16[1024]{0:T(1024)(128)(2,1)S(1)}, bf16[1024]{0:T(1024)(128)(2,1)}, u32[]{:S(2)}) copy-start(bf16[1024]{0:T(1024)(128)(2,1)} %param.28) | copy-start | bytes 6148
  0.7 12.5 %copy-start.7 = (bf16[1024]{0:T(1024)(128)(2,1)S(1)}, bf16[1024]{0:T(1024)(128)(2,1)}, u32[]{:S(2)}) copy-start(bf16[1024]{0:T(1024)(128)(2,1)} %param.24) | copy-start | bytes 6148
  0.7 13.1 %copy-start.11 = (bf16[256]{0:T(256)(128)(2,1)S(1)}, bf16[256]{0:T(256)(128)(2,1)}, u32[]{:S(2)}) copy-start(bf16[256]{0:T(256)(128)(2,1)} %param.22) | copy-start | bytes 1540
  0.7 13.7 %copy-start.12 = (bf16[256]{0:T(256)(128)(2,1)S(1)}, bf16[256]{0:T(256)(128)(2,1)}, u32[]{:S(2)}) copy-start(bf16[256]{0:T(256)(128)(2,1)} %param.26) | copy-start | bytes 1540
  0.7 14.2 %copy-start.13 = (bf16[256]{0:T(256)(128)(2,1)S(1)}, bf16[256]{0:T(256)(128)(2,1)}, u32[]{:S(2)}) copy-start(bf16[256]{0:T(256)(128)(2,1)} %param.19) | copy-start | bytes 1540
  0.7 14.8 %copy-start.14 = (bf16[256]{0:T(256)(128)(2,1)S(1)}, bf16[256]{0:T(256)(128)(2,1)}, u32[]{:S(2)}) copy-start(bf16[256]{0:T(256)(128)(2,1)} %param.20) | copy-start | bytes 1540
  6.2 61.3 %collective-permute-start.1 = (bf16[2,4,544,256]{3,2,1,0:T(8,128)(2,1)}, bf16[2,4,544,256]{3,2,1,0:T(8,128)(2,1)}, u32[]{:S(2)}, u32[]{:S(2)}) collective-permute-start(bf16[2,4,544,256]{3,2,1,0:T(8,128)(2,1)} %get-tuple-element.53), channel_id=1, source_target_pairs={{0,4},{1,5},{2,6},{3,7},{4,8},{5,9},{6,10},{7,11},{8,12},{9,13},{1... | collective-permute-start | bytes 6684680 | tf_op jit(solution)/shard_map/ppermute | solution.py:732
  9.2 11.2 %collective-permute-start = (bf16[2,4,72,256]{3,2,1,0:T(8,128)(2,1)}, bf16[2,4,72,256]{3,2,1,0:T(8,128)(2,1)S(1)}, u32[]{:S(2)}, u32[]{:S(2)}) collective-permute-start(bf16[2,4,72,256]{3,2,1,0:T(8,128)(2,1)} %get-tuple-element.49), channel_id=1, source_target_pairs={{0,1},{1,2},{2,3},{3,0},{4,5},{5,6},{6,7},{7,4},{8,9},{9,10},{10,1... | collective-permute-start | bytes 884744 | tf_op jit(solution)/shard_map/ppermute | solution.py:732
  9.2 58.3 %collective-permute-start.2 = (bf16[2,4,72,256]{3,2,1,0:T(8,128)(2,1)}, bf16[2,4,72,256]{3,2,1,0:T(8,128)(2,1)S(1)}, u32[]{:S(2)}, u32[]{:S(2)}) collective-permute-start(bf16[2,4,72,256]{3,2,1,0:T(8,128)(2,1)} %get-tuple-element.49), channel_id=1, source_target_pairs={{0,5},{1,6},{2,7},{3,4},{4,9},{5,10},{6,11},{7,8},{8,13},{9,14},{1... | collective-permute-start | bytes 884744 | tf_op jit(solution)/shard_map/ppermute | solution.py:732
  20.4 3.3 %copy-start.8 = (bf16[2,4,72,256]{3,2,1,0:T(8,128)(2,1)}, bf16[2,4,72,256]{3,2,1,0:T(8,128)(2,1)S(1)}, u32[]{:S(2)}) copy-start(bf16[2,4,72,256]{3,2,1,0:T(8,128)(2,1)S(1)} %collective-permute-done.refs_5_.refs_6_.refs_7_.refs_8_) | copy-start | bytes 884740
  67.5 0.7 copy-start.9
  68.2 69.3 %copy-start.10 = (bf16[2,1,72,256]{3,2,1,0:T(8,128)(2,1)S(1)}, bf16[2,1,72,256]{3,2,1,0:T(8,128)(2,1)}, u32[]{:S(2)}) copy-start(bf16[2,1,72,256]{3,2,1,0:T(8,128)(2,1)} %get-tuple-element.63) | copy-start | bytes 221188
  137.5 89.7 %collective-permute-start.3 = (bf16[2,4,544,256]{3,2,1,0:T(8,128)(2,1)}, bf16[2,4,544,256]{3,2,1,0:T(8,128)(2,1)S(1)}, u32[]{:S(2)}, u32[]{:S(2)}) collective-permute-start(bf16[2,4,544,256]{3,2,1,0:T(8,128)(2,1)} %get-tuple-element.62), channel_id=1, source_target_pairs={{0,28},{1,29},{2,30},{3,31},{4,0},{5,1},{6,2},{7,3},{8,4},{9,5},{1... | collective-permute-start | bytes 6684680 | tf_op jit(solution)/shard_map/ppermute | solution.py:732
  137.6 89.5 %collective-permute-start.4 = (bf16[2,1,72,256]{3,2,1,0:T(8,128)(2,1)S(1)}, bf16[2,1,72,256]{3,2,1,0:T(8,128)(2,1)S(1)}, u32[]{:S(2)}, u32[]{:S(2)}) collective-permute-start(bf16[2,1,72,256]{3,2,1,0:T(8,128)(2,1)S(1)} %copy-done.10), channel_id=1, source_target_pairs={{0,3},{1,0},{2,1},{3,2},{4,7},{5,4},{6,5},{7,6},{8,11},{9,8},{10,9... | collective-permute-start | bytes 221192 | tf_op jit(solution)/shard_map/ppermute | solution.py:732
  139.6 87.5 %collective-permute-start.6 = (bf16[2,2,72,256]{3,2,1,0:T(8,128)(2,1)}, bf16[2,2,72,256]{3,2,1,0:T(8,128)(2,1)S(1)}, u32[]{:S(2)}, u32[]{:S(2)}) collective-permute-start(bf16[2,2,72,256]{3,2,1,0:T(8,128)(2,1)} %get-tuple-element.65), channel_id=1, source_target_pairs={{0,3},{1,0},{2,1},{3,2},{4,7},{5,4},{6,5},{7,6},{8,11},{9,8},{10,9... | collective-permute-start | bytes 442376 | tf_op jit(solution)/shard_map/ppermute | solution.py:732
  139.7 87.4 %collective-permute-start.7 = (bf16[2,2,72,256]{3,2,1,0:T(8,128)(2,1)}, bf16[2,2,72,256]{3,2,1,0:T(8,128)(2,1)S(1)}, u32[]{:S(2)}, u32[]{:S(2)}) collective-permute-start(bf16[2,2,72,256]{3,2,1,0:T(8,128)(2,1)} %get-tuple-element.65), channel_id=1, source_target_pairs={{0,31},{1,28},{2,29},{3,30},{4,3},{5,0},{6,1},{7,2},{8,7},{9,4},{1... | collective-permute-start | bytes 442376 | tf_op jit(solution)/shard_map/ppermute | solution.py:732
  180.5 46.6 %collective-permute-start.5 = (bf16[2,1,72,256]{3,2,1,0:T(8,128)(2,1)}, bf16[2,1,72,256]{3,2,1,0:T(8,128)(2,1)S(1)}, u32[]{:S(2)}, u32[]{:S(2)}) collective-permute-start(bf16[2,1,72,256]{3,2,1,0:T(8,128)(2,1)} %get-tuple-element.64), channel_id=1, source_target_pairs={{0,3},{1,0},{2,1},{3,2},{4,7},{5,4},{6,5},{7,6},{8,11},{9,8},{10,9... | collective-permute-start | bytes 221192 | tf_op jit(solution)/shard_map/ppermute | solution.py:732
  227.1 0.6 copy-start.3
  227.1 0.6 copy-start.4
  227.1 0.7 copy-start.1
  227.1 0.7 copy-start.2
  227.1 1.5 copy-start

commit v3 on v2

--- a/solution.py
+++ b/solution.py
@@ -59,39 +59,8 @@
     return jax.ShapeDtypeStruct(shape, dtype)
 
 
-def strips_kernel(tokens_ref, cotangent_ref, rows_ref, cols_ref):
-    _, col_count, row_count, width = tokens_ref.shape
-    for a, ref in enumerate((tokens_ref, cotangent_ref)):
-        cols_ref[a, 0] = ref[0, col_count - HALF_X :].reshape(HALF_X * row_count, width)
-        for start in range(0, col_count, PACKED_COLS):
-            count = min(PACKED_COLS, col_count - start)
-            block = ref[0, start : start + count].astype(F32)
-            packed = jnp.concatenate(
-                [block[c, row_count - HALF_Y :] for c in range(count)], axis=0
-            )
-            rows_ref[a, 0, start * HALF_Y : (start + count) * HALF_Y, :] = packed.astype(BF16)
-
-
 def packed_rows(col_count):
     return -(-col_count * HALF_Y // 16) * 16
-
-
-def cut_strips(tokens, cotangent):
-    level_count, col_count, row_count, width = tokens.shape
-    field = pl.BlockSpec((1, col_count, row_count, width), lambda i: (i, 0, 0, 0))
-
-    def strip(count):
-        return pl.BlockSpec((2, 1, count, width), lambda i: (0, i, 0, 0))
-
-    counts = (packed_rows(col_count), HALF_X * row_count)
-    return pl.pallas_call(
-        strips_kernel,
-        grid=(level_count,),
-        in_specs=[field, field],
-        out_specs=[strip(count) for count in counts],
-        out_shape=[shape_of((2, level_count, count, width), BF16) for count in counts],
-        compiler_params=pltpu.CompilerParams(vmem_limit_bytes=VMEM_LIMIT),
-    )(tokens, cotangent)
 
 
 def offset_pick(key_x, key_z):
@@ -221,11 +190,11 @@
     return picked
 
 
-def store_windows(field, z_pieces, out_ref):
+def store_windows(field, western, out_ref):
     width = out_ref.shape[1]
     for c in range(HALF_X):
         out_ref[c * CELLS : (c + 1) * CELLS, :] = jnp.concatenate(
-            [z_pieces(c, z) for z in range(WZ)], axis=0
+            [western(c, z) for z in range(WZ)], axis=0
         )
     own_cols = out_ref.shape[0] // CELLS - HALF_X
     for start in range(0, own_cols, PACKED_COLS):
@@ -239,85 +208,121 @@
     return jnp.stack([rows[c * HALF_Y : (c + 1) * HALF_Y] for c in range(count)], axis=0)
 
 
-def mask_scores(bias, level_wraps, straddles, first_band, crop_own, crop_before, row_count):
+def mask_scores(bias, level_wraps, base, first_band, crop_own, crop_before, row_count):
     def parts(cell):
-        z, y = (cell % CELLS) // WY, cell % WY
+        z, row = (cell % CELLS) // WY, base + cell % WY
         part = 2 * jnp.where(z == WZ - 1, level_wraps, 0)
-        if straddles:
-            part = part + jnp.where(y >= HALF_Y, first_band, 0)
-            own = y - HALF_Y >= row_count - crop_own
-            before = row_count - HALF_Y + y >= row_count - crop_before
-            valid = jnp.where(y >= HALF_Y, own.astype(jnp.int32), before.astype(jnp.int32))
-        else:
-            valid = (HALF_Y + y >= row_count - crop_own).astype(jnp.int32)
-        return part, valid
+        part = part + jnp.where((row >= 0) & (row < HALF_Y), first_band, 0)
+        crop = jnp.where(row >= 0, crop_own, crop_before)
+        return part, jnp.where(row >= 0, row, row + row_count) >= row_count - crop
 
     key = iota(bias.shape, 0)
     query = iota(bias.shape, 1) % WINDOW
     key_part, key_valid = parts(key)
     query_part, _ = parts(query)
-    allowed = (key_part == query_part) & ((key_valid > 0) | (key == query))
+    allowed = (key_part == query_part) & (key_valid | (key == query))
     return jnp.where(allowed, bias, bias + MASKED_SCORE)
 
 
-def block_kernel(straddles, first_pair, last, *refs):
-    refs = list(refs)
-
-    def take(count):
-        taken, refs[:count] = refs[:count], []
-        return taken
-
-    (crop_ref,) = take(1)
-    field_refs = [take(WZ), take(WZ)]
-    col_refs = [take(WZ), take(WZ)]
-    row_refs, corner_refs = ([take(WZ), take(WZ)], [take(WZ), take(WZ)]) if straddles else (None, None)
-    bias_ref, vec_ref, w_qkv_ref, w_proj_ref, w_up_ref, w_down_ref = take(6)
-    grad_in_ref, small_in_ref, scores_in_ref = take(3)
-    out_ref, edge_ref, grad_ref, small_ref = take(4)
-    (score_sum_ref,) = take(0 if last else 1) or (None,)
-    (back_ref,) = take(1 if straddles else 0) or (None,)
-    score_bias_ref, xw_ref, gw_ref, qkv_ref, prob_ref, att_ref, dqkv_ref = take(7)
-    if last:
-        (score_sum_ref,) = take(1)
-
-    step = pl.program_id(0)
+GROUPS = 4
+
+
+def group_pair(group):
+    return group // 2
+
+
+def field_level(pair, z):
+    return lax.rem(WZ * pair + z + WZ // 2, 2 * WZ)
+
+
+def block_kernel(
+    crop_ref, tokens_ref, cotangent_ref, bias_ref, vec_ref, w_qkv_ref, w_proj_ref, w_up_ref, w_down_ref,
+    win_ref, rows_back_ref, edge_back_ref, corner_back_ref, grad_ref, small_ref,
+    fields_ref, rows_out_ref, rows_in_ref, cols_in_ref, corner_in_ref, out_ref,
+    score_bias_ref, xw_ref, gw_ref, qkv_ref, prob_ref, att_ref, dqkv_ref, score_sum_ref,
+    field_sems, halo_sems, rows_sems, back_sems, edge_sems, corner_sems, out_sems,
+):
     width = vec_ref.shape[1]
     hidden_width = w_up_ref.shape[1]
-    _, col_count, row_count, _ = field_refs[0][0].shape
+    _, level_count, col_count, row_count, _ = fields_ref.shape
     band_count = crop_ref.shape[0]
     score_scale = (width // HEADS) ** -0.5
-
-    @pl.when(step == 0)
-    def _():
-        grad_ref[...] = grad_in_ref[...]
-        small_ref[...] = small_in_ref[...]
-        score_sum_ref[...] = scores_in_ref[...]
-
-    band = lax.axis_index("lat")
-    score_bias_ref[...] = mask_scores(
-        bias_ref[...], (step + first_pair == 1).astype(jnp.int32), straddles,
-        (band == 0).astype(jnp.int32), crop_ref[band],
-        crop_ref[lax.rem(band + band_count - 1, band_count)], row_count,
-    )
-
-    for a, target in enumerate((xw_ref, gw_ref)):
-        def field(start, count, z, a=a):
-            rows = field_refs[a][z][0, start : start + count].astype(F32)
-            if not straddles:
-                return rows[:, HALF_Y : HALF_Y + WY]
-            strip = row_refs[a][z][0, 0, start * HALF_Y : (start + count) * HALF_Y, :].astype(F32)
-            return jnp.concatenate([unpack_strip(strip, count), rows[:, :HALF_Y]], axis=1)
-
-        def western(c, z, a=a):
-            own = slice(c * row_count, (c + 1) * row_count)
-            rows = col_refs[a][z][0, 0, own, :].astype(F32)
-            if not straddles:
-                return rows[HALF_Y : HALF_Y + WY]
-            before = corner_refs[a][z][0, 0, own, :].astype(F32)
-            return jnp.concatenate([before[row_count - HALF_Y :], rows[:HALF_Y]], axis=0)
-
-        store_windows(field, western, target)
-
+    lat, lon = lax.axis_index("lat"), lax.axis_index("lon")
+    lat_size, lon_size = lax.axis_size("lat"), lax.axis_size("lon")
+
+    def device(lat_step, lon_step):
+        return (
+            lax.rem(lat + lat_step + lat_size, lat_size), lax.rem(lon + lon_step + lon_size, lon_size)
+        )
+
+    steps = ((1, 0), (0, 1), (1, 1))
+    barrier = pltpu.get_barrier_semaphore()
+    for lat_step, lon_step in steps:
+        for sign in (1, -1):
+            pl.semaphore_signal(
+                barrier, inc=1, device_id=device(sign * lat_step, sign * lon_step), device_id_type=MESH
+            )
+
+    loads = []
+    for level in (1, 2, 3, 0):
+        for a, ref in enumerate((tokens_ref, cotangent_ref)):
+            loads.append(pltpu.make_async_copy(
+                ref.at[level], fields_ref.at[a, level], field_sems.at[len(loads)]
+            ))
+            loads[-1].start()
+
+    def remote(source, target, sems, lat_step, lon_step):
+        return pltpu.make_async_remote_copy(
+            src_ref=source, dst_ref=target, send_sem=sems.at[0], recv_sem=sems.at[1],
+            device_id=device(lat_step, lon_step), device_id_type=MESH,
+        )
+
+    last_cols = fields_ref.at[:, :, pl.ds(col_count - HALF_X, HALF_X)]
+    cols_copy = remote(last_cols, cols_in_ref, halo_sems.at[0], 0, 1)
+    corner_copy = remote(last_cols, corner_in_ref, halo_sems.at[1], 1, 1)
+
+    def rows_copy(pair):
+        return remote(rows_out_ref.at[pair], rows_in_ref.at[pair], rows_sems.at[pair], 1, 0)
+
+    def back_copy(pair):
+        return remote(rows_out_ref.at[pair], rows_back_ref.at[pair], back_sems.at[pair], -1, 0)
+
+    def edge_rows(group):
+        return out_ref.at[lax.rem(group, 2), :, pl.ds(0, edge_back_ref.shape[2])]
+
+    def edge_copy(group):
+        return remote(edge_rows(group), edge_back_ref.at[group], edge_sems.at[group], 0, -1)
+
+    def corner_back_copy(group):
+        pair = group_pair(group)
+        return remote(edge_rows(group), corner_back_ref.at[pair], corner_sems.at[pair], -1, -1)
+
+    def out_copy(group):
+        return pltpu.make_async_copy(
+            out_ref.at[lax.rem(group, 2)], win_ref.at[:, group], out_sems.at[group]
+        )
+
+    for pair in range(2):
+        for z in range(WZ):
+            level = (WZ * pair + z + WZ // 2) % level_count
+            for a in range(2):
+                loads[(pair * WZ + z) * 2 + a].wait()
+                for start in range(0, col_count, PACKED_COLS):
+                    count = min(PACKED_COLS, col_count - start)
+                    block = fields_ref[a, level, start : start + count].astype(F32)
+                    packed = [block[c, row_count - HALF_Y :] for c in range(count)]
+                    rows_out_ref[
+                        pair, a, z, start * HALF_Y : (start + count) * HALF_Y, :
+                    ] = jnp.concatenate(packed, axis=0).astype(BF16)
+        if pair == 0:
+            pl.semaphore_wait(barrier, 2 * len(steps))
+        rows_copy(pair).start()
+    cols_copy.start()
+    corner_copy.start()
+
+    grad_ref[...] = jnp.zeros_like(grad_ref)
+    small_ref[...] = jnp.zeros_like(small_ref)
+    score_sum_ref[...] = jnp.zeros_like(score_sum_ref)
     rows = BLOCK_WINDOWS * WINDOW
     shift_one, scale_one, shift_two, scale_two, b_proj, b_down = [
         vec_ref[i : i + 1, :] for i in range(6)
@@ -331,7 +336,10 @@
                 :, j * width : (j + 1) * width
             ]
 
-    def block(index, carry):
+    def column_sums(values):
+        return jnp.sum(values, axis=0, keepdims=True)
+
+    def block(index, slot):
         here = pl.ds(pl.multiple_of(index * rows, 16), rows)
         x32 = xw_ref[here, :]
         x = x32.astype(BF16)
@@ -358,18 +366,19 @@
         hidden = hidden.astype(BF16)
         second = dot_nn(hidden, w_down_ref[...]) + b_down
         norm_two, inverse_two = norm(second)
-        out_ref[0, 0, here, :] = (middle + norm_two * (1.0 + scale_two) + shift_two).astype(BF16)
+        out_ref[slot, 0, here, :] = (middle + norm_two * (1.0 + scale_two) + shift_two).astype(BF16)
 
         g = gw_ref[here, :]
         second_low = norm_back(g * (1.0 + scale_two), norm_two, inverse_two).astype(BF16)
+        pre_grad = dot_nt(second_low, w_down_ref[...]) * slope
         add_grad(8, dot_tn(second_low, hidden))
-        pre_grad = dot_nt(second_low, w_down_ref[...]) * slope
         pre_low = pre_grad.astype(BF16)
+        up_sums = column_sums(pre_grad)
+        middle_grad = g + dot_nt(pre_low, w_up_ref[...])
         add_grad(4, dot_tn(middle_low, pre_low))
-        middle_grad = g + dot_nt(pre_low, w_up_ref[...])
         branch_low = norm_back(middle_grad * (1.0 + scale_one), norm_one, inverse_one).astype(BF16)
+        att_ref[...] = dot_nt(branch_low, w_proj_ref[...]).astype(BF16)
         add_grad(3, dot_tn(att, branch_low))
-        att_ref[...] = dot_nt(branch_low, w_proj_ref[...]).astype(BF16)
 
         for w in range(BLOCK_WINDOWS):
             cells = pl.ds(w * WINDOW, WINDOW)
@@ -387,14 +396,9 @@
             dqkv_ref[cells, 2 * width :] = dot_nn(prob.astype(BF16), out_grad).astype(BF16)
 
         dqkv = dqkv_ref[...]
+        out_ref[slot, 1, here, :] = (middle_grad + dot_nt(dqkv, w_qkv_ref[...])).astype(BF16)
         add_grad(0, dot_tn(x, dqkv))
-        out_ref[1, 0, here, :] = (middle_grad + dot_nt(dqkv, w_qkv_ref[...])).astype(BF16)
-
-        def column_sums(values):
-            return jnp.sum(values, axis=0, keepdims=True)
-
         qkv_sums = column_sums(dqkv.astype(F32))
-        up_sums = column_sums(pre_grad)
         sums = [
             column_sums(middle_grad), column_sums(middle_grad * norm_one), column_sums(g),
             column_sums(g * norm_two), column_sums(branch_low.astype(F32)),
@@ -404,87 +408,151 @@
         sums += [up_sums[:, j * width : (j + 1) * width] for j in range(hidden_width // width)]
         sums += [jnp.zeros((VECTORS - len(sums), width), F32)]
         small_ref[:VECTORS, :] += jnp.concatenate(sums, axis=0)
-        return carry
-
-    lax.fori_loop(0, col_count // WX // BLOCK_WINDOWS, block, 0)
-    for a in range(2):
-        edge_ref[a, 0] = out_ref[a, 0, :EDGE, :]
-        if straddles:
+        return slot
+
+    def gather(pair, straddles):
+        for a, target in enumerate((xw_ref, gw_ref)):
+            def field(start, count, z, a=a):
+                own = fields_ref[a, field_level(pair, z), start : start + count].astype(F32)
+                if not straddles:
+                    return own[:, HALF_Y : HALF_Y + WY]
+                strip = rows_in_ref[pair, a, z, start * HALF_Y : (start + count) * HALF_Y, :]
+                return jnp.concatenate(
+                    [unpack_strip(strip.astype(F32), count), own[:, :HALF_Y]], axis=1
+                )
+
+            def western(c, z, a=a):
+                own = cols_in_ref[a, field_level(pair, z), c].astype(F32)
+                if not straddles:
+                    return own[HALF_Y : HALF_Y + WY]
+                before = corner_in_ref[a, field_level(pair, z), c].astype(F32)
+                return jnp.concatenate([before[row_count - HALF_Y :], own[:HALF_Y]], axis=0)
+
+            store_windows(field, western, target)
+
+    def send_back(pair, slot):
+        for a in range(2):
             for start in range(0, col_count - HALF_X, PACKED_COLS):
                 count = min(PACKED_COLS, col_count - HALF_X - start)
                 first = (start + HALF_X) * CELLS
-                cells = out_ref[a, 0, first : first + count * CELLS, :].astype(F32)
+                cells = out_ref[slot, a, first : first + count * CELLS, :].astype(F32)
                 for z in range(WZ):
                     pieces = [
                         cells[c * CELLS + z * WY : c * CELLS + z * WY + HALF_Y] for c in range(count)
                     ]
-                    back_ref[a, z, start * HALF_Y : (start + count) * HALF_Y, :] = jnp.concatenate(
-                        pieces, axis=0
-                    ).astype(BF16)
-    if last:
-        @pl.when(step == pl.num_programs(0) - 1)
+                    rows_out_ref[
+                        pair, a, z, start * HALF_Y : (start + count) * HALF_Y, :
+                    ] = jnp.concatenate(pieces, axis=0).astype(BF16)
+        back_copy(pair).start()
+
+    def group_step(group, carry):
+        pair, slot = group_pair(group), lax.rem(group, 2)
+        inner = (group == 0) | (group == GROUPS - 1)
+
+        @pl.when(group == 0)
         def _():
-            small_ref[VECTORS:, : HEADS * OFFSETS] = table_grad(score_sum_ref)
-
-
-def block_call(straddles, first_pair, pair_count, last, crop_rows, fields, halos, constants, sums):
-    level_count, col_count, row_count, width = fields[0].shape
-
-    def level_of(i, z):
-        return (WZ * (i + first_pair) + z + WZ // 2) % level_count
-
-    specs, values = [pl.BlockSpec(memory_space=pltpu.SMEM)], [crop_rows]
-    for field in fields:
-        for z in range(WZ):
-            specs.append(pl.BlockSpec(
-                (1, col_count, row_count, width), lambda i, z=z: (level_of(i, z), 0, 0, 0)
-            ))
-            values.append(field)
-    for halo in halos:
-        for a in range(2):
-            for z in range(WZ):
-                specs.append(pl.BlockSpec(
-                    (1, 1) + halo.shape[2:], lambda i, a=a, z=z: (a, level_of(i, z), 0, 0)
-                ))
-                values.append(halo)
-    specs += [whole(v.shape) for v in constants + sums]
-    values += constants + sums
-
+            cols_copy.wait_recv()
+
+        @pl.when(group == 1)
+        def _():
+            corner_copy.wait_recv()
+
+        @pl.when(group >= 2)
+        def _():
+            out_copy(group - 2).wait()
+            edge_copy(group - 2).wait_send()
+
+        @pl.when(group == GROUPS - 1)
+        def _():
+            corner_back_copy(1).wait_send()
+
+        @pl.when(inner)
+        def _():
+            gather(pair, False)
+
+        @pl.when(jnp.logical_not(inner))
+        def _():
+            rows_copy(pair).wait_recv()
+            gather(pair, True)
+
+        score_bias_ref[...] = mask_scores(
+            bias_ref[...], pair, jnp.where(inner, HALF_Y, -HALF_Y), (lat == 0).astype(jnp.int32),
+            crop_ref[lat], crop_ref[lax.rem(lat + band_count - 1, band_count)], row_count,
+        )
+        lax.fori_loop(0, col_count // WX // BLOCK_WINDOWS, block, slot)
+        out_copy(group).start()
+        edge_copy(group).start()
+
+        @pl.when(jnp.logical_not(inner))
+        def _():
+            corner_back_copy(group).start()
+            rows_copy(pair).wait_send()
+            send_back(pair, slot)
+
+        return carry
+
+    lax.fori_loop(0, GROUPS, group_step, 0)
+    small_ref[VECTORS:, : HEADS * OFFSETS] = table_grad(score_sum_ref)
+    for group in (2, 3):
+        out_copy(group).wait()
+        edge_copy(group).wait_send()
+    corner_back_copy(2).wait_send()
+    cols_copy.wait_send()
+    corner_copy.wait_send()
+    for pair in range(2):
+        back_copy(pair).wait()
+        corner_back_copy(pair + 1).wait_recv()
+    for group in range(GROUPS):
+        edge_copy(group).wait_recv()
+
+
+def block_call(crop_rows, tokens, cotangent, constants):
+    level_count, col_count, row_count, width = tokens.shape
+    vmem = pl.BlockSpec(memory_space=pltpu.VMEM)
     cells = col_count * CELLS
-    kept = sums[:2] if last else sums
-    out_specs = [
-        pl.BlockSpec((2, 1, count, width), lambda i: (0, i, 0, 0)) for count in (cells, EDGE)
-    ] + [whole(v.shape) for v in kept]
-    out_shape = [shape_of((2, pair_count, count, width), BF16) for count in (cells, EDGE)]
-    out_shape += [shape_of(v.shape, F32) for v in kept]
-    if straddles:
-        packed = packed_rows(col_count)
-        out_specs.append(pl.BlockSpec((2, WZ, packed, width), lambda i: (0, i, 0, 0)))
-        out_shape.append(shape_of((2, pair_count * WZ, packed, width), BF16))
     rows = BLOCK_WINDOWS * WINDOW
-    scratch = [
-        pltpu.VMEM((WINDOW, SCORES), F32),
-        pltpu.VMEM((cells, width), F32),
-        pltpu.VMEM((cells, width), F32),
-        pltpu.VMEM((rows, 3 * width), BF16),
-        pltpu.VMEM((BLOCK_WINDOWS, WINDOW, SCORES), F32),
-        pltpu.VMEM((rows, width), BF16),
-        pltpu.VMEM((rows, 3 * width), BF16),
-    ]
-    if last:
-        scratch.append(pltpu.VMEM((WINDOW, SCORES), F32))
+    edge = -(-EDGE // 16) * 16
+    pairs = level_count // WZ
+    strips = (pairs, 2, WZ, packed_rows(col_count), width)
+    grad_rows = 4 * width + 2 * constants[4].shape[1]
+    sends = pltpu.SemaphoreType.DMA
     return pl.pallas_call(
-        functools.partial(block_kernel, straddles, first_pair, last),
-        grid=(pair_count,),
-        in_specs=specs,
-        out_specs=out_specs,
-        out_shape=out_shape,
-        scratch_shapes=scratch,
+        block_kernel,
+        in_specs=[pl.BlockSpec(memory_space=pltpu.SMEM), ANY, ANY] + [vmem] * len(constants),
+        out_specs=[ANY] * 4 + [vmem] * 2,
+        out_shape=[
+            shape_of((2, GROUPS, cells, width), BF16),
+            shape_of(strips, BF16),
+            shape_of((GROUPS, 2, edge, width), BF16),
+            shape_of((pairs, 2, edge, width), BF16),
+            shape_of((grad_rows, width), F32),
+            shape_of((VECTORS + TABLE_ROWS, width), F32),
+        ],
+        scratch_shapes=[
+            pltpu.VMEM((2,) + tokens.shape, BF16),
+            pltpu.VMEM(strips, BF16),
+            pltpu.VMEM(strips, BF16),
+            pltpu.VMEM((2, level_count, HALF_X, row_count, width), BF16),
+            pltpu.VMEM((2, level_count, HALF_X, row_count, width), BF16),
+            pltpu.VMEM((2, 2, cells, width), BF16),
+            pltpu.VMEM((WINDOW, SCORES), F32),
+            pltpu.VMEM((cells, width), F32),
+            pltpu.VMEM((cells, width), F32),
+            pltpu.VMEM((rows, 3 * width), BF16),
+            pltpu.VMEM((BLOCK_WINDOWS, WINDOW, SCORES), F32),
+            pltpu.VMEM((rows, width), BF16),
+            pltpu.VMEM((rows, 3 * width), BF16),
+            pltpu.VMEM((WINDOW, SCORES), F32),
+            sends((2 * level_count,)), sends((2, 2)), sends((pairs, 2)), sends((pairs, 2)),
+            sends((GROUPS, 2)), sends((pairs, 2)), sends((GROUPS,)),
+        ],
         cost_estimate=pl.CostEstimate(
-            flops=pair_count * cells * 5_200_000, bytes_accessed=16 * 2**20, transcendentals=0
+            flops=GROUPS * cells * 5_200_000, bytes_accessed=32 * 2**20, transcendentals=0
         ),
-        compiler_params=pltpu.CompilerParams(vmem_limit_bytes=VMEM_LIMIT),
-    )(*values)
+        compiler_params=pltpu.CompilerParams(
+            collective_id=1, has_side_effects=True, vmem_limit_bytes=VMEM_LIMIT
+        ),
+    )(crop_rows, tokens, cotangent, *constants)
 
 
 def halved(rows, count):
@@ -614,38 +682,39 @@
 
 
 def merge_kernel(
-    first_ref, second_ref, straddle_ref, rows_ref, first_edge_ref, second_edge_ref,
-    straddle_edge_ref, corner_ref, grad_ref, small_ref, context_ref, *out_refs,
+    inner_ref, straddle_ref, rows_ref, inner_edge_ref, straddle_edge_ref, corner_ref,
+    grad_ref, small_ref, context_ref, *out_refs,
 ):
     fields, grads = out_refs[:2], out_refs[2:]
     _, col_count, row_count, width = fields[0].shape
     step = pl.program_id(0)
 
-    def piece(ref, a, first_col, count, first, size):
-        block = ref[a, 0, first_col * CELLS : (first_col + count) * CELLS, :].astype(F32)
+    def piece(rows_of, a, first_col, count, first, size):
+        block = rows_of(a)[first_col * CELLS : (first_col + count) * CELLS, :].astype(F32)
         return block.reshape(count, CELLS, width)[:, first : first + size]
 
-    for pair, z in ((0, 0), (0, 1), (1, 0), (1, 1)):
-        inner_ref = (first_ref, second_ref)[pair]
-        inner_edge_ref = (first_edge_ref, second_edge_ref)[pair]
-
-        @pl.when(step == pair * WZ + z)
+    straddle, inner = lambda a: straddle_ref.at[a, 0], lambda a: inner_ref.at[a, 0]
+    straddle_edge, inner_edge, corner = (
+        lambda a, ref=ref: ref.at[0, a] for ref in (straddle_edge_ref, inner_edge_ref, corner_ref)
+    )
+    for z in range(WZ):
+        @pl.when(lax.rem(step, WZ) == z)
         def _():
             first = z * WY
             for a, field in enumerate(fields):
                 for start in range(0, col_count - HALF_X, PACKED_COLS):
                     count = min(PACKED_COLS, col_count - HALF_X - start)
-                    strip = rows_ref[a, 0, start * HALF_Y : (start + count) * HALF_Y, :]
+                    strip = rows_ref[0, a, 0, start * HALF_Y : (start + count) * HALF_Y, :]
                     block = jnp.concatenate([
-                        piece(straddle_ref, a, start + HALF_X, count, first + HALF_Y, HALF_Y),
-                        piece(inner_ref, a, start + HALF_X, count, first, WY),
+                        piece(straddle, a, start + HALF_X, count, first + HALF_Y, HALF_Y),
+                        piece(inner, a, start + HALF_X, count, first, WY),
                         unpack_strip(strip.astype(F32), count),
                     ], axis=1)
                     field[0, start : start + count] = block.astype(BF16)
                 block = jnp.concatenate([
-                    piece(straddle_edge_ref, a, 0, HALF_X, first + HALF_Y, HALF_Y),
-                    piece(inner_edge_ref, a, 0, HALF_X, first, WY),
-                    piece(corner_ref, a, 0, HALF_X, first, HALF_Y),
+                    piece(straddle_edge, a, 0, HALF_X, first + HALF_Y, HALF_Y),
+                    piece(inner_edge, a, 0, HALF_X, first, WY),
+                    piece(corner, a, 0, HALF_X, first, HALF_Y),
                 ], axis=1)
                 field[0, col_count - HALF_X :] = block.astype(BF16)
 
@@ -686,17 +755,24 @@
             ref[...] = small_ref[i : i + 1, :]
 
 
-def merge(
-    field_shape, hidden_width, first, second, straddle, rows, first_edge, second_edge,
-    straddle_edge, corner, grad, small, context,
-):
+def merge(field_shape, hidden_width, windows, rows_back, edge_back, corner_back, grad, small, context):
     level_count, col_count, row_count, width = field_shape
 
     def level_of(i):
         return (i + WZ // 2) % level_count
 
-    def by_pair(value):
-        return pl.BlockSpec((2, 1) + value.shape[2:], lambda i: (0, i // WZ, 0, 0))
+    def group_of(pair, straddles):
+        return 1 + pair if straddles else (GROUPS - 1) * pair
+
+    def windows_of(straddles):
+        return pl.BlockSpec(
+            (2, 1) + windows.shape[2:], lambda i: (0, group_of(i // WZ, straddles), 0, 0)
+        )
+
+    def edge_of(straddles):
+        return pl.BlockSpec(
+            (1,) + edge_back.shape[1:], lambda i: (group_of(i // WZ, straddles), 0, 0, 0)
+        )
 
     shapes = [
         (width, 3 * width), (width, width), (width, hidden_width), (hidden_width, width),
@@ -708,72 +784,36 @@
         merge_kernel,
         grid=(level_count,),
         in_specs=[
-            whole(first.shape), whole(second.shape), by_pair(straddle),
-            pl.BlockSpec((2, 1) + rows.shape[2:], lambda i: (0, i, 0, 0)),
-            whole(first_edge.shape), whole(second_edge.shape), by_pair(straddle_edge),
-            by_pair(corner),
+            windows_of(False), windows_of(True),
+            pl.BlockSpec((1, 2, 1) + rows_back.shape[3:], lambda i: (i // WZ, 0, i % WZ, 0, 0)),
+            edge_of(False), edge_of(True),
+            pl.BlockSpec((1,) + corner_back.shape[1:], lambda i: (i // WZ, 0, 0, 0)),
         ] + [whole(v.shape) for v in (grad, small, context)],
         out_specs=[field, field] + [whole(s) for s in shapes],
         out_shape=[shape_of(field_shape, BF16)] * 2 + [shape_of(s, F32) for s in shapes],
         compiler_params=pltpu.CompilerParams(vmem_limit_bytes=VMEM_LIMIT),
-    )(
-        first, second, straddle, rows, first_edge, second_edge, straddle_edge, corner, grad, small,
-        context,
-    )
-
-
-def pass_along(block, lat_step, lon_step):
-    lat, lon = lax.axis_size("lat"), lax.axis_size("lon")
-    route = []
-    for i in range(lat):
-        for j in range(lon):
-            target = ((i + lat_step) % lat) * lon + (j + lon_step) % lon
-            route.append((i * lon + j, target))
-    return lax.ppermute(block, ("lat", "lon"), route)
+    )(windows, windows, rows_back, edge_back, edge_back, corner_back, grad, small, context)
 
 
 def on_device(
     tokens, cotangent, w_qkv, q_bias, v_bias, w_proj, b_proj, w_up, b_up, w_down, b_down,
     w_mod, b_mod, rel_table, crop_rows, lead_hours,
 ):
-    width = tokens.shape[-1]
     fields = [field.transpose(0, 2, 1, 3) for field in (tokens, cotangent)]
-    rows, own_cols = cut_strips(*fields)
-    cols = pass_along(own_cols, 0, 1)
-    rows = pass_along(rows, 1, 0)
-    corner = pass_along(own_cols, 1, 1)
-
     table = rel_table.transpose(1, 3, 0, 2).reshape(HEADS * OFFSETS, 2 * WY - 1)
     bias, vecs, context = set_up(
         lead_hours, w_mod, b_mod, b_proj, b_down, q_bias, v_bias, b_up, table
     )
     constants = [bias, vecs, w_qkv, w_proj, w_up, w_down]
-    sums = [
-        jnp.zeros((4 * width + 2 * w_up.shape[1], width), F32),
-        jnp.zeros((VECTORS + TABLE_ROWS, width), F32),
-        jnp.zeros((WINDOW, SCORES), F32),
-    ]
-    first, first_edge, *sums = block_call(
-        False, 0, 1, False, crop_rows, fields, [cols], constants, sums
+    windows, rows_back, edge_back, corner_back, grad, small = block_call(
+        crop_rows, *fields, constants
     )
-    straddle, straddle_edge, *sums, rows_back = block_call(
-        True, 0, 2, False, crop_rows, fields, [cols, rows, corner], constants, sums
-    )
-    rows_back = pass_along(rows_back, -1, 0)
-    corner_back = pass_along(straddle_edge, -1, -1)
-    straddle_edge = pass_along(straddle_edge, 0, -1)
-    first_edge = pass_along(first_edge, 0, -1)
-    second, second_edge, grad, small = block_call(
-        False, 1, 1, True, crop_rows, fields, [cols], constants, sums
-    )
-    second_edge = pass_along(second_edge, 0, -1)
     grad, small = sum_over_devices(grad, small)
     (
         mixed, token_grad, grad_qkv, grad_proj, grad_up, grad_down, grad_mod, grad_mod_bias,
         grad_proj_bias, grad_down_bias, grad_q_bias, grad_v_bias, grad_up_bias,
     ) = merge(
-        fields[0].shape, w_up.shape[1], first, second, straddle, rows_back, first_edge, second_edge,
-        straddle_edge, corner_back, grad, small, context,
+        fields[0].shape, w_up.shape[1], windows, rows_back, edge_back, corner_back, grad, small, context
     )
     table_sum = small[VECTORS : VECTORS + 2 * WY - 1, : HEADS * OFFSETS][::-1]
     grad_table = table_sum.reshape(2 * WY - 1, 2 * WZ - 1, 2 * WX - 1, HEADS).transpose(3, 1, 0, 2)

time: 245 us -> 224 us (0.914); the launches traced: 241 us -> 224 us
  starting transfers between devices: 10.8 us -> 0 us
  waiting for transfers between devices: 6.77 us -> 0 us
    ppermute x8 -> x0, starting transfers between devices: 10.8 us -> none  [pass_along(): return lax.ppermute(block, ('lat', 'lon'), route)]
    ppermute x8 -> x0, waiting for transfers between devices: 6.77 us -> none  [pass_along(): return lax.ppermute(block, ('lat', 'lon'), route)]
    broadcast_in_dim x6, local copies, waits for them, and re-layouts: 3.45 us -> 7.43 us  [set_up(): vectors = [v[None] for v in (b_mod, b_proj, b_down, q_bias, v_bias, b_up)]]
    broadcast_in_dim x3 -> x0, local copies, waits for them, and re-layouts: 3.25 us -> none  [the longest x1 1.87 us: on_device(): jnp.zeros((4 * width + 2 * w_up.shape[1], width), F32)]
    pallas_call x5 -> x2, Pallas kernels: 163 us -> 166 us  [the longest x1 153 us: block_call(): pl.pallas_call(block_kernel, in_specs=[pl.BlockSpec(memory_space=pltpu.SM...]
  transfers between devices with their start and end apart: 8 -> 0, of which waited for: 1 -> 0; matrix products, arithmetic and copies ran while one was open for 4% -> 0% of each run, Pallas kernels for 51% -> 0%
where the time goes in v3:
time: 224 us
  Pallas kernels  213 us (95%)
  local copies, waits for them, and re-layouts  9.69 us (4%)
    pallas_call x1, Pallas kernels, block_call(): pl.pallas_call(block_kernel, in_specs=[pl.BlockSpec(memory_space=pltpu.SM...  153 us
    pallas_call x1, Pallas kernels, sum_over_devices(): pl.pallas_call(functools.partial(sum_kernel, tuple(bits), halvings, parts...  43.1 us
    pallas_call x1, Pallas kernels, merge(): pl.pallas_call(merge_kernel, grid=(level_count,), in_specs=[windows_of(Fa...  12.6 us
    broadcast_in_dim x6, local copies, waits for them, and re-layouts, set_up(): vectors = [v[None] for v in (b_mod, b_proj, b_down, q_bias, v_bias, b_up)]  7.43 us

profile of v3, /device:TPU:0, one launch (start us, length us, event | category | flops | bytes accessed | tf_op | source)
XLA Modules:
  0.0 223.7 jit_solution(16512415567394558975)
XLA Ops:
  1.3 1.2 broadcast_in_dim.21.q_bias_ref
  2.5 1.2 broadcast_in_dim.22.v_bias_ref
  3.7 1.2 broadcast_in_dim.19.b_proj_ref
  5.0 1.2 broadcast_in_dim.20.b_down_ref
  6.2 1.3 broadcast_in_dim.23.b_up_ref
  7.4 1.3 broadcast_in_dim.18.b_mod_ref
  8.7 1.4 reshape.34.table_ref
  10.1 3.7 %shard_map.263 = (f32[144,576]{1,0:T(8,128)}, f32[16,256]{1,0:T(8,128)}, f32[256,128]{1,0:T(8,128)}) custom-call(s32[1]{0:T(128)S(6)} %copy.32.lead_ref, bf16[256,1024]{1,0:T(8,128)(2,1)} %w_mod_ref.1, bf16[1,1024]{1,0:T(2,128)(2,1)} %broadcast_in_dim.18.b_mod_ref, bf16[1,256]{1,0:T(2,128)(2,1)} %broadcast_in_dim.19.b_proj_ref, ...), custom_call_target="tpu_custom_call" | custom-call | tf_op jit(solution)/shard_map/pallas_call | solution.py:121
  13.8 153.3 %shard_map.264 = (bf16[2,4,2160,256]{3,2,1,0:T(8,128)(2,1)}, bf16[2,2,2,544,256]{4,3,2,1,0:T(8,128)(2,1)}, bf16[4,2,80,256]{3,2,1,0:T(8,128)(2,1)}, bf16[2,2,80,...) custom-call(s32[8]{0:T(128)} %crop_ref.1, bf16[4,90,24,256]{3,2,1,0:T(8,128)(2,1)} %bitcast.16, ...), custom_call_target="tpu_custom_call" | custom-call | flops 44928000000 | bytes 33554432 | tf_op jit(solution)/shard_map/pallas_call | solution.py:519
  167.2 43.1 %shard_map.265 = (bf16[3072,256]{1,0:T(8,128)(2,1)}, f32[40,256]{1,0:T(8,128)}) custom-call(f32[3072,256]{1,0:T(8,128)} %get-tuple-element.44.grad_ref, f32[40,256]{1,0:T(8,128)} %get-tuple-element.45.small_ref), custom_call_target="tpu_custom_call" | custom-call | tf_op jit(solution)/shard_map/pallas_call | solution.py:664
  210.2 0.0 copy-start
  210.2 12.6 %shard_map.266 = (bf16[4,90,24,256]{3,2,1,0:T(8,128)(2,1)}, bf16[4,90,24,256]{3,2,1,0:T(8,128)(2,1)}, f32[256,768]{1,0:T(8,128)}, f32[256,256]{1,0:T(8,128)}, f3...) custom-call(bf16[2,4,2160,256]{3,2,1,0:T(8,128)(2,1)} %get-tuple-ele, ...), custom_call_target="tpu_custom_call" | custom-call | tf_op jit(solution)/shard_map/pallas_call | solution.py:783
  222.8 0.0 copy-done
  222.8 0.1 rev.3
  222.9 0.1 copy.31
  223.1 0.7 reshape.35
  (1 shorter events, 0.0 us)
Async XLA Ops:
  210.2 12.6 %copy-start = (f32[40,256]{1,0:T(8,128)S(1)}, f32[40,256]{1,0:T(8,128)}, u32[]{:S(2)}) copy-start(f32[40,256]{1,0:T(8,128)} %get-tuple-element.47.small_ref) | copy-start | bytes 122884

commit v4 on v3

--- a/solution.py
+++ b/solution.py
@@ -73,8 +73,7 @@
 
 
 def setup_kernel(
-    lead_ref, w_mod_ref, b_mod_ref, b_proj_ref, b_down_ref, q_bias_ref, v_bias_ref, b_up_ref,
-    table_ref, bias_ref, vec_ref, context_ref,
+    lead_ref, w_mod_ref, vectors_ref, table_ref, bias_ref, vec_ref, context_ref,
 ):
     width = w_mod_ref.shape[0]
     half = width // 2
@@ -91,14 +90,10 @@
             pieces.append(
                 jnp.sum(context * w_mod_ref[:, start : start + lanes].astype(F32), axis=0, keepdims=True)
             )
-        vec_ref[part : part + 1, :] = jnp.concatenate(pieces, axis=1) + b_mod_ref[
-            :, part * width : (part + 1) * width
-        ].astype(F32)
-    rows = [b_proj_ref[...], b_down_ref[...], q_bias_ref[...], jnp.zeros((1, width), BF16), v_bias_ref[...]]
-    rows += [b_up_ref[:, j * width : (j + 1) * width] for j in range(4)]
-    rows += [jnp.zeros((1, width), BF16)] * (VECTORS - 4 - len(rows))
-    for i, row in enumerate(rows):
-        vec_ref[4 + i : 5 + i, :] = row.astype(F32)
+        vec_ref[part : part + 1, :] = (
+            jnp.concatenate(pieces, axis=1) + vectors_ref[part : part + 1, :].astype(F32)
+        )
+    vec_ref[4:, :] = vectors_ref[4:, :].astype(F32)
 
     offsets_y = 2 * WY - 1
     backwards = iota((TABLE_ROWS, offsets_y), 0) + iota((TABLE_ROWS, offsets_y), 1) == offsets_y - 1
@@ -114,13 +109,12 @@
             bias_ref[start : start + WY, :] = rows
 
 
-def set_up(lead_hours, w_mod, b_mod, b_proj, b_down, q_bias, v_bias, b_up, table):
+def set_up(lead_hours, w_mod, vectors, table):
     width = w_mod.shape[0]
     vmem = pl.BlockSpec(memory_space=pltpu.VMEM)
-    vectors = [v[None] for v in (b_mod, b_proj, b_down, q_bias, v_bias, b_up)]
     return pl.pallas_call(
         setup_kernel,
-        in_specs=[pl.BlockSpec(memory_space=pltpu.SMEM)] + [vmem] * 8,
+        in_specs=[pl.BlockSpec(memory_space=pltpu.SMEM)] + [vmem] * 3,
         out_specs=[vmem] * 3,
         out_shape=[
             shape_of((WINDOW, SCORES), F32),
@@ -128,7 +122,7 @@
             shape_of((width, 128), F32),
         ],
         compiler_params=pltpu.CompilerParams(vmem_limit_bytes=VMEM_LIMIT),
-    )(lead_hours, w_mod, *vectors, table)
+    )(lead_hours, w_mod, vectors, table)
 
 
 def table_grad(score_sum_ref):
@@ -208,13 +202,21 @@
     return jnp.stack([rows[c * HALF_Y : (c + 1) * HALF_Y] for c in range(count)], axis=0)
 
 
-def mask_scores(bias, level_wraps, base, first_band, crop_own, crop_before, row_count):
+def mask_scores(bias, level_wraps, base, band, band_count, crop_ref, row_count):
+    crops = [
+        crop_ref[lax.rem(band + step + band_count, band_count)] for step in (-1, 0, 1)
+    ]
+    firsts = [
+        (lax.rem(band + step + band_count, band_count) == 0).astype(jnp.int32) for step in (0, 1)
+    ]
+
     def parts(cell):
         z, row = (cell % CELLS) // WY, base + cell % WY
         part = 2 * jnp.where(z == WZ - 1, level_wraps, 0)
-        part = part + jnp.where((row >= 0) & (row < HALF_Y), first_band, 0)
-        crop = jnp.where(row >= 0, crop_own, crop_before)
-        return part, jnp.where(row >= 0, row, row + row_count) >= row_count - crop
+        part = part + jnp.where((row >= 0) & (row < HALF_Y), firsts[0], 0)
+        part = part + jnp.where((row >= row_count) & (row < row_count + HALF_Y), firsts[1], 0)
+        crop = jnp.where(row < 0, crops[0], jnp.where(row < row_count, crops[1], crops[2]))
+        return part, (row + row_count) % row_count >= row_count - crop
 
     key = iota(bias.shape, 0)
     query = iota(bias.shape, 1) % WINDOW
@@ -225,6 +227,7 @@
 
 
 GROUPS = 4
+TOWARD = (1, 1)
 
 
 def group_pair(group):
@@ -238,7 +241,7 @@
 def block_kernel(
     crop_ref, tokens_ref, cotangent_ref, bias_ref, vec_ref, w_qkv_ref, w_proj_ref, w_up_ref, w_down_ref,
     win_ref, rows_back_ref, edge_back_ref, corner_back_ref, grad_ref, small_ref,
-    fields_ref, rows_out_ref, rows_in_ref, cols_in_ref, corner_in_ref, out_ref,
+    fields_ref, rows_out_ref, rows_in_ref, cols_in_ref, corner_out_ref, corner_in_ref, out_ref,
     score_bias_ref, xw_ref, gw_ref, qkv_ref, prob_ref, att_ref, dqkv_ref, score_sum_ref,
     field_sems, halo_sems, rows_sems, back_sems, edge_sems, corner_sems, out_sems,
 ):
@@ -255,7 +258,7 @@
             lax.rem(lat + lat_step + lat_size, lat_size), lax.rem(lon + lon_step + lon_size, lon_size)
         )
 
-    steps = ((1, 0), (0, 1), (1, 1))
+    steps = [(0, 1)] + [(t, lon_step) for t in sorted(set(TOWARD)) for lon_step in (0, 1)]
     barrier = pltpu.get_barrier_semaphore()
     for lat_step, lon_step in steps:
         for sign in (1, -1):
@@ -279,13 +282,20 @@
 
     last_cols = fields_ref.at[:, :, pl.ds(col_count - HALF_X, HALF_X)]
     cols_copy = remote(last_cols, cols_in_ref, halo_sems.at[0], 0, 1)
-    corner_copy = remote(last_cols, corner_in_ref, halo_sems.at[1], 1, 1)
+    corner_copies = [
+        remote(corner_out_ref.at[pair], corner_in_ref.at[pair], halo_sems.at[1 + pair], TOWARD[pair], 1)
+        for pair in range(2)
+    ]
 
     def rows_copy(pair):
-        return remote(rows_out_ref.at[pair], rows_in_ref.at[pair], rows_sems.at[pair], 1, 0)
+        return remote(
+            rows_out_ref.at[pair], rows_in_ref.at[pair], rows_sems.at[pair], TOWARD[pair], 0
+        )
 
     def back_copy(pair):
-        return remote(rows_out_ref.at[pair], rows_back_ref.at[pair], back_sems.at[pair], -1, 0)
+        return remote(
+            rows_out_ref.at[pair], rows_back_ref.at[pair], back_sems.at[pair], -TOWARD[pair], 0
+        )
 
     def edge_rows(group):
         return out_ref.at[lax.rem(group, 2), :, pl.ds(0, edge_back_ref.shape[2])]
@@ -293,9 +303,10 @@
     def edge_copy(group):
         return remote(edge_rows(group), edge_back_ref.at[group], edge_sems.at[group], 0, -1)
 
-    def corner_back_copy(group):
-        pair = group_pair(group)
-        return remote(edge_rows(group), corner_back_ref.at[pair], corner_sems.at[pair], -1, -1)
+    def corner_back_copy(pair):
+        return remote(
+            edge_rows(1 + pair), corner_back_ref.at[pair], corner_sems.at[pair], -TOWARD[pair], -1
+        )
 
     def out_copy(group):
         return pltpu.make_async_copy(
@@ -303,22 +314,31 @@
         )
 
     for pair in range(2):
+        corners = []
+        sent = slice(row_count - HALF_Y, row_count) if TOWARD[pair] == 1 else slice(0, HALF_Y)
         for z in range(WZ):
             level = (WZ * pair + z + WZ // 2) % level_count
             for a in range(2):
-                loads[(pair * WZ + z) * 2 + a].wait()
+                if pair == 0:
+                    loads[z * 2 + a].wait()
                 for start in range(0, col_count, PACKED_COLS):
                     count = min(PACKED_COLS, col_count - start)
                     block = fields_ref[a, level, start : start + count].astype(F32)
-                    packed = [block[c, row_count - HALF_Y :] for c in range(count)]
+                    packed = [block[c, sent] for c in range(count)]
                     rows_out_ref[
                         pair, a, z, start * HALF_Y : (start + count) * HALF_Y, :
                     ] = jnp.concatenate(packed, axis=0).astype(BF16)
+                block = fields_ref[a, level, col_count - HALF_X :].astype(F32)
+                corners += [block[c, sent] for c in range(HALF_X)]
+        spare = corner_out_ref.shape[1] - HALF_Y * len(corners)
+        corners.append(jnp.zeros((spare, width), F32))
+        corner_out_ref[pair] = jnp.concatenate(corners, axis=0).astype(BF16)
         if pair == 0:
             pl.semaphore_wait(barrier, 2 * len(steps))
-        rows_copy(pair).start()
-    cols_copy.start()
-    corner_copy.start()
+            rows_copy(0).start()
+            for load in loads[2 * WZ :]:
+                load.wait()
+            cols_copy.start()
 
     grad_ref[...] = jnp.zeros_like(grad_ref)
     small_ref[...] = jnp.zeros_like(small_ref)
@@ -339,7 +359,14 @@
     def column_sums(values):
         return jnp.sum(values, axis=0, keepdims=True)
 
-    def block(index, slot):
+    def block(index, group):
+        slot = lax.rem(group, 2)
+
+        @pl.when((group == 0) & (index == 2))
+        def _():
+            rows_copy(1).start()
+            corner_copies[1].start()
+
         here = pl.ds(pl.multiple_of(index * rows, 16), rows)
         x32 = xw_ref[here, :]
         x = x32.astype(BF16)
@@ -408,41 +435,51 @@
         sums += [up_sums[:, j * width : (j + 1) * width] for j in range(hidden_width // width)]
         sums += [jnp.zeros((VECTORS - len(sums), width), F32)]
         small_ref[:VECTORS, :] += jnp.concatenate(sums, axis=0)
-        return slot
-
-    def gather(pair, straddles):
+        return group
+
+    def gather(pair, group):
+        def assemble(own, strip, axis):
+            if group in (0, GROUPS - 1):
+                return lax.slice_in_dim(own, HALF_Y, HALF_Y + WY, axis=axis)
+            if TOWARD[pair] == 1:
+                return jnp.concatenate([strip, lax.slice_in_dim(own, 0, HALF_Y, axis=axis)], axis=axis)
+            return jnp.concatenate(
+                [lax.slice_in_dim(own, row_count - HALF_Y, row_count, axis=axis), strip], axis=axis
+            )
+
         for a, target in enumerate((xw_ref, gw_ref)):
             def field(start, count, z, a=a):
                 own = fields_ref[a, field_level(pair, z), start : start + count].astype(F32)
-                if not straddles:
-                    return own[:, HALF_Y : HALF_Y + WY]
-                strip = rows_in_ref[pair, a, z, start * HALF_Y : (start + count) * HALF_Y, :]
-                return jnp.concatenate(
-                    [unpack_strip(strip.astype(F32), count), own[:, :HALF_Y]], axis=1
-                )
+                strip = None
+                if group in (1, 2):
+                    strip = rows_in_ref[pair, a, z, start * HALF_Y : (start + count) * HALF_Y, :]
+                    strip = unpack_strip(strip.astype(F32), count)
+                return assemble(own, strip, 1)
 
             def western(c, z, a=a):
                 own = cols_in_ref[a, field_level(pair, z), c].astype(F32)
-                if not straddles:
-                    return own[HALF_Y : HALF_Y + WY]
-                before = corner_in_ref[a, field_level(pair, z), c].astype(F32)
-                return jnp.concatenate([before[row_count - HALF_Y :], own[:HALF_Y]], axis=0)
+                strip = None
+                if group in (1, 2):
+                    place = ((z * 2 + a) * HALF_X + c) * HALF_Y
+                    strip = corner_in_ref[pair].astype(F32)[place : place + HALF_Y]
+                return assemble(own, strip, 0)
 
             store_windows(field, western, target)
 
     def send_back(pair, slot):
+        sent = 0 if TOWARD[pair] == 1 else HALF_Y
         for a in range(2):
             for start in range(0, col_count - HALF_X, PACKED_COLS):
                 count = min(PACKED_COLS, col_count - HALF_X - start)
                 first = (start + HALF_X) * CELLS
                 cells = out_ref[slot, a, first : first + count * CELLS, :].astype(F32)
                 for z in range(WZ):
-                    pieces = [
-                        cells[c * CELLS + z * WY : c * CELLS + z * WY + HALF_Y] for c in range(count)
-                    ]
+                    places = [c * CELLS + z * WY + sent for c in range(count)]
                     rows_out_ref[
                         pair, a, z, start * HALF_Y : (start + count) * HALF_Y, :
-                    ] = jnp.concatenate(pieces, axis=0).astype(BF16)
+                    ] = jnp.concatenate(
+                        [cells[p : p + HALF_Y] for p in places], axis=0
+                    ).astype(BF16)
         back_copy(pair).start()
 
     def group_step(group, carry):
@@ -451,11 +488,8 @@
 
         @pl.when(group == 0)
         def _():
+            corner_copies[0].start()
             cols_copy.wait_recv()
-
-        @pl.when(group == 1)
-        def _():
-            corner_copy.wait_recv()
 
         @pl.when(group >= 2)
         def _():
@@ -464,30 +498,34 @@
 
         @pl.when(group == GROUPS - 1)
         def _():
-            corner_back_copy(1).wait_send()
+            corner_back_copy(0).wait_send()
 
         @pl.when(inner)
         def _():
-            gather(pair, False)
-
-        @pl.when(jnp.logical_not(inner))
-        def _():
-            rows_copy(pair).wait_recv()
-            gather(pair, True)
-
+            gather(pair, 0)
+
+        for straddling in range(2):
+            @pl.when(group == 1 + straddling)
+            def _():
+                rows_copy(straddling).wait_recv()
+                corner_copies[straddling].wait_recv()
+                gather(straddling, 1 + straddling)
+
+        bases = [-HALF_Y if step == 1 else row_count - HALF_Y for step in TOWARD]
+        base = jnp.where(inner, HALF_Y, jnp.where(group == 1, bases[0], bases[1]))
         score_bias_ref[...] = mask_scores(
-            bias_ref[...], pair, jnp.where(inner, HALF_Y, -HALF_Y), (lat == 0).astype(jnp.int32),
-            crop_ref[lat], crop_ref[lax.rem(lat + band_count - 1, band_count)], row_count,
-        )
-        lax.fori_loop(0, col_count // WX // BLOCK_WINDOWS, block, slot)
+            bias_ref[...], pair, base, lat, band_count, crop_ref, row_count
+        )
+        lax.fori_loop(0, col_count // WX // BLOCK_WINDOWS, block, group)
         out_copy(group).start()
         edge_copy(group).start()
 
-        @pl.when(jnp.logical_not(inner))
-        def _():
-            corner_back_copy(group).start()
-            rows_copy(pair).wait_send()
-            send_back(pair, slot)
+        for straddling in range(2):
+            @pl.when(group == 1 + straddling)
+            def _():
+                corner_back_copy(straddling).start()
+                rows_copy(straddling).wait_send()
+                send_back(straddling, slot)
 
         return carry
 
@@ -496,12 +534,13 @@
     for group in (2, 3):
         out_copy(group).wait()
         edge_copy(group).wait_send()
-    corner_back_copy(2).wait_send()
+    corner_back_copy(1).wait_send()
     cols_copy.wait_send()
-    corner_copy.wait_send()
+    for copy in corner_copies:
+        copy.wait_send()
     for pair in range(2):
         back_copy(pair).wait()
-        corner_back_copy(pair + 1).wait_recv()
+        corner_back_copy(pair).wait_recv()
     for group in range(GROUPS):
         edge_copy(group).wait_recv()
 
@@ -533,7 +572,8 @@
             pltpu.VMEM(strips, BF16),
             pltpu.VMEM(strips, BF16),
             pltpu.VMEM((2, level_count, HALF_X, row_count, width), BF16),
-            pltpu.VMEM((2, level_count, HALF_X, row_count, width), BF16),
+            pltpu.VMEM((pairs, edge, width), BF16),
+            pltpu.VMEM((pairs, edge, width), BF16),
             pltpu.VMEM((2, 2, cells, width), BF16),
             pltpu.VMEM((WINDOW, SCORES), F32),
             pltpu.VMEM((cells, width), F32),
@@ -543,7 +583,7 @@
             pltpu.VMEM((rows, width), BF16),
             pltpu.VMEM((rows, 3 * width), BF16),
             pltpu.VMEM((WINDOW, SCORES), F32),
-            sends((2 * level_count,)), sends((2, 2)), sends((pairs, 2)), sends((pairs, 2)),
+            sends((2 * level_count,)), sends((3, 2)), sends((pairs, 2)), sends((pairs, 2)),
             sends((GROUPS, 2)), sends((pairs, 2)), sends((GROUPS,)),
         ],
         cost_estimate=pl.CostEstimate(
@@ -697,26 +737,30 @@
     straddle_edge, inner_edge, corner = (
         lambda a, ref=ref: ref.at[0, a] for ref in (straddle_edge_ref, inner_edge_ref, corner_ref)
     )
-    for z in range(WZ):
-        @pl.when(lax.rem(step, WZ) == z)
+    for pair, z in ((0, 0), (0, 1), (1, 0), (1, 1)):
+        @pl.when(step == pair * WZ + z)
         def _():
             first = z * WY
+            kept, sent = (HALF_Y, 0) if TOWARD[pair] == 1 else (0, HALF_Y)
+
+            def in_order(own, inner_rows, back):
+                parts = [own, inner_rows, back] if TOWARD[pair] == 1 else [back, inner_rows, own]
+                return jnp.concatenate(parts, axis=1).astype(BF16)
+
             for a, field in enumerate(fields):
                 for start in range(0, col_count - HALF_X, PACKED_COLS):
                     count = min(PACKED_COLS, col_count - HALF_X - start)
                     strip = rows_ref[0, a, 0, start * HALF_Y : (start + count) * HALF_Y, :]
-                    block = jnp.concatenate([
-                        piece(straddle, a, start + HALF_X, count, first + HALF_Y, HALF_Y),
+                    field[0, start : start + count] = in_order(
+                        piece(straddle, a, start + HALF_X, count, first + kept, HALF_Y),
                         piece(inner, a, start + HALF_X, count, first, WY),
                         unpack_strip(strip.astype(F32), count),
-                    ], axis=1)
-                    field[0, start : start + count] = block.astype(BF16)
-                block = jnp.concatenate([
-                    piece(straddle_edge, a, 0, HALF_X, first + HALF_Y, HALF_Y),
+                    )
+                field[0, col_count - HALF_X :] = in_order(
+                    piece(straddle_edge, a, 0, HALF_X, first + kept, HALF_Y),
                     piece(inner_edge, a, 0, HALF_X, first, WY),
-                    piece(corner, a, 0, HALF_X, first, HALF_Y),
-                ], axis=1)
-                field[0, col_count - HALF_X :] = block.astype(BF16)
+                    piece(corner, a, 0, HALF_X, first + sent, HALF_Y),
+                )
 
     grad_qkv, grad_proj, grad_up, grad_down, grad_mod, *vectors = grads
 
@@ -801,9 +845,11 @@
 ):
     fields = [field.transpose(0, 2, 1, 3) for field in (tokens, cotangent)]
     table = rel_table.transpose(1, 3, 0, 2).reshape(HEADS * OFFSETS, 2 * WY - 1)
-    bias, vecs, context = set_up(
-        lead_hours, w_mod, b_mod, b_proj, b_down, q_bias, v_bias, b_up, table
-    )
+    nothing = jnp.zeros_like(q_bias)
+    vectors = jnp.concatenate(
+        [b_mod, b_proj, b_down, q_bias, nothing, v_bias, b_up] + [nothing] * 3
+    ).reshape(VECTORS, -1)
+    bias, vecs, context = set_up(lead_hours, w_mod, vectors, table)
     constants = [bias, vecs, w_qkv, w_proj, w_up, w_down]
     windows, rows_back, edge_back, corner_back, grad, small = block_call(
         crop_rows, *fields, constants

time: 224 us -> 199 us (0.89)
  Pallas kernels: 213 us -> 189 us
    pallas_call x1, Pallas kernels: 153 us -> 129 us  [block_call(): pl.pallas_call(block_kernel, in_specs=[pl.BlockSpec(memory_space=pltpu.SM...]
    broadcast_in_dim x6 -> x1, local copies, waits for them, and re-layouts: 7.43 us -> 0.01 us  [on_device(): nothing = jnp.zeros_like(q_bias)]
    unnamed x2 -> x9, local copies, waits for them, and re-layouts: 0.01 us -> 5.1 us
where the time goes in v4:
time: 199 us
  Pallas kernels  189 us (95%)
  local copies, waits for them, and re-layouts  8.18 us (4%)
    pallas_call x1, Pallas kernels, block_call(): pl.pallas_call(block_kernel, in_specs=[pl.BlockSpec(memory_space=pltpu.SM...  129 us
    pallas_call x1, Pallas kernels, sum_over_devices(): pl.pallas_call(functools.partial(sum_kernel, tuple(bits), halvings, parts...  43.7 us
    pallas_call x1, Pallas kernels, merge(): pl.pallas_call(merge_kernel, grid=(level_count,), in_specs=[windows_of(Fa...  12.6 us
    unnamed x9, local copies, waits for them, and re-layouts  5.1 us

profile of v4, /device:TPU:0, one launch (start us, length us, event | category | flops | bytes accessed | tf_op | source)
XLA Modules:
  0.0 198.8 jit_solution(2372718769048664692)
XLA Ops:
  1.3 0.7 constant_dynamic-update-slice_fusion
  2.0 0.8 dynamic-update-slice.1
  2.8 0.8 dynamic-update-slice.2
  3.6 0.8 dynamic-update-slice.3
  4.5 0.2 dynamic-update-slice.4
  4.7 0.8 dynamic-update-slice.5
  5.5 0.8 dynamic-update-slice.6
  6.4 0.2 dynamic-update-slice.7
  6.6 0.6 reshape.37.vectors_ref
  7.2 1.4 reshape.38.table_ref
  8.6 3.6 %shard_map.263 = (f32[144,576]{1,0:T(8,128)}, f32[16,256]{1,0:T(8,128)}, f32[256,128]{1,0:T(8,128)}) custom-call(s32[1]{0:T(128)S(6)} %copy.39.lead_ref, bf16[256,1024]{1,0:T(8,128)(2,1)} %w_mod_ref.1, bf16[16,256]{1,0:T(8,128)(2,1)} %reshape.37.vectors_ref, bf16[132,23]{1,0:T(8,128)(2,1)} %reshape.38.table_ref), custom_call_target="tpu_custom_call" | custom-call | tf_op jit(solution)/shard_map/pallas_call | solution.py:115
  12.3 129.3 %shard_map.264 = (bf16[2,4,2160,256]{3,2,1,0:T(8,128)(2,1)}, bf16[2,2,2,544,256]{4,3,2,1,0:T(8,128)(2,1)}, bf16[4,2,80,256]{3,2,1,0:T(8,128)(2,1)}, bf16[2,2,80,...) custom-call(s32[8]{0:T(128)} %crop_ref.1, bf16[4,90,24,256]{3,2,1,0:T(8,128)(2,1)} %bitcast.16, ...), custom_call_target="tpu_custom_call" | custom-call | flops 44928000000 | bytes 33554432 | tf_op jit(solution)/shard_map/pallas_call | solution.py:558
  141.6 43.7 %shard_map.265 = (bf16[3072,256]{1,0:T(8,128)(2,1)}, f32[40,256]{1,0:T(8,128)}) custom-call(f32[3072,256]{1,0:T(8,128)} %get-tuple-element.44.grad_ref, f32[40,256]{1,0:T(8,128)} %get-tuple-element.45.small_ref), custom_call_target="tpu_custom_call" | custom-call | tf_op jit(solution)/shard_map/pallas_call | solution.py:704
  185.3 0.0 copy-start
  185.3 12.6 %shard_map.266 = (bf16[4,90,24,256]{3,2,1,0:T(8,128)(2,1)}, bf16[4,90,24,256]{3,2,1,0:T(8,128)(2,1)}, f32[256,768]{1,0:T(8,128)}, f32[256,256]{1,0:T(8,128)}, f3...) custom-call(bf16[2,4,2160,256]{3,2,1,0:T(8,128)(2,1)} %get-tuple-ele, ...), custom_call_target="tpu_custom_call" | custom-call | tf_op jit(solution)/shard_map/pallas_call | solution.py:827
  197.9 0.0 copy-done
  197.9 0.1 rev.3
  198.0 0.1 copy.31
  198.1 0.7 reshape.39
  (3 shorter events, 0.0 us)
Async XLA Ops:
  185.3 12.6 %copy-start = (f32[40,256]{1,0:T(8,128)S(1)}, f32[40,256]{1,0:T(8,128)}, u32[]{:S(2)}) copy-start(f32[40,256]{1,0:T(8,128)} %get-tuple-element.47.small_ref) | copy-start | bytes 122884

commit v5 on v4

--- a/solution.py
+++ b/solution.py
@@ -20,6 +20,7 @@
 BLOCK_WINDOWS = 5
 OFFSETS = (2 * WZ - 1) * (2 * WX - 1)
 VECTORS = 16
+LANES = 128
 TABLE_ROWS = 2 * WY
 EDGE = HALF_X * CELLS
 PACKED_COLS = 8
@@ -73,7 +74,8 @@
 
 
 def setup_kernel(
-    lead_ref, w_mod_ref, vectors_ref, table_ref, bias_ref, vec_ref, context_ref,
+    lead_ref, w_mod_ref, b_mod_ref, b_proj_ref, b_down_ref, q_bias_ref, v_bias_ref, b_up_ref,
+    table_ref, bias_ref, vec_ref, context_ref,
 ):
     width = w_mod_ref.shape[0]
     half = width // 2
@@ -91,13 +93,21 @@
                 jnp.sum(context * w_mod_ref[:, start : start + lanes].astype(F32), axis=0, keepdims=True)
             )
         vec_ref[part : part + 1, :] = (
-            jnp.concatenate(pieces, axis=1) + vectors_ref[part : part + 1, :].astype(F32)
-        )
-    vec_ref[4:, :] = vectors_ref[4:, :].astype(F32)
+            jnp.concatenate(pieces, axis=1)
+            + b_mod_ref[part * width : (part + 1) * width].astype(F32)[None]
+        )
+    vec_ref[4:, :] = jnp.zeros((VECTORS - 4, width), F32)
+    for i, ref in ((4, b_proj_ref), (5, b_down_ref), (6, q_bias_ref), (8, v_bias_ref)):
+        vec_ref[i : i + 1, :] = ref[...].astype(F32)[None]
+    for j in range(b_up_ref.shape[0] // width):
+        vec_ref[9 + j : 10 + j, :] = b_up_ref[j * width : (j + 1) * width].astype(F32)[None]
 
     offsets_y = 2 * WY - 1
     backwards = iota((TABLE_ROWS, offsets_y), 0) + iota((TABLE_ROWS, offsets_y), 1) == offsets_y - 1
-    table = dot_nt(backwards.astype(BF16), table_ref[...]).astype(BF16)
+    table = jnp.concatenate(
+        [table_ref[z, x].astype(F32) for z in range(2 * WZ - 1) for x in range(2 * WX - 1)], axis=0
+    ).astype(BF16)
+    table = dot_nt(backwards.astype(BF16), table).astype(BF16)
     query_y = iota((WY, SCORES), 1) % WY
     for key_x in range(WX):
         for key_z in range(WZ):
@@ -114,7 +124,7 @@
     vmem = pl.BlockSpec(memory_space=pltpu.VMEM)
     return pl.pallas_call(
         setup_kernel,
-        in_specs=[pl.BlockSpec(memory_space=pltpu.SMEM)] + [vmem] * 3,
+        in_specs=[pl.BlockSpec(memory_space=pltpu.SMEM)] + [vmem] * (2 + len(vectors)),
         out_specs=[vmem] * 3,
         out_shape=[
             shape_of((WINDOW, SCORES), F32),
@@ -122,7 +132,7 @@
             shape_of((width, 128), F32),
         ],
         compiler_params=pltpu.CompilerParams(vmem_limit_bytes=VMEM_LIMIT),
-    )(lead_hours, w_mod, vectors, table)
+    )(lead_hours, w_mod, *vectors, table)
 
 
 def table_grad(score_sum_ref):
@@ -147,6 +157,31 @@
     return total
 
 
+def halved(rows, count):
+    sizes = [rows >> (i + 1) for i in range(count)]
+    return sizes, [sum(sizes[:i]) for i in range(count + 1)]
+
+
+def sum_bits():
+    bits = [("lon", 0), ("lon", 1), ("lat", 0), ("lat", 1), ("lat", 2)]
+    bits = [b for b in bits if 2 ** b[1] < lax.axis_size(b[0])]
+    bits += [("lat", b) for b in range(3, lax.axis_size("lat").bit_length() - 1)]
+    bits += [("lon", b) for b in range(2, lax.axis_size("lon").bit_length() - 1)]
+    return bits, min(5, len(bits))
+
+
+def peer_sizes():
+    lons, lats = lax.axis_size("lon") // 2, min(8, lax.axis_size("lat"))
+    return lons, lats, lons * lats
+
+
+def sum_parts(width, hidden_width):
+    qkv_rows = 3 * width * (width // LANES)
+    rest = (width + 2 * hidden_width) * (width // LANES)
+    first = -(-rest // 1024) * 512
+    return [(qkv_rows, first), (qkv_rows + first, rest - first), (0, qkv_rows)]
+
+
 def row_mean(values):
     return jnp.mean(values, axis=-1, keepdims=True)
 
@@ -240,10 +275,12 @@
 
 def block_kernel(
     crop_ref, tokens_ref, cotangent_ref, bias_ref, vec_ref, w_qkv_ref, w_proj_ref, w_up_ref, w_down_ref,
-    win_ref, rows_back_ref, edge_back_ref, corner_back_ref, grad_ref, small_ref,
-    fields_ref, rows_out_ref, rows_in_ref, cols_in_ref, corner_out_ref, corner_in_ref, out_ref,
-    score_bias_ref, xw_ref, gw_ref, qkv_ref, prob_ref, att_ref, dqkv_ref, score_sum_ref,
-    field_sems, halo_sems, rows_sems, back_sems, edge_sems, corner_sems, out_sems,
+    win_ref, rows_back_ref, edge_back_ref, corner_back_ref, sum_ref, small_ref,
+    grad_ref, send_ref, recv_ref, more_ref, small_recv_ref, scatter_ref, pieces_ref, fields_ref, rows_out_ref, rows_in_ref, cols_in_ref, corner_out_ref, corner_in_ref, out_ref,
+    score_bias_ref, xw_ref, gw_ref, qkv_ref, prob_ref, att_ref, middle_grad_ref, dqkv_ref,
+    score_sum_ref,
+    field_sems, halo_sems, rows_sems, back_sems, edge_sems, corner_sems, out_sems, sum_sems, small_sems,
+    peer_sems,
 ):
     width = vec_ref.shape[1]
     hidden_width = w_up_ref.shape[1]
@@ -265,6 +302,26 @@
             pl.semaphore_signal(
                 barrier, inc=1, device_id=device(sign * lat_step, sign * lon_step), device_id_type=MESH
             )
+
+    bits, halvings = sum_bits()
+    own_bit, partner = {}, {}
+    for axis, bit in bits:
+        place = lat if axis == "lat" else lon
+        own_bit[axis, bit] = (place // 2**bit) % 2
+        moved = place + 2**bit * (1 - 2 * own_bit[axis, bit])
+        partner[axis, bit] = (moved, lon) if axis == "lat" else (lat, moved)
+        pl.semaphore_signal(barrier, inc=1, device_id=partner[axis, bit], device_id_type=MESH)
+    peer_lons, peer_lats, peer_count = peer_sizes()
+    my_peer = lon // 2 + peer_lons * (lat % peer_lats)
+
+    def peer(step):
+        index = (my_peer + step) % peer_count
+        return index, (
+            (lat // peer_lats) * peer_lats + index // peer_lons, 2 * (index % peer_lons) + lon % 2
+        )
+
+    for step in range(1, peer_count):
+        pl.semaphore_signal(barrier, inc=1, device_id=peer(step)[1], device_id_type=MESH)
 
     loads = []
     for level in (1, 2, 3, 0):
@@ -334,7 +391,7 @@
         corners.append(jnp.zeros((spare, width), F32))
         corner_out_ref[pair] = jnp.concatenate(corners, axis=0).astype(BF16)
         if pair == 0:
-            pl.semaphore_wait(barrier, 2 * len(steps))
+            pl.semaphore_wait(barrier, 2 * len(steps) + len(bits) + peer_count - 1)
             rows_copy(0).start()
             for load in loads[2 * WZ :]:
                 load.wait()
@@ -351,91 +408,270 @@
     b_up = jnp.concatenate([vec_ref[i : i + 1, :] for i in range(9, 13)], axis=1)
 
     def add_grad(first, value):
-        for j in range(value.shape[1] // width):
+        for j in range(value.shape[1] // LANES):
             grad_ref[(first + j) * width : (first + j + 1) * width, :] += value[
-                :, j * width : (j + 1) * width
+                :, j * LANES : (j + 1) * LANES
             ]
+
+    parts = sum_parts(width, hidden_width)
+    sizes, send_starts = zip(*[halved(count, halvings) for _, count in parts])
+    orders, lows = [], []
+    for p, (first, _) in enumerate(parts):
+        order = list(bits[:halvings])
+        if p == 1 and halvings > 2:
+            order[1], order[2] = order[2], order[1]
+        orders.append(order)
+        lows.append([first])
+        for s, bit in enumerate(order):
+            lows[p].append(lows[p][s] + own_bit[bit] * sizes[p][s])
+
+    def to_partner(source, target, sems, bit):
+        return pltpu.make_async_remote_copy(
+            src_ref=source, dst_ref=target, send_sem=sems.at[0], recv_sem=sems.at[1],
+            device_id=partner[bit], device_id_type=MESH,
+        )
+
+    def half_place(p, s):
+        return pl.ds(sum(starts[-1] for starts in send_starts[:p]) + send_starts[p][s], sizes[p][s])
+
+    def half_copy(p, s):
+        place = half_place(p, s)
+        return to_partner(send_ref.at[place], recv_ref.at[place], sum_sems.at[p, s], orders[p][s])
+
+    def halve(p, s):
+        size, bit = sizes[p][s], orders[p][s]
+        away = pl.multiple_of(lows[p][s] + (1 - own_bit[bit]) * size, 16)
+        send_ref[half_place(p, s), :] = grad_ref[pl.ds(away, size), :].astype(BF16)
+        half_copy(p, s).start()
+
+    def add_half(p, s):
+        half_copy(p, s).wait()
+        here = pl.ds(pl.multiple_of(lows[p][s + 1], 16), sizes[p][s])
+        grad_ref[here, :] += recv_ref[half_place(p, s), :].astype(F32)
+
+    def shard_done(p):
+        here = pl.ds(pl.multiple_of(lows[p][halvings], 16), sizes[p][-1])
+        sum_ref[here, :] = grad_ref[here, :].astype(BF16)
+        exchange_shard(p, here, sizes[p][-1])
+
+    def exchange_shard(p, here, count):
+        for s in range(halvings, len(bits)):
+            mine = more_ref.at[0, p, s - halvings, pl.ds(0, count)]
+            theirs = more_ref.at[1, p, s - halvings, pl.ds(0, count)]
+            mine[...] = sum_ref[here, :]
+            copy = to_partner(mine, theirs, sum_sems.at[p, s], bits[s])
+            copy.start()
+            copy.wait()
+            sum_ref[here, :] = (mine[...].astype(F32) + theirs[...].astype(F32)).astype(BF16)
+
+    def give_copy(p, s):
+        here = sum_ref.at[pl.ds(pl.multiple_of(lows[p][s + 1], 16), sizes[p][s]), :]
+        return to_partner(here, here, sum_sems.at[p, len(bits) + s], orders[p][s])
+
+    def sum_step(p, k):
+        if 1 <= k <= halvings:
+            add_half(p, k - 1)
+        if k < halvings:
+            halve(p, k)
+        if k == halvings:
+            shard_done(p)
+        if halvings < k <= 2 * halvings:
+            give_copy(p, 2 * halvings - k).wait()
+        if halvings <= k < 2 * halvings:
+            give_copy(p, 2 * halvings - 1 - k).start()
+
+    early, late = (0, 1), 2
+    hidden_steps = min(4, halvings)
+
+    piece = sizes[late][0] // peer_count
+
+    def piece_place(index):
+        return pl.ds(pl.multiple_of(lows[late][1] + index * piece, 16), piece)
+
+    def scatter_copy(step):
+        index, there = peer(step)
+        return pltpu.make_async_remote_copy(
+            src_ref=scatter_ref.at[pl.ds(pl.multiple_of(index * piece, 16), piece), :],
+            dst_ref=pieces_ref.at[step], send_sem=peer_sems.at[0, step, 0],
+            recv_sem=peer_sems.at[0, step, 1], device_id=there, device_id_type=MESH,
+        )
+
+    def gather_copy(step):
+        mine = sum_ref.at[piece_place(my_peer), :]
+        return pltpu.make_async_remote_copy(
+            src_ref=mine, dst_ref=mine, send_sem=peer_sems.at[1, step, 0],
+            recv_sem=peer_sems.at[1, step, 1], device_id=peer(step)[1], device_id_type=MESH,
+        )
+
+    def late_step(k):
+        others = range(1, peer_count)
+        if k == 0:
+            halve(late, 0)
+        elif k == 1:
+            add_half(late, 0)
+            half = pl.ds(pl.multiple_of(lows[late][1], 16), sizes[late][0])
+            scatter_ref[...] = grad_ref[half, :].astype(BF16)
+            for step in others:
+                scatter_copy(step).start()
+        elif k == 2:
+            total = grad_ref[piece_place(my_peer), :]
+            for step in others:
+                scatter_copy(step).wait()
+                total = total + pieces_ref[step].astype(F32)
+            sum_ref[piece_place(my_peer), :] = total.astype(BF16)
+            exchange_shard(late, piece_place(my_peer), piece)
+            for step in others:
+                gather_copy(step).start()
+        elif k == 3:
+            for step in others:
+                gather_copy(step).wait()
+            give_copy(late, 0).start()
+        elif k == 4:
+            give_copy(late, 0).wait()
 
     def column_sums(values):
         return jnp.sum(values, axis=0, keepdims=True)
 
-    def block(index, group):
+    def forward(index, group, kept):
         slot = lax.rem(group, 2)
-
-        @pl.when((group == 0) & (index == 2))
-        def _():
-            rows_copy(1).start()
-            corner_copies[1].start()
-
         here = pl.ds(pl.multiple_of(index * rows, 16), rows)
         x32 = xw_ref[here, :]
         x = x32.astype(BF16)
-        qkv_ref[...] = (dot_nn(x, w_qkv_ref[...]) + qkv_shift).astype(BF16)
+        qkv_ref[kept] = (dot_nn(x, w_qkv_ref[...]) + qkv_shift).astype(BF16)
         for w in range(BLOCK_WINDOWS):
             cells = pl.ds(w * WINDOW, WINDOW)
-            queries = by_head(qkv_ref[cells, :width] * BF16(score_scale))
-            scores = dot_nt(qkv_ref[cells, width : 2 * width], queries) + score_bias_ref[...]
+            queries = by_head(qkv_ref[kept, cells, :width] * BF16(score_scale))
+            scores = dot_nt(qkv_ref[kept, cells, width : 2 * width], queries) + score_bias_ref[...]
             top = jnp.max(scores, axis=0, keepdims=True)
             exps = jnp.exp(scores - top)
             prob = exps * (1.0 / jnp.sum(exps, axis=0, keepdims=True))
-            prob_ref[w] = prob
-            att_ref[cells, :] = own_head(
-                dot_tn(prob.astype(BF16), qkv_ref[cells, 2 * width :])
+            prob_ref[kept, w] = prob
+            att_ref[kept, cells, :] = own_head(
+                dot_tn(prob.astype(BF16), qkv_ref[kept, cells, 2 * width :])
             ).astype(BF16)
-
-        att = att_ref[...]
+            yield
+
+        att = att_ref[kept]
         branch = dot_nn(att, w_proj_ref[...]) + b_proj
+        yield
         norm_one, inverse_one = norm(branch)
         middle = x32 + norm_one * (1.0 + scale_one) + shift_one
         middle_low = middle.astype(BF16)
         pre = dot_nn(middle_low, w_up_ref[...]) + b_up
+        yield
         hidden, slope = gelu_both(pre)
         hidden = hidden.astype(BF16)
         second = dot_nn(hidden, w_down_ref[...]) + b_down
+        yield
         norm_two, inverse_two = norm(second)
         out_ref[slot, 0, here, :] = (middle + norm_two * (1.0 + scale_two) + shift_two).astype(BF16)
 
         g = gw_ref[here, :]
+        yield
         second_low = norm_back(g * (1.0 + scale_two), norm_two, inverse_two).astype(BF16)
         pre_grad = dot_nt(second_low, w_down_ref[...]) * slope
-        add_grad(8, dot_tn(second_low, hidden))
+        yield
+        add_grad(16, dot_tn(second_low, hidden))
+        yield
         pre_low = pre_grad.astype(BF16)
         up_sums = column_sums(pre_grad)
         middle_grad = g + dot_nt(pre_low, w_up_ref[...])
-        add_grad(4, dot_tn(middle_low, pre_low))
+        yield
+        add_grad(8, dot_tn(middle_low, pre_low))
+        yield
         branch_low = norm_back(middle_grad * (1.0 + scale_one), norm_one, inverse_one).astype(BF16)
-        att_ref[...] = dot_nt(branch_low, w_proj_ref[...]).astype(BF16)
-        add_grad(3, dot_tn(att, branch_low))
-
-        for w in range(BLOCK_WINDOWS):
-            cells = pl.ds(w * WINDOW, WINDOW)
-            queries = by_head(qkv_ref[cells, :width] * BF16(score_scale))
-            out_grad = by_head(att_ref[cells, :])
-            prob = prob_ref[w]
-            prob_grad = dot_nt(qkv_ref[cells, 2 * width :], out_grad)
-            score_grad = prob * (prob_grad - jnp.sum(prob_grad * prob, axis=0, keepdims=True))
-            score_sum_ref[...] += score_grad
-            score_grad = score_grad.astype(BF16)
-            dqkv_ref[cells, :width] = (
-                own_head(dot_tn(score_grad, qkv_ref[cells, width : 2 * width])) * score_scale
-            ).astype(BF16)
-            dqkv_ref[cells, width : 2 * width] = dot_nn(score_grad, queries).astype(BF16)
-            dqkv_ref[cells, 2 * width :] = dot_nn(prob.astype(BF16), out_grad).astype(BF16)
-
-        dqkv = dqkv_ref[...]
-        out_ref[slot, 1, here, :] = (middle_grad + dot_nt(dqkv, w_qkv_ref[...])).astype(BF16)
-        add_grad(0, dot_tn(x, dqkv))
-        qkv_sums = column_sums(dqkv.astype(F32))
+        att_ref[kept] = dot_nt(branch_low, w_proj_ref[...]).astype(BF16)
+        yield
+        add_grad(6, dot_tn(att, branch_low))
+        middle_grad_ref[kept] = middle_grad
         sums = [
             column_sums(middle_grad), column_sums(middle_grad * norm_one), column_sums(g),
             column_sums(g * norm_two), column_sums(branch_low.astype(F32)),
             column_sums(second_low.astype(F32)),
         ]
-        sums += [qkv_sums[:, j * width : (j + 1) * width] for j in range(3)]
+        sums += [jnp.zeros((1, width), F32)] * 3
         sums += [up_sums[:, j * width : (j + 1) * width] for j in range(hidden_width // width)]
         sums += [jnp.zeros((VECTORS - len(sums), width), F32)]
         small_ref[:VECTORS, :] += jnp.concatenate(sums, axis=0)
-        return group
+
+    def backward(index, group, kept):
+        slot = lax.rem(group, 2)
+        here = pl.ds(pl.multiple_of(index * rows, 16), rows)
+
+        for w in range(BLOCK_WINDOWS):
+            cells = pl.ds(w * WINDOW, WINDOW)
+            queries = by_head(qkv_ref[kept, cells, :width] * BF16(score_scale))
+            out_grad = by_head(att_ref[kept, cells, :])
+            prob = prob_ref[kept, w]
+            prob_grad = dot_nt(qkv_ref[kept, cells, 2 * width :], out_grad)
+            score_grad = prob * (prob_grad - jnp.sum(prob_grad * prob, axis=0, keepdims=True))
+            score_sum_ref[...] += score_grad
+            score_grad = score_grad.astype(BF16)
+            dqkv_ref[cells, :width] = (
+                own_head(dot_tn(score_grad, qkv_ref[kept, cells, width : 2 * width])) * score_scale
+            ).astype(BF16)
+            dqkv_ref[cells, width : 2 * width] = dot_nn(score_grad, queries).astype(BF16)
+            dqkv_ref[cells, 2 * width :] = dot_nn(prob.astype(BF16), out_grad).astype(BF16)
+            yield
+
+        dqkv = dqkv_ref[...]
+        out_ref[slot, 1, here, :] = (
+            middle_grad_ref[kept] + dot_nt(dqkv, w_qkv_ref[...])
+        ).astype(BF16)
+        add_grad(0, dot_tn(xw_ref[here, :].astype(BF16), dqkv))
+        qkv_sums = column_sums(dqkv.astype(F32))
+        sums = [qkv_sums[:, j * width : (j + 1) * width] for j in range(3)]
+        small_ref[6:9, :] += jnp.concatenate(sums, axis=0)
+
+    def together(*stages):
+        stages = list(stages)
+        while stages:
+            for stage in list(stages):
+                try:
+                    next(stage)
+                except StopIteration:
+                    stages.remove(stage)
+
+    blocks = col_count // WX // BLOCK_WINDOWS
+
+    def plain_blocks(group):
+        def block(index, carry):
+            @pl.when((group == 0) & (index == 2))
+            def _():
+                rows_copy(1).start()
+                corner_copies[1].start()
+
+            together(forward(index, group, 0))
+            together(backward(index, group, 0))
+            return carry
+
+        lax.fori_loop(0, blocks, block, 0)
+
+    def last_blocks(group):
+        def forwards(index, carry):
+            together(forward(index, group, index))
+            return carry
+
+        def backwards(index, carry):
+            stage = backward(index, group, index)
+            for _ in range(BLOCK_WINDOWS // 2 + 1):
+                next(stage)
+            for step in range(hidden_steps):
+                @pl.when(index == step)
+                def _():
+                    for p in early:
+                        sum_step(p, step + 1)
+
+            together(stage)
+            return carry
+
+        lax.fori_loop(0, blocks, forwards, 0)
+        for p in early:
+            sum_step(p, 0)
+        lax.fori_loop(0, blocks, backwards, 0)
+        for step in range(blocks, hidden_steps):
+            for p in early:
+                sum_step(p, step + 1)
 
     def gather(pair, group):
         def assemble(own, strip, axis):
@@ -516,7 +752,14 @@
         score_bias_ref[...] = mask_scores(
             bias_ref[...], pair, base, lat, band_count, crop_ref, row_count
         )
-        lax.fori_loop(0, col_count // WX // BLOCK_WINDOWS, block, group)
+        @pl.when(group < GROUPS - 1)
+        def _():
+            plain_blocks(group)
+
+        @pl.when(group == GROUPS - 1)
+        def _():
+            last_blocks(group)
+
         out_copy(group).start()
         edge_copy(group).start()
 
@@ -530,7 +773,20 @@
         return carry
 
     lax.fori_loop(0, GROUPS, group_step, 0)
+    late_step(0)
     small_ref[VECTORS:, : HEADS * OFFSETS] = table_grad(score_sum_ref)
+    early_steps = 2 * halvings - hidden_steps
+    for k in range(max(early_steps, 4, len(bits))):
+        if k < len(bits):
+            small_copy = to_partner(small_ref, small_recv_ref.at[k], small_sems.at[k], bits[k])
+            small_copy.start()
+        if k < early_steps:
+            for p in early:
+                sum_step(p, hidden_steps + 1 + k)
+        late_step(k + 1)
+        if k < len(bits):
+            small_copy.wait()
+            small_ref[...] += small_recv_ref[k]
     for group in (2, 3):
         out_copy(group).wait()
         edge_copy(group).wait_send()
@@ -551,9 +807,16 @@
     cells = col_count * CELLS
     rows = BLOCK_WINDOWS * WINDOW
     edge = -(-EDGE // 16) * 16
+    blocks = col_count // WX // BLOCK_WINDOWS
     pairs = level_count // WZ
     strips = (pairs, 2, WZ, packed_rows(col_count), width)
-    grad_rows = 4 * width + 2 * constants[4].shape[1]
+    grad_rows = (4 * width + 2 * constants[4].shape[1]) * (width // LANES)
+    bits, halvings = sum_bits()
+    parts = sum_parts(width, constants[4].shape[1])
+    more = max(1, len(bits) - halvings)
+    late_rows = parts[2][1] // 2
+    shard = max([count >> halvings for _, count in parts] + [late_rows // peer_sizes()[2]])
+    half_rows = sum(halved(count, halvings)[1][-1] for _, count in parts)
     sends = pltpu.SemaphoreType.DMA
     return pl.pallas_call(
         block_kernel,
@@ -564,10 +827,17 @@
             shape_of(strips, BF16),
             shape_of((GROUPS, 2, edge, width), BF16),
             shape_of((pairs, 2, edge, width), BF16),
-            shape_of((grad_rows, width), F32),
+            shape_of((grad_rows, LANES), BF16),
             shape_of((VECTORS + TABLE_ROWS, width), F32),
         ],
         scratch_shapes=[
+            pltpu.VMEM((grad_rows, LANES), F32),
+            pltpu.VMEM((half_rows, LANES), BF16),
+            pltpu.VMEM((half_rows, LANES), BF16),
+            pltpu.VMEM((2, len(parts), more, shard, LANES), BF16),
+            pltpu.VMEM((max(1, len(bits)), VECTORS + TABLE_ROWS, width), F32),
+            pltpu.VMEM((late_rows, LANES), BF16),
+            pltpu.VMEM((peer_sizes()[2], late_rows // peer_sizes()[2], LANES), BF16),
             pltpu.VMEM((2,) + tokens.shape, BF16),
             pltpu.VMEM(strips, BF16),
             pltpu.VMEM(strips, BF16),
@@ -578,13 +848,16 @@
             pltpu.VMEM((WINDOW, SCORES), F32),
             pltpu.VMEM((cells, width), F32),
             pltpu.VMEM((cells, width), F32),
-            pltpu.VMEM((rows, 3 * width), BF16),
-            pltpu.VMEM((BLOCK_WINDOWS, WINDOW, SCORES), F32),
-            pltpu.VMEM((rows, width), BF16),
+            pltpu.VMEM((blocks, rows, 3 * width), BF16),
+            pltpu.VMEM((blocks, BLOCK_WINDOWS, WINDOW, SCORES), F32),
+            pltpu.VMEM((blocks, rows, width), BF16),
+            pltpu.VMEM((blocks, rows, width), F32),
             pltpu.VMEM((rows, 3 * width), BF16),
             pltpu.VMEM((WINDOW, SCORES), F32),
             sends((2 * level_count,)), sends((3, 2)), sends((pairs, 2)), sends((pairs, 2)),
             sends((GROUPS, 2)), sends((pairs, 2)), sends((GROUPS,)),
+            sends((len(parts), len(bits) + halvings, 2)), sends((max(1, len(bits)), 2)),
+            sends((2, peer_sizes()[2], 2)),
         ],
         cost_estimate=pl.CostEstimate(
             flops=GROUPS * cells * 5_200_000, bytes_accessed=32 * 2**20, transcendentals=0
@@ -593,132 +866,6 @@
             collective_id=1, has_side_effects=True, vmem_limit_bytes=VMEM_LIMIT
         ),
     )(crop_rows, tokens, cotangent, *constants)
-
-
-def halved(rows, count):
-    sizes = [rows >> (i + 1) for i in range(count)]
-    return sizes, [sum(sizes[:i]) for i in range(count + 1)]
-
-
-def sum_kernel(
-    bits, halvings, parts, grad_ref, small_ref, out_ref, small_out_ref,
-    acc_ref, send_ref, recv_ref, more_ref, small_recv_ref, sems, small_sems,
-):
-    axes = ("lat", "lon")
-    places = {axis: lax.axis_index(axis) for axis in axes}
-    own_bit, partner = {}, {}
-    for axis, bit in bits:
-        value = (places[axis] // 2**bit) % 2
-        own_bit[axis, bit] = value
-        moved = dict(places)
-        moved[axis] = places[axis] + 2**bit * (1 - 2 * value)
-        partner[axis, bit] = tuple(moved[name] for name in axes)
-
-    barrier = pltpu.get_barrier_semaphore()
-    for bit in bits:
-        pl.semaphore_signal(barrier, inc=1, device_id=partner[bit], device_id_type=MESH)
-    pl.semaphore_wait(barrier, len(bits))
-
-    def send(source, target, pair, bit):
-        copy = pltpu.make_async_remote_copy(
-            src_ref=source, dst_ref=target, send_sem=pair.at[0], recv_sem=pair.at[1],
-            device_id=partner[bit], device_id_type=MESH,
-        )
-        copy.start()
-        return copy
-
-    part_rows = grad_ref.shape[0] // parts
-    sizes, starts = halved(part_rows, halvings)
-    shard = sizes[-1]
-    orders = []
-    for p in range(parts):
-        order = list(bits[:halvings])
-        if p == 1 and halvings > 2:
-            order[1], order[2] = order[2], order[1]
-        orders.append(order)
-    low = [p * part_rows for p in range(parts)]
-    small_out_ref[...] = small_ref[...]
-    acc_ref[...] = grad_ref[...]
-
-    def halve(p, s):
-        bit, size = orders[p][s], sizes[s]
-        place = pl.ds(p * starts[-1] + starts[s], size)
-        away = pl.multiple_of(low[p] + (1 - own_bit[bit]) * size, 16)
-        send_ref[place, :] = acc_ref[pl.ds(away, size), :].astype(BF16)
-        low[p] = low[p] + own_bit[bit] * size
-        return send(send_ref.at[place], recv_ref.at[place], sems.at[p, s], bit)
-
-    def add_half(p, s, copy):
-        size = sizes[s]
-        copy.wait()
-        place = pl.ds(p * starts[-1] + starts[s], size)
-        here = pl.ds(pl.multiple_of(low[p], 16), size)
-        acc_ref[here, :] += recv_ref[place, :].astype(F32)
-
-    copies = [halve(p, 0) for p in range(parts)]
-    for s, bit in enumerate(bits):
-        small_copy = send(small_out_ref, small_recv_ref.at[s], small_sems.at[s], bit)
-        if s < halvings:
-            for p in range(parts):
-                add_half(p, s, copies[p])
-                if s + 1 < halvings:
-                    copies[p] = halve(p, s + 1)
-        small_copy.wait()
-        small_out_ref[...] += small_recv_ref[s]
-
-    for p in range(parts):
-        here = pl.ds(pl.multiple_of(low[p], 16), shard)
-        out_ref[here, :] = acc_ref[here, :].astype(BF16)
-        for s in range(halvings, len(bits)):
-            mine = more_ref.at[0, p, s - halvings]
-            theirs = more_ref.at[1, p, s - halvings]
-            mine[...] = out_ref[here, :]
-            send(mine, theirs, sems.at[p, s], bits[s]).wait()
-            out_ref[here, :] = (mine[...].astype(F32) + theirs[...].astype(F32)).astype(BF16)
-
-    def give(p, s):
-        here = out_ref.at[pl.ds(pl.multiple_of(low[p], 16), sizes[s]), :]
-        low[p] = low[p] - own_bit[orders[p][s]] * sizes[s]
-        return send(here, here, sems.at[p, len(bits) + s], orders[p][s])
-
-    copies = [give(p, halvings - 1) for p in range(parts)]
-    for s in reversed(range(halvings)):
-        for p in range(parts):
-            copies[p].wait()
-            if s:
-                copies[p] = give(p, s - 1)
-
-
-def sum_over_devices(grad, small):
-    bits = [("lon", 0), ("lon", 1), ("lat", 0), ("lat", 1), ("lat", 2)]
-    bits = [b for b in bits if 2 ** b[1] < lax.axis_size(b[0])]
-    bits += [("lat", b) for b in range(3, lax.axis_size("lat").bit_length() - 1)]
-    bits += [("lon", b) for b in range(2, lax.axis_size("lon").bit_length() - 1)]
-    if not bits:
-        return grad.astype(BF16), small
-    halvings, parts = min(5, len(bits)), 2
-    rows, width = grad.shape
-    sizes, starts = halved(rows // parts, halvings)
-    more = max(1, len(bits) - halvings)
-    vmem = pl.BlockSpec(memory_space=pltpu.VMEM)
-    return pl.pallas_call(
-        functools.partial(sum_kernel, tuple(bits), halvings, parts),
-        in_specs=[vmem, vmem],
-        out_specs=[vmem, vmem],
-        out_shape=[shape_of(grad.shape, BF16), shape_of(small.shape, F32)],
-        scratch_shapes=[
-            pltpu.VMEM(grad.shape, F32),
-            pltpu.VMEM((parts * starts[-1], width), BF16),
-            pltpu.VMEM((parts * starts[-1], width), BF16),
-            pltpu.VMEM((2, parts, more, sizes[-1], width), BF16),
-            pltpu.VMEM((len(bits),) + small.shape, F32),
-            pltpu.SemaphoreType.DMA((parts, len(bits) + halvings, 2)),
-            pltpu.SemaphoreType.DMA((len(bits), 2)),
-        ],
-        compiler_params=pltpu.CompilerParams(
-            collective_id=0, has_side_effects=True, vmem_limit_bytes=VMEM_LIMIT
-        ),
-    )(grad, small)
 
 
 def merge_kernel(
@@ -765,7 +912,11 @@
     grad_qkv, grad_proj, grad_up, grad_down, grad_mod, *vectors = grads
 
     def slab(index):
-        return grad_ref[index * width : (index + 1) * width, :].astype(F32)
+        per_slab = width // LANES
+        return jnp.concatenate([
+            grad_ref[j * width : (j + 1) * width, :].astype(F32)
+            for j in range(index * per_slab, (index + 1) * per_slab)
+        ], axis=1)
 
     @pl.when(step == 0)
     def _():
@@ -844,17 +995,13 @@
     w_mod, b_mod, rel_table, crop_rows, lead_hours,
 ):
     fields = [field.transpose(0, 2, 1, 3) for field in (tokens, cotangent)]
-    table = rel_table.transpose(1, 3, 0, 2).reshape(HEADS * OFFSETS, 2 * WY - 1)
-    nothing = jnp.zeros_like(q_bias)
-    vectors = jnp.concatenate(
-        [b_mod, b_proj, b_down, q_bias, nothing, v_bias, b_up] + [nothing] * 3
-    ).reshape(VECTORS, -1)
+    table = rel_table.transpose(1, 3, 0, 2)
+    vectors = (b_mod, b_proj, b_down, q_bias, v_bias, b_up)
     bias, vecs, context = set_up(lead_hours, w_mod, vectors, table)
     constants = [bias, vecs, w_qkv, w_proj, w_up, w_down]
     windows, rows_back, edge_back, corner_back, grad, small = block_call(
         crop_rows, *fields, constants
     )
-    grad, small = sum_over_devices(grad, small)
     (
         mixed, token_grad, grad_qkv, grad_proj, grad_up, grad_down, grad_mod, grad_mod_bias,
         grad_proj_bias, grad_down_bias, grad_q_bias, grad_v_bias, grad_up_bias,

time: 199 us -> 177 us (0.89)
  Pallas kernels: 189 us -> 175 us
  local copies, waits for them, and re-layouts: 8.18 us -> 0.86 us
    pallas_call x1 -> x0, Pallas kernels: 43.7 us -> none  [sum_over_devices(): pl.pallas_call(functools.partial(sum_kernel, tuple(bits), halvings, parts...]
    pallas_call x1, Pallas kernels: 129 us -> 158 us  [block_call(): pl.pallas_call(block_kernel, in_specs=[pl.BlockSpec(memory_space=pltpu.SM...]
    unnamed x9 -> x2, local copies, waits for them, and re-layouts: 5.1 us -> 0.01 us
    reshape x2 -> x0, local copies, waits for them, and re-layouts: 2.01 us -> none  [the longest x1 1.4 us: on_device(): table = rel_table.transpose(1, 3, 0, 2).reshape(HEADS * OFFSETS, 2 * WY - 1)]
where the time goes in v5:
time: 177 us
  Pallas kernels  175 us (99%)
    pallas_call x1, Pallas kernels, block_call(): pl.pallas_call(block_kernel, in_specs=[pl.BlockSpec(memory_space=pltpu.SM...  158 us
    pallas_call x1, Pallas kernels, merge(): pl.pallas_call(merge_kernel, grid=(level_count,), in_specs=[windows_of(Fa...  12.6 us
    pallas_call x1, Pallas kernels, set_up(): pl.pallas_call(setup_kernel, in_specs=[pl.BlockSpec(memory_space=pltpu.SM...  3.71 us

profile of v5, /device:TPU:0, one launch (start us, length us, event | category | flops | bytes accessed | tf_op | source)
XLA Modules:
  0.0 176.8 jit_solution(1773804437383140401)
XLA Ops:
  1.3 3.7 %shard_map.263 = (f32[144,576]{1,0:T(8,128)}, f32[16,256]{1,0:T(8,128)}, f32[256,128]{1,0:T(8,128)}) custom-call(s32[1]{0:T(128)S(6)} %copy.32.lead_ref, bf16[256,1024]{1,0:T(8,128)(2,1)} %w_mod_ref.1, bf16[1024]{0:T(1024)(128)(2,1)} %b_mod_ref.1, bf16[256]{0:T(256)(128)(2,1)} %b_proj_ref.1, bf16[256]{0:T(256)(128)(2,1)} %b_down_ref.1, ...), custom_call_target="tpu_custom_call" | custom-call | tf_op jit(solution)/shard_map/pallas_call | solution.py:125
  5.0 158.2 %shard_map.264 = (bf16[2,4,2160,256]{3,2,1,0:T(8,128)(2,1)}, bf16[2,2,2,544,256]{4,3,2,1,0:T(8,128)(2,1)}, bf16[4,2,80,256]{3,2,1,0:T(8,128)(2,1)}, bf16[2,2,80,...) custom-call(s32[8]{0:T(128)} %crop_ref.1, bf16[4,90,24,256]{3,2,1,0:T(8,128)(2,1)} %bitcast.16, ...), custom_call_target="tpu_custom_call" | custom-call | flops 44928000000 | bytes 33554432 | tf_op jit(solution)/shard_map/pallas_call | solution.py:821
  163.2 0.0 copy-start
  163.3 12.6 %shard_map.265 = (bf16[4,90,24,256]{3,2,1,0:T(8,128)(2,1)}, bf16[4,90,24,256]{3,2,1,0:T(8,128)(2,1)}, f32[256,768]{1,0:T(8,128)}, f32[256,256]{1,0:T(8,128)}, f3...) custom-call(bf16[2,4,2160,256]{3,2,1,0:T(8,128)(2,1)} %get-tuple-ele, ...), custom_call_target="tpu_custom_call" | custom-call | tf_op jit(solution)/shard_map/pallas_call | solution.py:978
  175.9 0.0 copy-done
  175.9 0.1 rev.3
  176.0 0.1 copy.31
  176.1 0.7 reshape.31
  (1 shorter events, 0.0 us)
Async XLA Ops:
  163.2 12.6 %copy-start = (f32[40,256]{1,0:T(8,128)S(1)}, f32[40,256]{1,0:T(8,128)}, u32[]{:S(2)}) copy-start(f32[40,256]{1,0:T(8,128)} %get-tuple-element.43.small_ref) | copy-start | bytes 122884

commit v6 on v5

--- a/solution.py
+++ b/solution.py
@@ -73,7 +73,7 @@
     return iota((HEADS * OFFSETS, SCORES), 0) == place
 
 
-def setup_kernel(
+def set_up(
     lead_ref, w_mod_ref, b_mod_ref, b_proj_ref, b_down_ref, q_bias_ref, v_bias_ref, b_up_ref,
     table_ref, bias_ref, vec_ref, context_ref,
 ):
@@ -119,22 +119,6 @@
             bias_ref[start : start + WY, :] = rows
 
 
-def set_up(lead_hours, w_mod, vectors, table):
-    width = w_mod.shape[0]
-    vmem = pl.BlockSpec(memory_space=pltpu.VMEM)
-    return pl.pallas_call(
-        setup_kernel,
-        in_specs=[pl.BlockSpec(memory_space=pltpu.SMEM)] + [vmem] * (2 + len(vectors)),
-        out_specs=[vmem] * 3,
-        out_shape=[
-            shape_of((WINDOW, SCORES), F32),
-            shape_of((VECTORS, width), F32),
-            shape_of((width, 128), F32),
-        ],
-        compiler_params=pltpu.CompilerParams(vmem_limit_bytes=VMEM_LIMIT),
-    )(lead_hours, w_mod, *vectors, table)
-
-
 def table_grad(score_sum_ref):
     query_y = iota((WY, SCORES), 1) % WY
     total = jnp.zeros((TABLE_ROWS, HEADS * OFFSETS), F32)
@@ -274,8 +258,10 @@
 
 
 def block_kernel(
-    crop_ref, tokens_ref, cotangent_ref, bias_ref, vec_ref, w_qkv_ref, w_proj_ref, w_up_ref, w_down_ref,
-    win_ref, rows_back_ref, edge_back_ref, corner_back_ref, sum_ref, small_ref,
+    crop_ref, lead_ref, tokens_ref, cotangent_ref, w_mod_ref, b_mod_ref, b_proj_ref, b_down_ref,
+    q_bias_ref, v_bias_ref, b_up_ref, table_ref, w_qkv_ref, w_proj_ref, w_up_ref, w_down_ref,
+    win_ref, rows_back_ref, edge_back_ref, corner_back_ref, sum_ref, small_ref, context_ref,
+    bias_ref, vec_ref,
     grad_ref, send_ref, recv_ref, more_ref, small_recv_ref, scatter_ref, pieces_ref, fields_ref, rows_out_ref, rows_in_ref, cols_in_ref, corner_out_ref, corner_in_ref, out_ref,
     score_bias_ref, xw_ref, gw_ref, qkv_ref, prob_ref, att_ref, middle_grad_ref, dqkv_ref,
     score_sum_ref,
@@ -330,6 +316,11 @@
                 ref.at[level], fields_ref.at[a, level], field_sems.at[len(loads)]
             ))
             loads[-1].start()
+
+    set_up(
+        lead_ref, w_mod_ref, b_mod_ref, b_proj_ref, b_down_ref, q_bias_ref, v_bias_ref, b_up_ref,
+        table_ref, bias_ref, vec_ref, context_ref,
+    )
 
     def remote(source, target, sems, lat_step, lon_step):
         return pltpu.make_async_remote_copy(
@@ -801,7 +792,7 @@
         edge_copy(group).wait_recv()
 
 
-def block_call(crop_rows, tokens, cotangent, constants):
+def block_call(crop_rows, lead_hours, tokens, cotangent, constants):
     level_count, col_count, row_count, width = tokens.shape
     vmem = pl.BlockSpec(memory_space=pltpu.VMEM)
     cells = col_count * CELLS
@@ -810,9 +801,9 @@
     blocks = col_count // WX // BLOCK_WINDOWS
     pairs = level_count // WZ
     strips = (pairs, 2, WZ, packed_rows(col_count), width)
-    grad_rows = (4 * width + 2 * constants[4].shape[1]) * (width // LANES)
+    grad_rows = (4 * width + 2 * constants[-2].shape[1]) * (width // LANES)
     bits, halvings = sum_bits()
-    parts = sum_parts(width, constants[4].shape[1])
+    parts = sum_parts(width, constants[-2].shape[1])
     more = max(1, len(bits) - halvings)
     late_rows = parts[2][1] // 2
     shard = max([count >> halvings for _, count in parts] + [late_rows // peer_sizes()[2]])
@@ -820,8 +811,8 @@
     sends = pltpu.SemaphoreType.DMA
     return pl.pallas_call(
         block_kernel,
-        in_specs=[pl.BlockSpec(memory_space=pltpu.SMEM), ANY, ANY] + [vmem] * len(constants),
-        out_specs=[ANY] * 4 + [vmem] * 2,
+        in_specs=[pl.BlockSpec(memory_space=pltpu.SMEM)] * 2 + [ANY, ANY] + [vmem] * len(constants),
+        out_specs=[ANY] * 4 + [vmem] * 3,
         out_shape=[
             shape_of((2, GROUPS, cells, width), BF16),
             shape_of(strips, BF16),
@@ -829,8 +820,11 @@
             shape_of((pairs, 2, edge, width), BF16),
             shape_of((grad_rows, LANES), BF16),
             shape_of((VECTORS + TABLE_ROWS, width), F32),
+            shape_of((width, LANES), F32),
         ],
         scratch_shapes=[
+            pltpu.VMEM((WINDOW, SCORES), F32),
+            pltpu.VMEM((VECTORS, width), F32),
             pltpu.VMEM((grad_rows, LANES), F32),
             pltpu.VMEM((half_rows, LANES), BF16),
             pltpu.VMEM((half_rows, LANES), BF16),
@@ -865,14 +859,15 @@
         compiler_params=pltpu.CompilerParams(
             collective_id=1, has_side_effects=True, vmem_limit_bytes=VMEM_LIMIT
         ),
-    )(crop_rows, tokens, cotangent, *constants)
+    )(crop_rows, lead_hours, tokens, cotangent, *constants)
 
 
 def merge_kernel(
     inner_ref, straddle_ref, rows_ref, inner_edge_ref, straddle_edge_ref, corner_ref,
     grad_ref, small_ref, context_ref, *out_refs,
 ):
-    fields, grads = out_refs[:2], out_refs[2:]
+    fields, grads, vectors, sems = out_refs[:2], out_refs[2:7], out_refs[7:13], out_refs[-1]
+    staged = out_refs[13:-1]
     _, col_count, row_count, width = fields[0].shape
     step = pl.program_id(0)
 
@@ -909,7 +904,10 @@
                     piece(corner, a, 0, HALF_X, first + sent, HALF_Y),
                 )
 
-    grad_qkv, grad_proj, grad_up, grad_down, grad_mod, *vectors = grads
+    grad_qkv, grad_proj, grad_up, grad_down, grad_mod = staged
+
+    def leave(index):
+        return pltpu.make_async_copy(staged[index], grads[index], sems.at[index])
 
     def slab(index):
         per_slab = width // LANES
@@ -923,31 +921,37 @@
         for j in range(3):
             grad_qkv[:, j * width : (j + 1) * width] = slab(j)
         grad_proj[...] = slab(3)
+        leave(0).start()
+        leave(1).start()
+        for part in range(4):
+            row = small_ref[part : part + 1, :]
+            for j in range(0, width, LANES):
+                grad_mod[:, part * width + j : part * width + j + LANES] = (
+                    context_ref[...] * row[:, j : j + LANES]
+                )
+        leave(4).start()
 
     @pl.when(step == 1)
     def _():
         for j in range(grad_up.shape[1] // width):
             grad_up[:, j * width : (j + 1) * width] = slab(4 + j)
+        leave(2).start()
 
     @pl.when(step == 2)
     def _():
         for j in range(grad_down.shape[0] // width):
             grad_down[j * width : (j + 1) * width, :] = slab(8 + j).T
+        leave(3).start()
 
     @pl.when(step == 3)
     def _():
-        lanes = context_ref.shape[1]
-        for part in range(4):
-            row = small_ref[part : part + 1, :]
-            for j in range(0, width, lanes):
-                grad_mod[:, part * width + j : part * width + j + lanes] = (
-                    context_ref[...] * row[:, j : j + lanes]
-                )
         mod_bias, proj_bias, down_bias, q_bias, v_bias, up_bias = vectors
         mod_bias[...] = jnp.concatenate([small_ref[i : i + 1, :] for i in range(4)], axis=1)
         up_bias[...] = jnp.concatenate([small_ref[i : i + 1, :] for i in range(9, 13)], axis=1)
         for ref, i in ((proj_bias, 4), (down_bias, 5), (q_bias, 6), (v_bias, 8)):
             ref[...] = small_ref[i : i + 1, :]
+        for index in range(len(staged)):
+            leave(index).wait()
 
 
 def merge(field_shape, hidden_width, windows, rows_back, edge_back, corner_back, grad, small, context):
@@ -971,9 +975,9 @@
 
     shapes = [
         (width, 3 * width), (width, width), (width, hidden_width), (hidden_width, width),
-        (width, 4 * width), (1, 4 * width), (1, width), (1, width), (1, width), (1, width),
-        (1, hidden_width),
+        (width, 4 * width),
     ]
+    vectors = [(1, 4 * width), (1, width), (1, width), (1, width), (1, width), (1, hidden_width)]
     field = pl.BlockSpec((1,) + field_shape[1:], lambda i: (level_of(i), 0, 0, 0))
     return pl.pallas_call(
         merge_kernel,
@@ -984,8 +988,11 @@
             edge_of(False), edge_of(True),
             pl.BlockSpec((1,) + corner_back.shape[1:], lambda i: (i // WZ, 0, 0, 0)),
         ] + [whole(v.shape) for v in (grad, small, context)],
-        out_specs=[field, field] + [whole(s) for s in shapes],
-        out_shape=[shape_of(field_shape, BF16)] * 2 + [shape_of(s, F32) for s in shapes],
+        out_specs=[field, field] + [ANY] * len(shapes) + [whole(s) for s in vectors],
+        out_shape=[shape_of(field_shape, BF16)] * 2 + [shape_of(s, F32) for s in shapes + vectors],
+        scratch_shapes=[pltpu.VMEM(s, F32) for s in shapes] + [
+            pltpu.SemaphoreType.DMA((len(shapes),))
+        ],
         compiler_params=pltpu.CompilerParams(vmem_limit_bytes=VMEM_LIMIT),
     )(windows, windows, rows_back, edge_back, edge_back, corner_back, grad, small, context)
 
@@ -996,11 +1003,10 @@
 ):
     fields = [field.transpose(0, 2, 1, 3) for field in (tokens, cotangent)]
     table = rel_table.transpose(1, 3, 0, 2)
-    vectors = (b_mod, b_proj, b_down, q_bias, v_bias, b_up)
-    bias, vecs, context = set_up(lead_hours, w_mod, vectors, table)
-    constants = [bias, vecs, w_qkv, w_proj, w_up, w_down]
-    windows, rows_back, edge_back, corner_back, grad, small = block_call(
-        crop_rows, *fields, constants
+    windows, rows_back, edge_back, corner_back, grad, small, context = block_call(
+        crop_rows, lead_hours, *fields, (
+            w_mod, b_mod, b_proj, b_down, q_bias, v_bias, b_up, table, w_qkv, w_proj, w_up, w_down,
+        )
     )
     (
         mixed, token_grad, grad_qkv, grad_proj, grad_up, grad_down, grad_mod, grad_mod_bias,

time: 177 us -> 177 us (level)
    pallas_call x1 -> x0, Pallas kernels: 3.71 us -> none  [set_up(): pl.pallas_call(setup_kernel, in_specs=[pl.BlockSpec(memory_space=pltpu.SM...]
    pallas_call x1, Pallas kernels: 158 us -> 162 us  [block_call(): pl.pallas_call(block_kernel, in_specs=[pl.BlockSpec(memory_space=pltpu.SM...]
where the time goes in v6:
time: 177 us
  Pallas kernels  174 us (98%)
    pallas_call x1, Pallas kernels, block_call(): pl.pallas_call(block_kernel, in_specs=[pl.BlockSpec(memory_space=pltpu.SM...  162 us
    pallas_call x1, Pallas kernels, merge(): pl.pallas_call(merge_kernel, grid=(level_count,), in_specs=[windows_of(Fa...  12.5 us

profile of v6, /device:TPU:0, one launch (start us, length us, event | category | flops | bytes accessed | tf_op | source)
XLA Modules:
  0.0 176.5 jit_solution(16879301981035375095)
XLA Ops:
  1.3 161.8 %shard_map.263 = (bf16[2,4,2160,256]{3,2,1,0:T(8,128)(2,1)}, bf16[2,2,2,544,256]{4,3,2,1,0:T(8,128)(2,1)}, bf16[4,2,80,256]{3,2,1,0:T(8,128)(2,1)}, bf16[2,2,80,...) custom-call(s32[8]{0:T(128)} %crop_ref.1, s32[1]{0:T(128)S(6)} %copy.32.lead_ref, ...), custom_call_target="tpu_custom_call" | custom-call | flops 44928000000 | bytes 33554432 | tf_op jit(solution)/shard_map/pallas_call | solution.py:812
  163.1 0.0 copy-start
  163.1 12.5 %shard_map.264 = (bf16[4,90,24,256]{3,2,1,0:T(8,128)(2,1)}, bf16[4,90,24,256]{3,2,1,0:T(8,128)(2,1)}, f32[256,768]{1,0:T(8,128)}, f32[256,256]{1,0:T(8,128)}, f3...) custom-call(bf16[2,4,2160,256]{3,2,1,0:T(8,128)(2,1)} %get-tuple-ele, ...), custom_call_target="tpu_custom_call" | custom-call | tf_op jit(solution)/shard_map/pallas_call | solution.py:982
  175.6 0.0 copy-done
  175.6 0.1 rev.3
  175.7 0.1 copy.31
  175.8 0.7 reshape.31
  (1 shorter events, 0.0 us)
Async XLA Ops:
  163.1 12.5 %copy-start = (f32[40,256]{1,0:T(8,128)S(1)}, f32[40,256]{1,0:T(8,128)}, u32[]{:S(2)}) copy-start(f32[40,256]{1,0:T(8,128)} %get-tuple-element.39.small_ref) | copy-start | bytes 122884

commit v7 on v5

--- a/solution.py
+++ b/solution.py
@@ -186,8 +186,11 @@
     return jnp.mean(values, axis=-1, keepdims=True)
 
 
-def norm(values):
-    center = values - row_mean(values)
+def centered(values):
+    return values - row_mean(values)
+
+
+def norm_centered(center):
     inverse = lax.rsqrt(row_mean(center * center) + NORM_EPSILON)
     return center * inverse, inverse
 
@@ -276,7 +279,8 @@
 def block_kernel(
     crop_ref, tokens_ref, cotangent_ref, bias_ref, vec_ref, w_qkv_ref, w_proj_ref, w_up_ref, w_down_ref,
     win_ref, rows_back_ref, edge_back_ref, corner_back_ref, sum_ref, small_ref,
-    grad_ref, send_ref, recv_ref, more_ref, small_recv_ref, scatter_ref, pieces_ref, fields_ref, rows_out_ref, rows_in_ref, cols_in_ref, corner_out_ref, corner_in_ref, out_ref,
+    grad_ref, send_ref, recv_ref, more_ref, small_recv_ref, scatter_ref, pieces_ref, proj_centered_ref,
+    down_centered_ref, fields_ref, rows_out_ref, rows_in_ref, cols_in_ref, corner_out_ref, corner_in_ref, out_ref,
     score_bias_ref, xw_ref, gw_ref, qkv_ref, prob_ref, att_ref, middle_grad_ref, dqkv_ref,
     score_sum_ref,
     field_sems, halo_sems, rows_sems, back_sems, edge_sems, corner_sems, out_sems, sum_sems, small_sems,
@@ -404,6 +408,9 @@
     shift_one, scale_one, shift_two, scale_two, b_proj, b_down = [
         vec_ref[i : i + 1, :] for i in range(6)
     ]
+    b_proj, b_down = centered(b_proj), centered(b_down)
+    for centered_ref, ref in ((proj_centered_ref, w_proj_ref), (down_centered_ref, w_down_ref)):
+        centered_ref[...] = centered(ref[...].astype(F32)).astype(BF16)
     qkv_shift = jnp.concatenate([vec_ref[i : i + 1, :] for i in range(6, 9)], axis=1)
     b_up = jnp.concatenate([vec_ref[i : i + 1, :] for i in range(9, 13)], axis=1)
 
@@ -552,18 +559,18 @@
             yield
 
         att = att_ref[kept]
-        branch = dot_nn(att, w_proj_ref[...]) + b_proj
+        branch = dot_nn(att, proj_centered_ref[...]) + b_proj
         yield
-        norm_one, inverse_one = norm(branch)
+        norm_one, inverse_one = norm_centered(branch)
         middle = x32 + norm_one * (1.0 + scale_one) + shift_one
         middle_low = middle.astype(BF16)
         pre = dot_nn(middle_low, w_up_ref[...]) + b_up
         yield
         hidden, slope = gelu_both(pre)
         hidden = hidden.astype(BF16)
-        second = dot_nn(hidden, w_down_ref[...]) + b_down
+        second = dot_nn(hidden, down_centered_ref[...]) + b_down
         yield
-        norm_two, inverse_two = norm(second)
+        norm_two, inverse_two = norm_centered(second)
         out_ref[slot, 0, here, :] = (middle + norm_two * (1.0 + scale_two) + shift_two).astype(BF16)
 
         g = gw_ref[here, :]
@@ -838,6 +845,8 @@
             pltpu.VMEM((max(1, len(bits)), VECTORS + TABLE_ROWS, width), F32),
             pltpu.VMEM((late_rows, LANES), BF16),
             pltpu.VMEM((peer_sizes()[2], late_rows // peer_sizes()[2], LANES), BF16),
+            pltpu.VMEM((width, width), BF16),
+            pltpu.VMEM((constants[4].shape[1], width), BF16),
             pltpu.VMEM((2,) + tokens.shape, BF16),
             pltpu.VMEM(strips, BF16),
             pltpu.VMEM(strips, BF16),

time: 177 us -> 175 us (0.989)
  Pallas kernels: 175 us -> 173 us
where the time goes in v7:
time: 175 us
  Pallas kernels  173 us (99%)
    pallas_call x1, Pallas kernels, block_call(): pl.pallas_call(block_kernel, in_specs=[pl.BlockSpec(memory_space=pltpu.SM...  157 us
    pallas_call x1, Pallas kernels, merge(): pl.pallas_call(merge_kernel, grid=(level_count,), in_specs=[windows_of(Fa...  12.6 us
    pallas_call x1, Pallas kernels, set_up(): pl.pallas_call(setup_kernel, in_specs=[pl.BlockSpec(memory_space=pltpu.SM...  3.71 us

profile of v7, /device:TPU:0, one launch (start us, length us, event | category | flops | bytes accessed | tf_op | source)
XLA Modules:
  0.0 175.1 jit_solution(13767087497389996848)
XLA Ops:
  1.3 3.7 %shard_map.263 = (f32[144,576]{1,0:T(8,128)}, f32[16,256]{1,0:T(8,128)}, f32[256,128]{1,0:T(8,128)}) custom-call(s32[1]{0:T(128)S(6)} %copy.32.lead_ref, bf16[256,1024]{1,0:T(8,128)(2,1)} %w_mod_ref.1, bf16[1024]{0:T(1024)(128)(2,1)} %b_mod_ref.1, bf16[256]{0:T(256)(128)(2,1)} %b_proj_ref.1, bf16[256]{0:T(256)(128)(2,1)} %b_down_ref.1, ...), custom_call_target="tpu_custom_call" | custom-call | tf_op jit(solution)/shard_map/pallas_call | solution.py:125
  5.0 156.5 %shard_map.264 = (bf16[2,4,2160,256]{3,2,1,0:T(8,128)(2,1)}, bf16[2,2,2,544,256]{4,3,2,1,0:T(8,128)(2,1)}, bf16[4,2,80,256]{3,2,1,0:T(8,128)(2,1)}, bf16[2,2,80,...) custom-call(s32[8]{0:T(128)} %crop_ref.1, bf16[4,90,24,256]{3,2,1,0:T(8,128)(2,1)} %bitcast.16, ...), custom_call_target="tpu_custom_call" | custom-call | flops 44928000000 | bytes 33554432 | tf_op jit(solution)/shard_map/pallas_call | solution.py:828
  161.5 0.0 copy-start
  161.5 12.6 %shard_map.265 = (bf16[4,90,24,256]{3,2,1,0:T(8,128)(2,1)}, bf16[4,90,24,256]{3,2,1,0:T(8,128)(2,1)}, f32[256,768]{1,0:T(8,128)}, f32[256,256]{1,0:T(8,128)}, f3...) custom-call(bf16[2,4,2160,256]{3,2,1,0:T(8,128)(2,1)} %get-tuple-ele, ...), custom_call_target="tpu_custom_call" | custom-call | tf_op jit(solution)/shard_map/pallas_call | solution.py:987
  174.2 0.0 copy-done
  174.2 0.1 rev.3
  174.3 0.1 copy.31
  174.4 0.7 reshape.31
  (1 shorter events, 0.0 us)
Async XLA Ops:
  161.5 12.6 %copy-start = (f32[40,256]{1,0:T(8,128)S(1)}, f32[40,256]{1,0:T(8,128)}, u32[]{:S(2)}) copy-start(f32[40,256]{1,0:T(8,128)} %get-tuple-element.43.small_ref) | copy-start | bytes 122884
